TPU v7x, 1024 devices: a whole 8x8x8 slice. The times are simulated.
1024 devices in a mesh: gx: 8 (over x), gy: 8 (over y), gz: 16 (over z, core).
Axes of the slice: x: 8, y: 8, z: 8, core: 2. Of those that a mesh axis runs over, the one named last changes fastest.
Arguments:
- source: float32 [4, 128, 128, 2048], P(None, 'gx', 'gy', 'gz'), may hold values from -6 to 6
- material_ids: int32 [16, 16, 256], P('gx', 'gy', 'gz'), may hold values from 0 to 7
- material_table: float32 [8], replicated, may hold values from 0.1 to 10
- roughness: float32 [128, 128, 2048], P('gx', 'gy', 'gz'), may hold values from 0.5 to 2
Outputs:
- correction: float32 [4, 128, 128, 2048], P(None, 'gx', 'gy', 'gz')
All inputs are finite; a program needn't handle non-finite values.
Results may differ from a plain program's by a relative error of at most 0.0001.
Values sent between devices are 32-bit elements; how exact they have to be, the bound alone decides.
No kernel may reach another device: no remote copies, remote signals or barrier semaphores. Data moves between devices by JAX's collectives and lax.ppermute only.
A program may use at most 128 MiB of HBM per device.

v0:
```python
import jax
import jax.numpy as jnp
from jax import lax
from jax.sharding import PartitionSpec as P

SWEEPS = 2
COARSE_ITERS = 8


OMEGA = 0.8


def extended(x, sides, width):
    for axis, dim in sides:
        peers, length = (lax.axis_size(axis), x.shape[dim])
        up = [(i, (i + 1) % peers) for i in range(peers - 1)]
        down = [(j, i) for i, j in up]
        last = lax.slice_in_dim(x, length - width, length, axis=dim)
        leading = lax.slice_in_dim(x, 0, width, axis=dim)
        before = lax.ppermute(last, axis, up)
        after = lax.ppermute(leading, axis, down)
        x = jnp.concatenate([before, x, after], axis=dim)
    return x


def neighbours(padded):
    total = padded[:, 2:, 1:-1, 1:-1] + padded[:, :-2, 1:-1, 1:-1]
    total = total + padded[:, 1:-1, 2:, 1:-1] + padded[:, 1:-1, :-2, 1:-1]
    total = total + padded[:, 1:-1, 1:-1, 2:] + padded[:, 1:-1, 1:-1, :-2]
    return total


def local_pad(weighted):
    return jnp.pad(weighted, ((0, 0), (1, 1), (1, 1), (1, 1)))


def halo_pad(weighted):
    return extended(weighted, (("gx", 1), ("gy", 2), ("gz", 3)), 1)


def operate(field, root_coef, pad_func):
    weighted = root_coef * field
    return root_coef * (6.0 * weighted - neighbours(pad_func(weighted)))


def relax(field, right_side, root_coef, step_scale, pad_func):
    return field + step_scale * (right_side - operate(field, root_coef, pad_func))


def coarsen(values):
    fields, size_a, size_b, size_c = values.shape
    shaped = values.reshape(fields, size_a // 2, 2, size_b // 2, 2, size_c // 2, 2)
    return shaped.sum(axis=(2, 4, 6))


def refine(values):
    return jnp.repeat(jnp.repeat(jnp.repeat(values, 2, axis=1), 2, axis=2), 2, axis=3)


def level_cycle(right_side, coefficient, pad_func, coarse_solve):
    root_coef = jnp.sqrt(coefficient)
    step_scale = OMEGA / (6.0 * coefficient)
    field = step_scale * right_side
    field = relax(field, right_side, root_coef, step_scale, pad_func)
    residual = right_side - operate(field, root_coef, pad_func)
    field = field + refine(coarse_solve(0.5 * coarsen(residual)))
    for sweep_index in range(SWEEPS):
        field = relax(field, right_side, root_coef, step_scale, pad_func)
    return field


def coarsest(right_side, coefficient):
    root_coef = jnp.sqrt(coefficient)
    step_scale = OMEGA / (6.0 * coefficient)
    field = step_scale * right_side
    for iter_index in range(COARSE_ITERS - 1):
        field = relax(field, right_side, root_coef, step_scale, local_pad)
    return field


def expand_blocks(blocks):
    return jnp.repeat(jnp.repeat(jnp.repeat(blocks, 8, axis=0), 8, axis=1), 8, axis=2)


def assemble(flat_rows, block_shape):
    fields, size_a, size_b, size_c = block_shape
    count_x = lax.axis_size("gx")
    count_y = lax.axis_size("gy")
    count_z = lax.axis_size("gz")
    shaped = flat_rows.reshape(count_x, count_y, count_z, fields, size_a, size_b, size_c)
    shaped = shaped.transpose(3, 0, 4, 1, 5, 2, 6)
    return shaped.reshape(fields, count_x * size_a, count_y * size_b, count_z * size_c)


def own_block(whole, block_shape):
    fields, size_a, size_b, size_c = block_shape
    start_x = lax.axis_index("gx") * size_a
    start_y = lax.axis_index("gy") * size_b
    start_z = lax.axis_index("gz") * size_c
    anchor = jnp.zeros((), jnp.int32)
    return lax.dynamic_slice(
        whole, (anchor, start_x, start_y, start_z), (fields, size_a, size_b, size_c)
    )


def shards(source, material_ids, material_table, roughness):
    choices_of = jnp.arange(material_table.shape[0], dtype=jnp.int32)
    matches = (material_ids[..., None] == choices_of).astype(jnp.float32)
    block_visc = jnp.sum(matches * material_table, axis=-1)
    viscosity = expand_blocks(block_visc) * roughness
    coef_zero = jnp.stack([viscosity, viscosity, viscosity, 1.0 / viscosity])
    coef_one = coarsen(coef_zero) * 0.125
    coef_two = coarsen(coef_one) * 0.125
    coef_three = coarsen(coef_two) * 0.125
    coef_four = coarsen(coef_three) * 0.125

    def merged(side_four):
        block_shape = side_four.shape
        gathered_side, gathered_coef = (
            lax.all_gather(side_four.reshape(1, -1), ("gx", "gy", "gz"), axis=0, tiled=True),
            lax.all_gather(coef_four.reshape(1, -1), ("gx", "gy", "gz"), axis=0, tiled=True),
        )
        whole_side = assemble(gathered_side, block_shape)
        whole_coef = assemble(gathered_coef, block_shape)
        whole_fix = coarsest(whole_side, whole_coef)
        return own_block(whole_fix, block_shape)

    def level_three(side_three):
        return level_cycle(side_three, coef_three, halo_pad, merged)

    def level_two(side_two):
        return level_cycle(side_two, coef_two, halo_pad, level_three)

    def level_one(side_one):
        return level_cycle(side_one, coef_one, halo_pad, level_two)

    return level_cycle(source, coef_zero, halo_pad, level_one)


def solution(mesh):
    return jax.shard_map(
        shards,
        mesh=mesh,
        in_specs=(P(None, "gx", "gy", "gz"), P("gx", "gy", "gz"), P(), P("gx", "gy", "gz")),
        out_specs=P(None, "gx", "gy", "gz"),
        check_vma=False,
    )
```

profile of v0, /device:TPU:479, one launch (start us, length us, event | category | flops | bytes accessed | tf_op | source)
XLA Modules:
  0.0 700.0 jit_solution(2662047132807955899)
XLA Ops:
  8.0 3.3 collective-permute-done.1
  22.1 9.5 %collective-permute-start.5 = (f32[4,18,18,1]{2,0,3,1:T(4,128)S(1)}, f32[4,18,18,1]{2,0,3,1:T(4,128)S(1)}, u32[]{:S(2)}, u32[]{:S(2)}) collective-permute-start(f32[4,18,18,1]{2,0,3,1:T(4,128)S(1)} %copy.983), channel_id=1, source_target_pairs={{0,1},{1,2},{2,3},{3,4},{4,5},{5,6},{6,7},{7,8},{8,9},{9,10},{10,1... | collective-permute-start | bytes 15560 | tf_op jit(solution)/shard_map/ppermute | solution.py:20
  34.7 4.0 collective-permute-done.4
  47.3 3.3 collective-permute-done.7
  56.0 9.7 %stack.20 = f32[1,8,2,8,2,64,2]{6,5,4,3,2,1,0:T(8,128)} reshape(f32[16,16,128]{2,1,0:T(8,128)S(1)} %get-tuple-element.42) | data formatting | bytes 262144 | tf_op jit(solution)/shard_map/stack | solution.py:111
  65.8 9.7 %stack.21 = f32[1,8,2,8,2,64,2]{6,5,4,3,2,1,0:T(8,128)} reshape(f32[16,16,128]{2,1,0:T(8,128)S(1)} %get-tuple-element.41) | data formatting | bytes 262144 | tf_op jit(solution)/shard_map/stack | solution.py:111
  76.6 4.2 collective-permute-start.11
  83.2 16.4 %maximum_reduce_fusion = f32[4,8,8,64]{3,2,1,0:T(8,128)S(1)} fusion(f32[1,8,2,8,2,64,2]{6,5,4,3,2,1,0:T(8,128)} %stack.21, f32[1,8,2,8,2,64,2]{6,5,4,3,2,1,0:T(8,128)} %stack.20), kind=kLoop, calls=%fused_computation | loop fusion | flops 507904 | bytes 327680 | tf_op jit(solution)/shard_map/reduce_sum | solution.py:53
  102.4 9.8 %copy.995 = f32[4,16,16,128]{0,3,2,1:T(8,128)} copy(f32[4,16,16,128]{3,2,1,0:T(8,128)} %fusion.23) | data formatting | bytes 1048576 | tf_op jit(solution)/shard_map/sub | solution.py:65
  112.1 11.7 %reduce_sum.97 = f32[4,8,8,64]{0,3,2,1:T(8,128)S(1)} reduce(f32[4,8,2,8,2,64,2]{0,6,5,4,3,2,1:T(2,128)} %bitcast.47, f32[]{:T(128)} %constant.14.clone.1), dimensions={2,4,6}, to_apply=%region_2.0 | reduce | flops 114688 | bytes 589828 | tf_op jit(solution)/shard_map/reduce_sum | solution.py:53
  142.5 6.8 collective-permute-start.17
  152.9 3.4 collective-permute-start.18
  162.8 3.4 collective-permute-start.20
  169.8 7.7 %collective-permute-start.23 = (f32[4,10,10,1]{3,0,2,1:T(4,128)S(1)}, f32[4,10,10,1]{3,0,2,1:T(4,128)S(1)}, u32[]{:S(2)}, u32[]{:S(2)}) collective-permute-start(f32[4,10,10,1]{3,0,2,1:T(4,128)S(1)} %get-tuple-element.98), channel_id=1, source_target_pairs={{0,1},{1,2},{2,3},{3,4},{4,5},{5,6},{6,7},{7,8},{8,9},{9,10},{10,1... | collective-permute-start | bytes 4808 | tf_op jit(solution)/shard_map/ppermute | solution.py:20
  188.9 3.7 collective-permute-done.25
  192.6 4.5 collective-permute-start.26
  199.4 4.9 collective-permute-done.27
  206.5 8.1 %collective-permute-start.29 = (f32[4,6,6,1]{3,0,2,1:T(4,128)S(1)}, f32[4,6,6,1]{3,0,2,1:T(4,128)S(1)}, u32[]{:S(2)}, u32[]{:S(2)}) collective-permute-start(f32[4,6,6,1]{3,0,2,1:T(4,128)S(1)} %get-tuple-element.140), channel_id=1, source_target_pairs={{0,1},{1,2},{2,3},{3,4},{4,5},{5,6},{6,7},{7,8},{8,9},{9,10},{10,1... | collective-permute-start | bytes 1736 | tf_op jit(solution)/shard_map/ppermute | solution.py:20
  221.6 3.7 collective-permute-done.31
  225.4 4.9 collective-permute-start.32
  237.8 8.3 %collective-permute-start.35 = (f32[4,6,6,1]{3,0,2,1:T(4,128)S(1)}, f32[4,6,6,1]{3,0,2,1:T(4,128)S(1)}, u32[]{:S(2)}, u32[]{:S(2)}) collective-permute-start(f32[4,6,6,1]{3,0,2,1:T(4,128)S(1)} %get-tuple-element.136), channel_id=1, source_target_pairs={{0,1},{1,2},{2,3},{3,4},{4,5},{5,6},{6,7},{7,8},{8,9},{9,10},{10,1... | collective-permute-start | bytes 1736 | tf_op jit(solution)/shard_map/ppermute | solution.py:20
  265.6 8.3 %collective-permute-start.41 = (f32[4,4,4,1]{3,2,1,0:T(4,128)S(1)}, f32[4,4,4,1]{3,2,1,0:T(4,128)S(1)}, u32[]{:S(2)}, u32[]{:S(2)}) collective-permute-start(f32[4,4,4,1]{3,2,1,0:T(4,128)S(1)} %get-tuple-element.170), channel_id=1, source_target_pairs={{0,1},{1,2},{2,3},{3,4},{4,5},{5,6},{6,7},{7,8},{8,9},{9,10},{10,1... | collective-permute-start | bytes 776 | tf_op jit(solution)/shard_map/ppermute | solution.py:20
  293.0 8.3 %collective-permute-start.47 = (f32[4,4,4,1]{3,2,1,0:T(4,128)S(1)}, f32[4,4,4,1]{3,2,1,0:T(4,128)S(1)}, u32[]{:S(2)}, u32[]{:S(2)}) collective-permute-start(f32[4,4,4,1]{3,2,1,0:T(4,128)S(1)} %get-tuple-element.164), channel_id=1, source_target_pairs={{0,1},{1,2},{2,3},{3,4},{4,5},{5,6},{6,7},{7,8},{8,9},{9,10},{10,1... | collective-permute-start | bytes 776 | tf_op jit(solution)/shard_map/ppermute | solution.py:20
  302.8 66.0 %all-gather = f32[1024,1,32]{2,1,0:T(1,128)S(1)} all-gather(f32[1,1,32]{2,1,0:T(1,128)S(1)} %reshape.143), channel_id=1, replica_groups=mesh['gx'=8,'gy'=8,'gz'=16] {'gx','gy','gz'}, dimensions={0}, use_global_device_ids=true | all-gather | bytes 131200 | tf_op jit(solution)/shard_map/all_gather | solution.py:121
  378.0 64.4 %all-gather.1 = f32[1024,1,32]{2,1,0:T(1,128)S(1)} all-gather(f32[1,1,32]{2,1,0:T(1,128)S(1)} %reshape.145), channel_id=1, replica_groups=mesh['gx'=8,'gy'=8,'gz'=16] {'gx','gy','gz'}, dimensions={0}, use_global_device_ids=true | all-gather | bytes 131200 | tf_op jit(solution)/shard_map/all_gather | solution.py:120
  463.5 4.9 collective-permute-start.52
  472.6 3.6 collective-permute-start.54
  480.8 4.1 collective-permute-start.56
  489.7 5.8 collective-permute-start.58
  495.6 4.4 collective-permute-start.59
  507.8 4.4 collective-permute-done.61
  520.0 4.8 collective-permute-start.64
  524.8 5.2 collective-permute-start.65
  532.1 3.6 collective-permute-start.66
  537.2 4.3 collective-permute-done.67
  550.0 3.7 collective-permute-start.70
  553.7 5.8 collective-permute-start.71
  580.5 7.0 %collective-permute-start.77 = (f32[4,10,10,1]{3,0,2,1:T(4,128)S(1)}, f32[4,10,10,1]{3,0,2,1:T(4,128)S(1)}, u32[]{:S(2)}, u32[]{:S(2)}) collective-permute-start(f32[4,10,10,1]{3,0,2,1:T(4,128)S(1)} %get-tuple-element.94), channel_id=1, source_target_pairs={{0,1},{1,2},{2,3},{3,4},{4,5},{5,6},{6,7},{7,8},{8,9},{9,10},{10,1... | collective-permute-start | bytes 4808 | tf_op jit(solution)/shard_map/ppermute | solution.py:20
  607.4 8.2 %collective-permute-start.83 = (f32[4,10,10,1]{3,0,2,1:T(4,128)S(1)}, f32[4,10,10,1]{3,0,2,1:T(4,128)S(1)}, u32[]{:S(2)}, u32[]{:S(2)}) collective-permute-start(f32[4,10,10,1]{3,0,2,1:T(4,128)S(1)} %get-tuple-element.90), channel_id=1, source_target_pairs={{0,1},{1,2},{2,3},{3,4},{4,5},{5,6},{6,7},{7,8},{8,9},{9,10},{10,1... | collective-permute-start | bytes 4808 | tf_op jit(solution)/shard_map/ppermute | solution.py:20
  630.4 3.3 collective-permute-done.85
  633.8 3.4 collective-permute-start.86
  639.2 4.5 collective-permute-done.87
  644.7 8.2 %collective-permute-start.89 = (f32[4,18,18,1]{2,0,3,1:T(4,128)S(1)}, f32[4,18,18,1]{2,0,3,1:T(4,128)S(1)}, u32[]{:S(2)}, u32[]{:S(2)}) collective-permute-start(f32[4,18,18,1]{2,0,3,1:T(4,128)S(1)} %copy.1097), channel_id=1, source_target_pairs={{0,1},{1,2},{2,3},{3,4},{4,5},{5,6},{6,7},{7,8},{8,9},{9,10},{10,1... | collective-permute-start | bytes 15560 | tf_op jit(solution)/shard_map/ppermute | solution.py:20
  655.9 4.0 collective-permute-done.88
  667.7 3.3 collective-permute-done.91
  671.1 4.9 collective-permute-start.92
  683.8 4.8 collective-permute-start.95
  691.6 4.0 collective-permute-done.94
  (453 shorter events, 298.9 us)
Async XLA Ops:
  22.1 12.0 %collective-permute-start.5 = (f32[4,18,18,1]{2,0,3,1:T(4,128)S(1)}, f32[4,18,18,1]{2,0,3,1:T(4,128)S(1)}, u32[]{:S(2)}, u32[]{:S(2)}) collective-permute-start(f32[4,18,18,1]{2,0,3,1:T(4,128)S(1)} %copy.983), channel_id=1, source_target_pairs={{0,1},{1,2},{2,3},{3,4},{4,5},{5,6},{6,7},{7,8},{8,9},{9,10},{10,1... | collective-permute-start | bytes 15560 | tf_op jit(solution)/shard_map/ppermute | solution.py:20
  32.2 6.5 collective-permute-start.4
  50.7 24.8 %collective-permute-start.8 = (f32[4,18,1,128]{3,0,2,1:T(4,128)S(1)}, f32[4,18,1,128]{3,0,2,1:T(4,128)S(1)}, u32[]{:S(2)}, u32[]{:S(2)}) collective-permute-start(f32[4,18,1,128]{3,0,2,1:T(4,128)S(1)} %copy.985), channel_id=1, source_target_pairs={{16,0},{32,16},{48,32},{64,48},{80,64},{96,80},{112,96},{17,1},{33... | collective-permute-start | bytes 110600 | tf_op jit(solution)/shard_map/ppermute | solution.py:21
  53.9 21.7 %collective-permute-start.9 = (f32[4,18,1,128]{3,0,2,1:T(4,128)S(1)}, f32[4,18,1,128]{3,0,2,1:T(4,128)S(1)}, u32[]{:S(2)}, u32[]{:S(2)}) collective-permute-start(f32[4,18,1,128]{3,0,2,1:T(4,128)S(1)} %copy.987), channel_id=1, source_target_pairs={{0,16},{16,32},{32,48},{48,64},{64,80},{80,96},{96,112},{1,17},{17... | collective-permute-start | bytes 110600 | tf_op jit(solution)/shard_map/ppermute | solution.py:20
  76.6 23.1 %collective-permute-start.11 = (f32[4,18,18,1]{2,0,3,1:T(4,128)S(1)}, f32[4,18,18,1]{2,0,3,1:T(4,128)S(1)}, u32[]{:S(2)}, u32[]{:S(2)}) collective-permute-start(f32[4,18,18,1]{2,0,3,1:T(4,128)S(1)} %copy.993), channel_id=1, source_target_pairs={{0,1},{1,2},{2,3},{3,4},{4,5},{5,6},{6,7},{7,8},{8,9},{9,10},{10,1... | collective-permute-start | bytes 15560 | tf_op jit(solution)/shard_map/ppermute | solution.py:20
  81.3 18.9 %collective-permute-start.10 = (f32[4,18,18,1]{2,0,3,1:T(4,128)S(1)}, f32[4,18,18,1]{2,0,3,1:T(4,128)S(1)}, u32[]{:S(2)}, u32[]{:S(2)}) collective-permute-start(f32[4,18,18,1]{2,0,3,1:T(4,128)S(1)} %copy.991), channel_id=1, source_target_pairs={{1,0},{2,1},{3,2},{4,3},{5,4},{6,5},{7,6},{8,7},{9,8},{10,9},{11,1... | collective-permute-start | bytes 15560 | tf_op jit(solution)/shard_map/ppermute | solution.py:21
  139.5 11.1 %collective-permute-start.16 = (f32[4,10,10,1]{3,0,2,1:T(4,128)S(1)}, f32[4,10,10,1]{3,0,2,1:T(4,128)S(1)}, u32[]{:S(2)}, u32[]{:S(2)}) collective-permute-start(f32[4,10,10,1]{3,0,2,1:T(4,128)S(1)} %get-tuple-element.101), channel_id=1, source_target_pairs={{1,0},{2,1},{3,2},{4,3},{5,4},{6,5},{7,6},{8,7},{9,8},{10,9},{11,1... | collective-permute-start | bytes 4808 | tf_op jit(solution)/shard_map/ppermute | solution.py:21
  142.5 9.3 %collective-permute-start.17 = (f32[4,10,10,1]{3,0,2,1:T(4,128)S(1)}, f32[4,10,10,1]{3,0,2,1:T(4,128)S(1)}, u32[]{:S(2)}, u32[]{:S(2)}) collective-permute-start(f32[4,10,10,1]{3,0,2,1:T(4,128)S(1)} %get-tuple-element.102), channel_id=1, source_target_pairs={{0,1},{1,2},{2,3},{3,4},{4,5},{5,6},{6,7},{7,8},{8,9},{9,10},{10,1... | collective-permute-start | bytes 4808 | tf_op jit(solution)/shard_map/ppermute | solution.py:20
  167.5 11.6 %collective-permute-start.22 = (f32[4,10,10,1]{3,0,2,1:T(4,128)S(1)}, f32[4,10,10,1]{3,0,2,1:T(4,128)S(1)}, u32[]{:S(2)}, u32[]{:S(2)}) collective-permute-start(f32[4,10,10,1]{3,0,2,1:T(4,128)S(1)} %get-tuple-element.97), channel_id=1, source_target_pairs={{1,0},{2,1},{3,2},{4,3},{5,4},{6,5},{7,6},{8,7},{9,8},{10,9},{11,1... | collective-permute-start | bytes 4808 | tf_op jit(solution)/shard_map/ppermute | solution.py:21
  169.8 10.4 %collective-permute-start.23 = (f32[4,10,10,1]{3,0,2,1:T(4,128)S(1)}, f32[4,10,10,1]{3,0,2,1:T(4,128)S(1)}, u32[]{:S(2)}, u32[]{:S(2)}) collective-permute-start(f32[4,10,10,1]{3,0,2,1:T(4,128)S(1)} %get-tuple-element.98), channel_id=1, source_target_pairs={{0,1},{1,2},{2,3},{3,4},{4,5},{5,6},{6,7},{7,8},{8,9},{9,10},{10,1... | collective-permute-start | bytes 4808 | tf_op jit(solution)/shard_map/ppermute | solution.py:20
  192.6 6.7 collective-permute-start.26
  197.2 7.2 %collective-permute-start.27 = (f32[4,6,1,32]{0,3,2,1:T(8,128)S(1)}, f32[4,6,1,32]{0,3,2,1:T(8,128)S(1)}, u32[]{:S(2)}, u32[]{:S(2)}) collective-permute-start(f32[4,6,1,32]{0,3,2,1:T(8,128)S(1)} %get-tuple-element.75), channel_id=1, source_target_pairs={{0,16},{16,32},{32,48},{48,64},{64,80},{80,96},{96,112},{1,17},{17... | collective-permute-start | bytes 9224 | tf_op jit(solution)/shard_map/ppermute | solution.py:20
  204.6 10.1 %collective-permute-start.28 = (f32[4,6,6,1]{3,0,2,1:T(4,128)S(1)}, f32[4,6,6,1]{3,0,2,1:T(4,128)S(1)}, u32[]{:S(2)}, u32[]{:S(2)}) collective-permute-start(f32[4,6,6,1]{3,0,2,1:T(4,128)S(1)} %get-tuple-element.139), channel_id=1, source_target_pairs={{1,0},{2,1},{3,2},{4,3},{5,4},{6,5},{7,6},{8,7},{9,8},{10,9},{11,1... | collective-permute-start | bytes 1736 | tf_op jit(solution)/shard_map/ppermute | solution.py:21
  206.5 9.5 %collective-permute-start.29 = (f32[4,6,6,1]{3,0,2,1:T(4,128)S(1)}, f32[4,6,6,1]{3,0,2,1:T(4,128)S(1)}, u32[]{:S(2)}, u32[]{:S(2)}) collective-permute-start(f32[4,6,6,1]{3,0,2,1:T(4,128)S(1)} %get-tuple-element.140), channel_id=1, source_target_pairs={{0,1},{1,2},{2,3},{3,4},{4,5},{5,6},{6,7},{7,8},{8,9},{9,10},{10,1... | collective-permute-start | bytes 1736 | tf_op jit(solution)/shard_map/ppermute | solution.py:20
  225.4 7.0 %collective-permute-start.32 = (f32[4,6,1,32]{0,3,2,1:T(8,128)S(1)}, f32[4,6,1,32]{0,3,2,1:T(8,128)S(1)}, u32[]{:S(2)}, u32[]{:S(2)}) collective-permute-start(f32[4,6,1,32]{0,3,2,1:T(8,128)S(1)} %get-tuple-element.74), channel_id=1, source_target_pairs={{16,0},{32,16},{48,32},{64,48},{80,64},{96,80},{112,96},{17,1},{33... | collective-permute-start | bytes 9224 | tf_op jit(solution)/shard_map/ppermute | solution.py:21
  230.2 5.4 collective-permute-start.33
  235.8 10.4 %collective-permute-start.34 = (f32[4,6,6,1]{3,0,2,1:T(4,128)S(1)}, f32[4,6,6,1]{3,0,2,1:T(4,128)S(1)}, u32[]{:S(2)}, u32[]{:S(2)}) collective-permute-start(f32[4,6,6,1]{3,0,2,1:T(4,128)S(1)} %get-tuple-element.135), channel_id=1, source_target_pairs={{1,0},{2,1},{3,2},{4,3},{5,4},{6,5},{7,6},{8,7},{9,8},{10,9},{11,1... | collective-permute-start | bytes 1736 | tf_op jit(solution)/shard_map/ppermute | solution.py:21
  237.8 9.7 %collective-permute-start.35 = (f32[4,6,6,1]{3,0,2,1:T(4,128)S(1)}, f32[4,6,6,1]{3,0,2,1:T(4,128)S(1)}, u32[]{:S(2)}, u32[]{:S(2)}) collective-permute-start(f32[4,6,6,1]{3,0,2,1:T(4,128)S(1)} %get-tuple-element.136), channel_id=1, source_target_pairs={{0,1},{1,2},{2,3},{3,4},{4,5},{5,6},{6,7},{7,8},{8,9},{9,10},{10,1... | collective-permute-start | bytes 1736 | tf_op jit(solution)/shard_map/ppermute | solution.py:20
  255.9 5.4 collective-permute-start.38
  263.7 10.3 %collective-permute-start.40 = (f32[4,4,4,1]{3,2,1,0:T(4,128)S(1)}, f32[4,4,4,1]{3,2,1,0:T(4,128)S(1)}, u32[]{:S(2)}, u32[]{:S(2)}) collective-permute-start(f32[4,4,4,1]{3,2,1,0:T(4,128)S(1)} %get-tuple-element.169), channel_id=1, source_target_pairs={{1,0},{2,1},{3,2},{4,3},{5,4},{6,5},{7,6},{8,7},{9,8},{10,9},{11,1... | collective-permute-start | bytes 776 | tf_op jit(solution)/shard_map/ppermute | solution.py:21
  265.6 9.4 %collective-permute-start.41 = (f32[4,4,4,1]{3,2,1,0:T(4,128)S(1)}, f32[4,4,4,1]{3,2,1,0:T(4,128)S(1)}, u32[]{:S(2)}, u32[]{:S(2)}) collective-permute-start(f32[4,4,4,1]{3,2,1,0:T(4,128)S(1)} %get-tuple-element.170), channel_id=1, source_target_pairs={{0,1},{1,2},{2,3},{3,4},{4,5},{5,6},{6,7},{7,8},{8,9},{9,10},{10,1... | collective-permute-start | bytes 776 | tf_op jit(solution)/shard_map/ppermute | solution.py:20
  283.3 5.4 collective-permute-start.44
  291.0 10.2 %collective-permute-start.46 = (f32[4,4,4,1]{3,2,1,0:T(4,128)S(1)}, f32[4,4,4,1]{3,2,1,0:T(4,128)S(1)}, u32[]{:S(2)}, u32[]{:S(2)}) collective-permute-start(f32[4,4,4,1]{3,2,1,0:T(4,128)S(1)} %get-tuple-element.163), channel_id=1, source_target_pairs={{1,0},{2,1},{3,2},{4,3},{5,4},{6,5},{7,6},{8,7},{9,8},{10,9},{11,1... | collective-permute-start | bytes 776 | tf_op jit(solution)/shard_map/ppermute | solution.py:21
  293.0 9.3 %collective-permute-start.47 = (f32[4,4,4,1]{3,2,1,0:T(4,128)S(1)}, f32[4,4,4,1]{3,2,1,0:T(4,128)S(1)}, u32[]{:S(2)}, u32[]{:S(2)}) collective-permute-start(f32[4,4,4,1]{3,2,1,0:T(4,128)S(1)} %get-tuple-element.164), channel_id=1, source_target_pairs={{0,1},{1,2},{2,3},{3,4},{4,5},{5,6},{6,7},{7,8},{8,9},{9,10},{10,1... | collective-permute-start | bytes 776 | tf_op jit(solution)/shard_map/ppermute | solution.py:20
  455.8 5.4 collective-permute-start.50
  463.5 7.7 %collective-permute-start.52 = (f32[4,4,4,1]{3,2,1,0:T(4,128)S(1)}, f32[4,4,4,1]{3,2,1,0:T(4,128)S(1)}, u32[]{:S(2)}, u32[]{:S(2)}) collective-permute-start(f32[4,4,4,1]{3,2,1,0:T(4,128)S(1)} %get-tuple-element.157), channel_id=1, source_target_pairs={{1,0},{2,1},{3,2},{4,3},{5,4},{6,5},{7,6},{8,7},{9,8},{10,9},{11,1... | collective-permute-start | bytes 776 | tf_op jit(solution)/shard_map/ppermute | solution.py:21
  480.8 6.1 collective-permute-start.56
  489.7 10.2 %collective-permute-start.58 = (f32[4,4,4,1]{3,2,1,0:T(4,128)S(1)}, f32[4,4,4,1]{3,2,1,0:T(4,128)S(1)}, u32[]{:S(2)}, u32[]{:S(2)}) collective-permute-start(f32[4,4,4,1]{3,2,1,0:T(4,128)S(1)} %get-tuple-element.151), channel_id=1, source_target_pairs={{1,0},{2,1},{3,2},{4,3},{5,4},{6,5},{7,6},{8,7},{9,8},{10,9},{11,1... | collective-permute-start | bytes 776 | tf_op jit(solution)/shard_map/ppermute | solution.py:21
  495.6 5.4 collective-permute-start.59
  506.2 5.9 collective-permute-start.61
  512.2 5.7 collective-permute-start.62
  514.4 5.4 collective-permute-start.63
  520.0 10.0 %collective-permute-start.64 = (f32[4,6,6,1]{3,0,2,1:T(4,128)S(1)}, f32[4,6,6,1]{3,0,2,1:T(4,128)S(1)}, u32[]{:S(2)}, u32[]{:S(2)}) collective-permute-start(f32[4,6,6,1]{3,0,2,1:T(4,128)S(1)} %get-tuple-element.131), channel_id=1, source_target_pairs={{1,0},{2,1},{3,2},{4,3},{5,4},{6,5},{7,6},{8,7},{9,8},{10,9},{11,1... | collective-permute-start | bytes 1736 | tf_op jit(solution)/shard_map/ppermute | solution.py:21
  524.8 6.6 collective-permute-start.65
  535.7 5.7 collective-permute-start.67
  541.5 5.9 collective-permute-start.68
  550.0 9.7 %collective-permute-start.70 = (f32[4,6,6,1]{3,0,2,1:T(4,128)S(1)}, f32[4,6,6,1]{3,0,2,1:T(4,128)S(1)}, u32[]{:S(2)}, u32[]{:S(2)}) collective-permute-start(f32[4,6,6,1]{3,0,2,1:T(4,128)S(1)} %get-tuple-element.127), channel_id=1, source_target_pairs={{1,0},{2,1},{3,2},{4,3},{5,4},{6,5},{7,6},{8,7},{9,8},{10,9},{11,1... | collective-permute-start | bytes 1736 | tf_op jit(solution)/shard_map/ppermute | solution.py:21
  553.7 7.2 %collective-permute-start.71 = (f32[4,6,6,1]{3,0,2,1:T(4,128)S(1)}, f32[4,6,6,1]{3,0,2,1:T(4,128)S(1)}, u32[]{:S(2)}, u32[]{:S(2)}) collective-permute-start(f32[4,6,6,1]{3,0,2,1:T(4,128)S(1)} %get-tuple-element.128), channel_id=1, source_target_pairs={{0,1},{1,2},{2,3},{3,4},{4,5},{5,6},{6,7},{7,8},{8,9},{9,10},{10,1... | collective-permute-start | bytes 1736 | tf_op jit(solution)/shard_map/ppermute | solution.py:20
  577.2 11.8 %collective-permute-start.76 = (f32[4,10,10,1]{3,0,2,1:T(4,128)S(1)}, f32[4,10,10,1]{3,0,2,1:T(4,128)S(1)}, u32[]{:S(2)}, u32[]{:S(2)}) collective-permute-start(f32[4,10,10,1]{3,0,2,1:T(4,128)S(1)} %get-tuple-element.93), channel_id=1, source_target_pairs={{1,0},{2,1},{3,2},{4,3},{5,4},{6,5},{7,6},{8,7},{9,8},{10,9},{11,1... | collective-permute-start | bytes 4808 | tf_op jit(solution)/shard_map/ppermute | solution.py:21
  580.5 9.7 %collective-permute-start.77 = (f32[4,10,10,1]{3,0,2,1:T(4,128)S(1)}, f32[4,10,10,1]{3,0,2,1:T(4,128)S(1)}, u32[]{:S(2)}, u32[]{:S(2)}) collective-permute-start(f32[4,10,10,1]{3,0,2,1:T(4,128)S(1)} %get-tuple-element.94), channel_id=1, source_target_pairs={{0,1},{1,2},{2,3},{3,4},{4,5},{5,6},{6,7},{7,8},{8,9},{9,10},{10,1... | collective-permute-start | bytes 4808 | tf_op jit(solution)/shard_map/ppermute | solution.py:20
  605.2 11.9 %collective-permute-start.82 = (f32[4,10,10,1]{3,0,2,1:T(4,128)S(1)}, f32[4,10,10,1]{3,0,2,1:T(4,128)S(1)}, u32[]{:S(2)}, u32[]{:S(2)}) collective-permute-start(f32[4,10,10,1]{3,0,2,1:T(4,128)S(1)} %get-tuple-element.89), channel_id=1, source_target_pairs={{1,0},{2,1},{3,2},{4,3},{5,4},{6,5},{7,6},{8,7},{9,8},{10,9},{11,1... | collective-permute-start | bytes 4808 | tf_op jit(solution)/shard_map/ppermute | solution.py:21
  607.4 10.9 %collective-permute-start.83 = (f32[4,10,10,1]{3,0,2,1:T(4,128)S(1)}, f32[4,10,10,1]{3,0,2,1:T(4,128)S(1)}, u32[]{:S(2)}, u32[]{:S(2)}) collective-permute-start(f32[4,10,10,1]{3,0,2,1:T(4,128)S(1)} %get-tuple-element.90), channel_id=1, source_target_pairs={{0,1},{1,2},{2,3},{3,4},{4,5},{5,6},{6,7},{7,8},{8,9},{9,10},{10,1... | collective-permute-start | bytes 4808 | tf_op jit(solution)/shard_map/ppermute | solution.py:20
  637.2 6.5 collective-permute-start.87
  644.7 10.6 %collective-permute-start.89 = (f32[4,18,18,1]{2,0,3,1:T(4,128)S(1)}, f32[4,18,18,1]{2,0,3,1:T(4,128)S(1)}, u32[]{:S(2)}, u32[]{:S(2)}) collective-permute-start(f32[4,18,18,1]{2,0,3,1:T(4,128)S(1)} %copy.1097), channel_id=1, source_target_pairs={{0,1},{1,2},{2,3},{3,4},{4,5},{5,6},{6,7},{7,8},{8,9},{9,10},{10,1... | collective-permute-start | bytes 15560 | tf_op jit(solution)/shard_map/ppermute | solution.py:20
  653.4 6.5 collective-permute-start.88
  671.1 6.8 collective-permute-start.92
  683.8 7.2 %collective-permute-start.95 = (f32[4,18,18,1]{2,0,3,1:T(4,128)S(1)}, f32[4,18,18,1]{2,0,3,1:T(4,128)S(1)}, u32[]{:S(2)}, u32[]{:S(2)}) collective-permute-start(f32[4,18,18,1]{2,0,3,1:T(4,128)S(1)} %copy.1107), channel_id=1, source_target_pairs={{0,1},{1,2},{2,3},{3,4},{4,5},{5,6},{6,7},{7,8},{8,9},{9,10},{10,1... | collective-permute-start | bytes 15560 | tf_op jit(solution)/shard_map/ppermute | solution.py:20
  689.1 6.5 collective-permute-start.94
  (63 other events, 1108.6 us)
where the time goes:
time: 711 us; the launch traced here: 700 us
  starting transfers between devices  311 us (44%)
  blocking collectives  130 us (18%)
  waiting for transfers between devices  123 us (17%)
  local copies, waits for them, and re-layouts  80 us (11%)
  other arithmetic  52.7 us (7%)
    ppermute x48, starting transfers between devices, extended(): before = lax.ppermute(last, axis, up)  165 us
    ppermute x48, starting transfers between devices, extended(): after = lax.ppermute(leading, axis, down)  146 us
    ppermute x48, waiting for transfers between devices, extended(): before = lax.ppermute(last, axis, up)  98.7 us
    all_gather x1, blocking collectives, merged(): lax.all_gather(coef_four.reshape(1, -1), ('gx', 'gy', 'gz'), axis=0, tile...  66 us
    all_gather x1, blocking collectives, merged(): lax.all_gather(side_four.reshape(1, -1), ('gx', 'gy', 'gz'), axis=0, tile...  64.4 us
    reduce_sum x9, other arithmetic, coarsen(): return shaped.sum(axis=(2, 4, 6))  31.2 us
    ppermute x48, waiting for transfers between devices, extended(): after = lax.ppermute(leading, axis, down)  24.5 us
    another operation x2, local copies, waits for them, and re-layouts, shards(): coef_zero = jnp.stack([viscosity, viscosity, viscosity, 1.0 / viscosity])  19.5 us
  transfers between devices with their start and end apart: 96, of which 57 were waited for; matrix products, arithmetic and copies ran while one was open for 6% of the time, Pallas kernels for 0%

commit v1 on v0

v1 whole, which is shorter than its diff:
```python
import functools

import jax
import jax.numpy as jnp
import numpy as np
from jax import lax
from jax.experimental import pallas as pl
from jax.experimental.pallas import tpu as pltpu
from jax.sharding import PartitionSpec as P

F32 = jnp.float32
COARSE_ITERS = 8
TAU = 0.8 / 6.0
LANES = 128
HX0, HY0, HZ0 = 10, 3, 16
Y0 = 16 + 2 * HY0
Y1 = 16
HZ2 = 10
HZ3 = 20


def mm(a, b):
    return jnp.dot(a, b, precision=lax.Precision.HIGHEST, preferred_element_type=F32)


def lane_of(n):
    return lax.broadcasted_iota(jnp.int32, (n, LANES), 1)


def lane_roll(x, shift):
    return pltpu.roll(x, shift % LANES, 1) if shift % LANES else x


def around(ref, x, row, n):
    mid = ref[x, pl.ds(row, n), :]
    total = ref[x - 1, pl.ds(row, n), :] + ref[x + 1, pl.ds(row, n), :]
    total = total + (ref[x, pl.ds(row - 1, n), :] + ref[x, pl.ds(row + 1, n), :])
    return mid, total + (lane_roll(mid, 1) + lane_roll(mid, -1))


def around_whole(ref, x, row, n, width):
    mid = ref[x, pl.ds(row, n), :]
    total = ref[x - 1, pl.ds(row, n), :] + ref[x + 1, pl.ds(row, n), :]
    total = total + (ref[x, pl.ds(row - 1, n), :] + ref[x, pl.ds(row + 1, n), :])
    place = lane_of(n) % width
    total = total + jnp.where(place == 0, 0.0, lane_roll(mid, 1))
    return mid, total + jnp.where(place == width - 1, 0.0, lane_roll(mid, -1))


def chunks(n, size):
    return [(r, min(size, n - r)) for r in range(0, n, size)]


def roots_of(c):
    live = c > 0.0
    inv = lax.rsqrt(jnp.where(live, c, 1.0))
    return jnp.where(live, c * inv, 0.0), jnp.where(live, inv, 0.0)


def inverse(root):
    live = root > 0.0
    return jnp.where(live, 1.0 / jnp.where(live, root, 1.0), 0.0)


def jacobi(live, mid, beta, total):
    return jnp.where(live, 0.2 * mid + beta + TAU * total, 0.0)


def pair_lanes(width, start, fields, out_width, out_start, scale, first=0):
    m = np.zeros((LANES, LANES), np.float32)
    for k, f in enumerate(fields):
        for j in range(out_width):
            for i in range(2):
                m[f * width + start + 2 * j + i, out_start + k * out_width + j] = scale
    return m


def repeat_lanes(width, shift, out_width, out_shift):
    m = np.zeros((LANES, LANES), np.float32)
    for f in range(4):
        for j in range(out_width):
            i = shift + (j - out_shift) // 2
            if 0 <= i < width:
                m[f * width + i, f * out_width + j] = 1.0
    return m


def rows_kernel(xlo, source, visc, xhi, rows, ylo, yhi):
    def put(x, f, plane):
        rows[x, pl.ds(f * Y0 + HY0, 16), :] = plane
        ylo[x, pl.ds(f * HY0, HY0), :] = plane[0:HY0]
        yhi[x, pl.ds(f * HY0, HY0), :] = plane[16 - HY0 : 16]

    def edge(x, carry):
        for f in range(5):
            put(x, f, xlo[f, x])
            put(x + HX0 + 16, f, xhi[f, x])
        return carry

    def own(x, carry):
        for f in range(4):
            put(x + HX0, f, source[f, x])
        put(x + HX0, 4, visc[x])
        return carry

    lax.fori_loop(0, HX0, edge, 0)
    lax.fori_loop(0, 16, own, 0)


def turn_kernel(rows, ylo, yhi, turned, zlo, zhi, stage):
    stage[...] = jnp.zeros_like(stage)

    def body(x, carry):
        stage[pl.ds(0, 5 * Y0), :] = rows[x, pl.ds(0, 5 * Y0), :]
        for f in range(5):
            stage[pl.ds(f * Y0, HY0), :] = ylo[x, pl.ds(f * HY0, HY0), :]
            stage[pl.ds(f * Y0 + HY0 + 16, HY0), :] = yhi[x, pl.ds(f * HY0, HY0), :]
        t = stage[...].T
        turned[x] = t
        zlo[x] = t[0:HZ0]
        zhi[x] = t[128 - HZ0 : 128]
        return carry

    lax.fori_loop(0, 16 + 2 * HX0, body, 0)


def down0_kernel(turned, zlo, zhi, qb, qc, out, ylo, yhi, w_kept, beta_kept, root_kept, beta, w, root, rsum, csum, rz, cz, stage):
    planes = 16 + 2 * HX0
    depth = 128 + 2 * HZ0
    beta[:, pl.ds(0, 8), :] = jnp.zeros((planes, 8, LANES), F32)
    beta[:, pl.ds(8 + depth, 8), :] = jnp.zeros((planes, 8, LANES), F32)
    w[:, pl.ds(0, 8), :] = jnp.zeros((planes, 8, LANES), F32)
    w[:, pl.ds(8 + depth, 8), :] = jnp.zeros((planes, 8, LANES), F32)

    def prepare(x, t, row, n):
        lane = lane_of(n)
        v = jnp.zeros_like(t)
        for f in range(4):
            v = jnp.where((lane >= f * Y0) & (lane < (f + 1) * Y0), lane_roll(t, f * Y0 - 4 * Y0), v)
        root_v, inv_v = roots_of(v)
        pressure = lane >= 3 * Y0
        root_x = jnp.where(pressure, inv_v, root_v)
        inv_x = jnp.where(pressure, root_v, inv_v)
        root[x, pl.ds(row, n), :] = root_x
        beta[x, pl.ds(8 + row, n), :] = TAU * t * inv_x

    def setup(x, carry):
        prepare(x, zlo[x], 0, HZ0)
        for r, n in chunks(128, 32):
            prepare(x, turned[x, pl.ds(r, n), :], HZ0 + r, n)
        prepare(x, zhi[x], HZ0 + 128, HZ0)
        return carry

    lax.fori_loop(0, planes, setup, 0)

    def smooth(x, carry):
        for r, n in chunks(depth, 32):
            mid, total = around(beta, x, 8 + r, n)
            w[x, pl.ds(8 + r, n), :] = jnp.where(root[x, pl.ds(r, n), :] > 0.0, 1.2 * mid + TAU * total, 0.0)
        return carry

    lax.fori_loop(1, planes - 1, smooth, 0)

    def restrict(k, carry):
        for r, n in chunks(depth, 32):
            res = jnp.zeros((n, LANES), F32)
            coef = jnp.zeros((n, LANES), F32)
            for i in range(2):
                x = 2 + 2 * k + i
                mid, total = around(w, x, 8 + r, n)
                root_x = root[x, pl.ds(r, n), :]
                res = res + root_x * ((1.0 / TAU) * beta[x, pl.ds(8 + r, n), :] - 6.0 * mid + total)
                coef = coef + root_x * root_x
            rsum[pl.ds(r, n), :] = res
            csum[pl.ds(r, n), :] = coef
        half = depth // 2
        rz[k] = rsum[pl.ds(0, half, stride=2), :] + rsum[pl.ds(1, half, stride=2), :]
        cz[k] = csum[pl.ds(0, half, stride=2), :] + csum[pl.ds(1, half, stride=2), :]
        return carry

    lax.fori_loop(0, 16, restrict, 0)
    stage[...] = jnp.zeros_like(stage)

    def coarse(k, carry):
        stage[pl.ds(0, depth // 2), :] = mm(rz[k], qb[...]) + mm(cz[k], qc[...])
        t = stage[...].T
        out[k] = t[0:48]
        for a in range(6):
            ylo[k, pl.ds(a * 4, 4), :] = t[a * 8 : a * 8 + 4]
            yhi[k, pl.ds(a * 4, 4), :] = t[a * 8 + 4 : a * 8 + 8]
        return carry

    lax.fori_loop(0, 16, coarse, 0)

    def keep(x, carry):
        w_kept[x] = w[x + 8, pl.ds(16, 144), :]
        beta_kept[x] = beta[x + 8, pl.ds(16, 144), :]
        root_kept[x] = root[x + 8, pl.ds(8, 144), :]
        return carry

    lax.fori_loop(0, 20, keep, 0)


def down1_kernel(own, ylo, yhi, qb, qc, block, w, beta, root, stage, rz, cz, rsum, csum):
    beta[...] = jnp.zeros_like(beta)
    w[...] = jnp.zeros_like(w)
    stage[...] = jnp.zeros_like(stage)

    def setup(x, carry):
        for a in range(6):
            stage[pl.ds(a * Y1 + 4, 8), :] = own[x, pl.ds(a * 8, 8), :]
            stage[pl.ds(a * Y1, 4), :] = ylo[x, pl.ds(a * 4, 4), :]
            stage[pl.ds(a * Y1 + 12, 4), :] = yhi[x, pl.ds(a * 4, 4), :]
        t = stage[...].T[0:80]
        lane = lane_of(80)
        c = jnp.where(lane < Y1, lane_roll(t, 64), jnp.where(lane < 2 * Y1, lane_roll(t, 80), lane_roll(t, 96)))
        c = jnp.where(lane < 4 * Y1, c, 0.0)
        root_x, inv_x = roots_of(c)
        root[x] = root_x
        beta[x, pl.ds(8, 80), :] = TAU * t * inv_x
        return carry

    lax.fori_loop(0, 16, setup, 0)

    def smooth(x, carry):
        for r, n in chunks(80, 40):
            mid, total = around(beta, x, 8 + r, n)
            w[x, pl.ds(8 + r, n), :] = jnp.where(root[x, pl.ds(r, n), :] > 0.0, 1.2 * mid + TAU * total, 0.0)
        return carry

    lax.fori_loop(1, 15, smooth, 0)
    for k in range(4):
        for r, n in chunks(64, 32):
            res = jnp.zeros((n, LANES), F32)
            coef = jnp.zeros((n, LANES), F32)
            for i in range(2):
                x = 4 + 2 * k + i
                mid, total = around(w, x, 16 + r, n)
                root_x = root[x, pl.ds(8 + r, n), :]
                res = res + root_x * ((1.0 / TAU) * beta[x, pl.ds(16 + r, n), :] - 6.0 * mid + total)
                coef = coef + root_x * root_x
            rsum[pl.ds(r, n), :] = res
            csum[pl.ds(r, n), :] = coef
        rz[pl.ds(k * 32, 32), :] = rsum[pl.ds(0, 32, stride=2), :] + rsum[pl.ds(1, 32, stride=2), :]
        cz[pl.ds(k * 32, 32), :] = csum[pl.ds(0, 32, stride=2), :] + csum[pl.ds(1, 32, stride=2), :]
    block[...] = (mm(rz[...], qb[...]) + mm(cz[...], qc[...])).T[0:24]


def plane_kernel(gx, gy, got, b, c, zlo, zhi, stage_b, stage_c):
    width = 4 * gy
    stage_b[...] = jnp.zeros_like(stage_b)
    stage_c[...] = jnp.zeros_like(stage_c)
    lane = lane_of(LANES)

    def body(i, carry):
        for j in range(gy):
            for a in range(4):
                stage_b[pl.ds(a * width + 4 * j, 4), :] = got[i * gy + j, pl.ds(4 * a, 4), :]
            for a in range(2):
                stage_c[pl.ds(a * width + 4 * j, 4), :] = got[i * gy + j, pl.ds(16 + 4 * a, 4), :]
        tb = stage_b[...].T
        tc = stage_c[...].T
        c_all = jnp.where(lane < width, tc, jnp.where(lane < 2 * width, lane_roll(tc, width), lane_roll(tc, 2 * width)))
        c_all = jnp.where(lane < 4 * width, c_all, 0.0)
        for x in range(4):
            at = 4 * i + x
            b[at] = tb[x * 32 : (x + 1) * 32]
            c[at] = c_all[x * 32 : (x + 1) * 32]
            for which, t in ((0, tb), (1, c_all)):
                zlo[which, at] = t[x * 32 : x * 32 + HZ2]
                zhi[which, at] = t[(x + 1) * 32 - HZ2 : (x + 1) * 32]
        return carry

    lax.fori_loop(0, gx, body, 0)


def down2_kernel(gx, gy, b, c, zlo, zhi, qb, qc, out, zup, zdown, w, beta, root, plane_b, plane_c, rsum, csum, rz, cz):
    size_x, width = 4 * gx, 4 * gy
    beta[...] = jnp.zeros_like(beta)
    w[...] = jnp.zeros_like(w)
    plane_b[...] = jnp.zeros_like(plane_b)
    plane_c[...] = jnp.zeros_like(plane_c)

    def setup(x, carry):
        for which, plane, own in ((0, plane_b, b), (1, plane_c, c)):
            plane[pl.ds(16 - HZ2, HZ2), :] = zlo[which, x]
            plane[pl.ds(16, 32), :] = own[x]
            plane[pl.ds(48, HZ2), :] = zhi[which, x]
        root_x, inv_x = roots_of(plane_c[...])
        root[x] = root_x
        beta[x + 1, pl.ds(8, 64), :] = TAU * plane_b[...] * inv_x
        return carry

    lax.fori_loop(0, size_x, setup, 0)

    def smooth(x, carry):
        for r, n in chunks(64, 32):
            mid, total = around_whole(beta, x + 1, 8 + r, n, width)
            w[x + 1, pl.ds(8 + r, n), :] = jnp.where(root[x, pl.ds(r, n), :] > 0.0, 1.2 * mid + TAU * total, 0.0)
        return carry

    lax.fori_loop(0, size_x, smooth, 0)
    restrict_whole(size_x, width, w, beta, root, rsum, csum, rz, cz)

    def coarse(k, carry):
        t = mm(rz[k], qb[...]) + mm(cz[k], qc[...])
        out[k] = t
        zup[k] = t[24 - HZ3 : 24]
        zdown[k] = t[8 : 8 + HZ3]
        return carry

    lax.fori_loop(0, size_x // 2, coarse, 0)


def restrict_whole(size_x, width, w, beta, root, rsum, csum, rz, cz):
    def body(k, carry):
        for r, n in chunks(64, 32):
            res = jnp.zeros((n, LANES), F32)
            coef = jnp.zeros((n, LANES), F32)
            for i in range(2):
                x = 2 * k + i
                mid, total = around_whole(w, x + 1, 8 + r, n, width)
                root_x = root[x, pl.ds(r, n), :]
                res = res + root_x * ((1.0 / TAU) * beta[x + 1, pl.ds(8 + r, n), :] - 6.0 * mid + total)
                coef = coef + root_x * root_x
            rsum[pl.ds(r, n), :] = res
            csum[pl.ds(r, n), :] = coef
        rz[k] = rsum[pl.ds(0, 32, stride=2), :] + rsum[pl.ds(1, 32, stride=2), :]
        cz[k] = csum[pl.ds(0, 32, stride=2), :] + csum[pl.ds(1, 32, stride=2), :]
        return carry

    lax.fori_loop(0, size_x // 2, body, 0)


def relax_whole(size_x, depth, width, src, dst, beta, root):
    def body(x, carry):
        for r, n in chunks(depth, 32):
            mid, total = around_whole(src, x + 1, 8 + r, n, width)
            live = root[x, pl.ds(r, n), :] > 0.0
            dst[x + 1, pl.ds(8 + r, n), :] = jacobi(live, mid, beta[x + 1, pl.ds(8 + r, n), :], total)
        return carry

    lax.fori_loop(0, size_x, body, 0)


def coarse_kernel(gx, gy, own, zlo, zhi, w2, beta2, root2, q3b, q3c, u4, u3, e2, beta3, w3, v3, root3, beta4, w4, v4, root4, plane, fine, rsum, csum, rz, cz, v2, w2b):
    size_x, width = 2 * gx, 2 * gy
    for ref in (beta3, w3, v3, beta4, w4, v4, plane, v2, w2b):
        ref[...] = jnp.zeros_like(ref)

    def setup(x, carry):
        plane[pl.ds(24 - HZ3, HZ3), :] = zlo[x]
        plane[pl.ds(24, 16), :] = own[x, pl.ds(8, 16), :]
        plane[pl.ds(40, HZ3), :] = zhi[x]
        t = plane[...]
        root_x, inv_x = roots_of(jnp.where(lane_of(64) < 4 * width, lane_roll(t, 64), 0.0))
        root3[x] = root_x
        beta3[x + 1, pl.ds(8, 64), :] = TAU * t * inv_x
        return carry

    lax.fori_loop(0, size_x, setup, 0)

    def smooth(x, carry):
        for r, n in chunks(64, 32):
            mid, total = around_whole(beta3, x + 1, 8 + r, n, width)
            w3[x + 1, pl.ds(8 + r, n), :] = jnp.where(root3[x, pl.ds(r, n), :] > 0.0, 1.2 * mid + TAU * total, 0.0)
        return carry

    lax.fori_loop(0, size_x, smooth, 0)
    restrict_whole(size_x, width, w3, beta3, root3, rsum, csum, rz, cz)

    def start4(x, carry):
        t = mm(rz[x], q3b[...]) + mm(cz[x], q3c[...])
        root_x, inv_x = roots_of(jnp.where(lane_of(32) < 4 * gy, lane_roll(t, 64), 0.0))
        root4[x] = root_x
        beta4[x + 1, pl.ds(8, 32), :] = TAU * t * inv_x
        w4[x + 1, pl.ds(8, 32), :] = TAU * t * inv_x
        return carry

    lax.fori_loop(0, gx, start4, 0)
    here, there = w4, v4
    for step in range(COARSE_ITERS - 1):
        relax_whole(gx, 32, gy, here, there, beta4, root4)
        here, there = there, here

    def up3(x, carry):
        e = mm(here[x + 1, pl.ds(8, 32), :] * inverse(root4[x]), u4[...])
        fine[pl.ds(0, 32, stride=2), :] = e
        fine[pl.ds(1, 32, stride=2), :] = e
        for i in range(2):
            at = 2 * x + i
            w3[at + 1, pl.ds(8, 64), :] = w3[at + 1, pl.ds(8, 64), :] + root3[at] * fine[...]
        return carry

    lax.fori_loop(0, gx, up3, 0)
    relax_whole(size_x, 64, width, w3, v3, beta3, root3)
    relax_whole(size_x, 64, width, v3, w3, beta3, root3)

    def up2(x, carry):
        e = mm(w3[x + 1, pl.ds(24, 32), :] * inverse(root3[x, pl.ds(16, 32), :]), u3[...])
        fine[pl.ds(0, 32, stride=2), :] = e
        fine[pl.ds(1, 32, stride=2), :] = e
        for i in range(2):
            at = 2 * x + i
            w2b[at + 1, pl.ds(8, 64), :] = w2[at + 1, pl.ds(8, 64), :] + root2[at] * fine[...]
        return carry

    lax.fori_loop(0, size_x, up2, 0)
    relax_whole(2 * size_x, 64, 2 * width, w2b, v2, beta2, root2)
    relax_whole(2 * size_x, 64, 2 * width, v2, w2b, beta2, root2)
    e2[pl.ds(0, 2), :, :] = jnp.zeros((2, 40, LANES), F32)
    e2[pl.ds(2 * size_x + 2, 2), :, :] = jnp.zeros((2, 40, LANES), F32)

    def finish(x, carry):
        e2[x + 2] = w2b[x + 1, pl.ds(20, 40), :] * inverse(root2[x, pl.ds(12, 40), :])
        return carry

    lax.fori_loop(0, 2 * size_x, finish, 0)


def up_kernel(place, e2, w1, beta1, root1, w0, beta0, root0, u2, u1, out, w1b, v1, w0b, v0, fine1, fine0):
    for ref in (w1b, v1, w0b, v0):
        ref[...] = jnp.zeros_like(ref)
    first = 4 * place[0]

    def up1(k, carry):
        e = mm(e2[first + k], u2[...])
        fine1[pl.ds(0, 40, stride=2), :] = e
        fine1[pl.ds(1, 40, stride=2), :] = e
        for i in range(2):
            x = 2 * k + i
            w1b[x, pl.ds(8, 80), :] = w1[x, pl.ds(8, 80), :] + root1[x] * fine1[...]
        return carry

    lax.fori_loop(0, 8, up1, 0)

    def relax1(src, dst, begin, end):
        def body(x, carry):
            for r, n in chunks(80, 40):
                mid, total = around(src, x, 8 + r, n)
                live = root1[x, pl.ds(r, n), :] > 0.0
                dst[x, pl.ds(8 + r, n), :] = jacobi(live, mid, beta1[x, pl.ds(8 + r, n), :], total)
            return carry

        lax.fori_loop(begin, end, body, 0)

    relax1(w1b, v1, 2, 14)
    relax1(v1, w1b, 3, 13)

    def up0(k, carry):
        x1 = k + 3
        e = mm(w1b[x1, pl.ds(12, 72), :] * inverse(root1[x1, pl.ds(4, 72), :]), u1[...])
        fine0[pl.ds(0, 72, stride=2), :] = e
        fine0[pl.ds(1, 72, stride=2), :] = e
        for i in range(2):
            x = 2 * k + i
            for r, n in chunks(144, 48):
                w0b[x, pl.ds(8 + r, n), :] = w0[x, pl.ds(r, n), :] + root0[x, pl.ds(r, n), :] * fine0[pl.ds(r, n), :]
        return carry

    lax.fori_loop(0, 10, up0, 0)

    def first0(x, carry):
        for r, n in chunks(144, 24):
            mid, total = around(w0b, x, 8 + r, n)
            live = root0[x, pl.ds(r, n), :] > 0.0
            v0[x, pl.ds(8 + r, n), :] = jacobi(live, mid, beta0[x, pl.ds(r, n), :], total)
        return carry

    lax.fori_loop(1, 19, first0, 0)

    def last0(k, carry):
        x = k + 2
        for r, n in chunks(128, 32):
            mid, total = around(v0, x, 16 + r, n)
            root_x = root0[x, pl.ds(8 + r, n), :]
            fine0[pl.ds(r, n), :] = jacobi(root_x > 0.0, mid, beta0[x, pl.ds(8 + r, n), :], total) * inverse(root_x)
        t = fine0[pl.ds(0, 128), :].T
        for f in range(4):
            out[f, k] = t[f * Y0 + HY0 : f * Y0 + HY0 + 16]
        return carry

    lax.fori_loop(0, 16, last0, 0)


def call(kernel, args, outs, scratch, smem=0):
    vmem = pl.BlockSpec(memory_space=pltpu.VMEM)
    scalar = pl.BlockSpec(memory_space=pltpu.SMEM)
    return pl.pallas_call(
        kernel,
        out_shape=[jax.ShapeDtypeStruct(s, F32) for s in outs],
        in_specs=[scalar] * smem + [vmem] * (len(args) - smem),
        out_specs=[vmem] * len(outs),
        scratch_shapes=[pltpu.VMEM(s, F32) for s in scratch],
        compiler_params=pltpu.CompilerParams(vmem_limit_bytes=60 * 1024 * 1024),
    )(*args)


def swap(to_up, to_down, axis):
    n = lax.axis_size(axis)
    from_below = lax.ppermute(to_up, axis, [(i, i + 1) for i in range(n - 1)])
    from_above = lax.ppermute(to_down, axis, [(i + 1, i) for i in range(n - 1)])
    return from_below, from_above


def shards(source, material_ids, material_table, roughness):
    gx, gy = lax.axis_size("gx"), lax.axis_size("gy")
    choices_of = jnp.arange(material_table.shape[0], dtype=jnp.int32)
    matches = (material_ids[..., None] == choices_of).astype(F32)
    block_visc = jnp.sum(matches * material_table, axis=-1)
    along_z = jnp.repeat(block_visc, 8, axis=2)
    visc = (jnp.broadcast_to(along_z[:, None, :, None, :], (2, 8, 2, 8, 128)).reshape(16, 16, 128)) * roughness

    low = jnp.concatenate([source[:, :HX0], visc[None, :HX0]], axis=0)
    high = jnp.concatenate([source[:, 16 - HX0 :], visc[None, 16 - HX0 :]], axis=0)
    xlo, xhi = swap(high, low, "gx")
    planes = 16 + 2 * HX0
    rows, ysend_lo, ysend_hi = call(
        rows_kernel, (xlo, source, visc, xhi), [(planes, 112, LANES), (planes, 16, LANES), (planes, 16, LANES)], []
    )
    ylo, yhi = swap(ysend_hi, ysend_lo, "gy")
    turned, zsend_lo, zsend_hi = call(
        turn_kernel,
        (rows, ylo, yhi),
        [(planes, 128, LANES), (planes, HZ0, LANES), (planes, HZ0, LANES)],
        [(LANES, LANES)],
    )
    zlo, zhi = swap(zsend_hi, zsend_lo, "gz")

    q0b = pair_lanes(Y0, HY0, (0, 1, 2, 3), 8, 0, 0.5)
    q0c = pair_lanes(Y0, HY0, (0, 3), 8, 32, 0.125)
    depth = 128 + 2 * HZ0
    own1, ysend_lo, ysend_hi, w0, beta0, root0 = call(
        down0_kernel,
        (turned, zlo, zhi, q0b, q0c),
        [(16, 48, LANES), (16, 24, LANES), (16, 24, LANES)] + [(20, 144, LANES)] * 3,
        [(planes, depth + 16, LANES)] * 2
        + [(planes, depth, LANES)]
        + [(depth, LANES)] * 2
        + [(16, depth // 2, LANES)] * 2
        + [(LANES, LANES)],
    )
    ylo, yhi = swap(ysend_hi, ysend_lo, "gy")

    q1b = pair_lanes(Y1, 4, (0, 1, 2, 3), 4, 0, 0.5)
    q1c = pair_lanes(Y1, 4, (0, 3), 4, 16, 0.125)
    block, w1, beta1, root1 = call(
        down1_kernel,
        (own1, ylo, yhi, q1b, q1c),
        [(24, LANES), (16, 96, LANES), (16, 96, LANES), (16, 80, LANES)],
        [(LANES, LANES)] * 3 + [(64, LANES)] * 2,
    )
    spread = jnp.broadcast_to(block[None], (gx * gy, 24, LANES))
    got = lax.all_to_all(spread, ("gx", "gy"), 0, 0, tiled=True)

    x2, x3 = 4 * gx, 2 * gx
    b2, c2, zsend_lo, zsend_hi = call(
        functools.partial(plane_kernel, gx, gy),
        (got,),
        [(x2, 32, LANES)] * 2 + [(2, x2, HZ2, LANES)] * 2,
        [(LANES, LANES)] * 2,
    )
    zlo, zhi = swap(zsend_hi, zsend_lo, "gz")

    q2b = pair_lanes(4 * gy, 0, (0, 1, 2, 3), 2 * gy, 0, 0.5)
    q2c = pair_lanes(4 * gy, 0, (0, 1, 2, 3), 2 * gy, 64, 0.125)
    own3, zsend_up, zsend_down, w2, beta2, root2 = call(
        functools.partial(down2_kernel, gx, gy),
        (b2, c2, zlo, zhi, q2b, q2c),
        [(x3, 32, LANES)] + [(x3, HZ3, LANES)] * 2 + [(x2 + 2, 80, LANES)] * 2 + [(x2, 64, LANES)],
        [(64, LANES)] * 4 + [(x3, 32, LANES)] * 2,
    )
    zlo, zhi = swap(zsend_up, zsend_down, "gz")

    q3b = pair_lanes(2 * gy, 0, (0, 1, 2, 3), gy, 0, 0.5)
    q3c = pair_lanes(2 * gy, 0, (0, 1, 2, 3), gy, 64, 0.125)
    u4 = repeat_lanes(gy, 0, 2 * gy, 0)
    u3 = repeat_lanes(2 * gy, 0, 4 * gy, 0)
    (e2,) = call(
        functools.partial(coarse_kernel, gx, gy),
        (own3, zlo, zhi, w2, beta2, root2, q3b, q3c, u4, u3),
        [(x2 + 4, 40, LANES)],
        [(x3 + 2, 80, LANES)] * 3
        + [(x3, 64, LANES)]
        + [(gx + 2, 48, LANES)] * 3
        + [(gx, 32, LANES)]
        + [(64, LANES)] * 4
        + [(gx, 32, LANES)] * 2
        + [(x2 + 2, 80, LANES)] * 2,
    )

    width = 4 * gy
    source_lane = lax.broadcasted_iota(jnp.int32, (LANES, LANES), 0)
    target_lane = lax.broadcasted_iota(jnp.int32, (LANES, LANES), 1)
    wanted_y = 4 * lax.axis_index("gy") - 2 + (target_lane % Y1) // 2
    wanted = (target_lane // Y1) * width + wanted_y
    valid = (wanted_y >= 0) & (wanted_y < width) & (target_lane < 4 * Y1)
    u2 = ((source_lane == wanted) & valid).astype(F32)
    u1 = repeat_lanes(Y1, 4, Y0, HY0)
    place = lax.axis_index("gx").astype(jnp.int32).reshape(1)
    (correction,) = call(
        up_kernel,
        (place, e2, w1, beta1, root1, w0, beta0, root0, u2, u1),
        [(4, 16, 16, LANES)],
        [(16, 96, LANES)] * 2 + [(20, 160, LANES)] * 2 + [(80, LANES), (144, LANES)],
        smem=1,
    )
    return correction


def solution(mesh):
    return jax.shard_map(
        shards,
        mesh=mesh,
        in_specs=(P(None, "gx", "gy", "gz"), P("gx", "gy", "gz"), P(), P("gx", "gy", "gz")),
        out_specs=P(None, "gx", "gy", "gz"),
        check_vma=False,
    )
```

time: 711 us -> 232 us (0.33)
  the two profiles are of different devices: /device:TPU:479 before, /device:TPU:261 now
where the time goes in v1:
time: 232 us; the launch traced here: 231 us
  Pallas kernels  99.1 us (43%)
  waiting for transfers between devices  76.9 us (33%)
  starting transfers between devices  43.9 us (19%)
  local copies, waits for them, and re-layouts  8.34 us (4%)
  other arithmetic  2.44 us (1%)
    pallas_call x8, Pallas kernels, call(): pl.pallas_call(kernel, out_shape=[jax.ShapeDtypeStruct(s, F32) for s in o...  99.1 us
    ppermute x6, waiting for transfers between devices, swap(): from_above = lax.ppermute(to_down, axis, [(i + 1, i) for i in range(n - 1)])  34 us
    all_to_all x1, waiting for transfers between devices, shards(): got = lax.all_to_all(spread, ('gx', 'gy'), 0, 0, tiled=True)  24.3 us
    ppermute x6, starting transfers between devices, swap(): from_below = lax.ppermute(to_up, axis, [(i, i + 1) for i in range(n - 1)])  22.1 us
    ppermute x6, waiting for transfers between devices, swap(): from_below = lax.ppermute(to_up, axis, [(i, i + 1) for i in range(n - 1)])  18.6 us
    ppermute x6, starting transfers between devices, swap(): from_above = lax.ppermute(to_down, axis, [(i + 1, i) for i in range(n - 1)])  11 us
    all_to_all x1, starting transfers between devices, shards(): got = lax.all_to_all(spread, ('gx', 'gy'), 0, 0, tiled=True)  10.8 us
    unnamed x28, local copies, waits for them, and re-layouts  5.36 us
  transfers between devices with their start and end apart: 13, of which 13 were waited for; matrix products, arithmetic and copies ran while one was open for 0% of the time, Pallas kernels for 0%

profile of v1, /device:TPU:261, one launch (start us, length us, event | category | flops | bytes accessed | tf_op | source)
XLA Modules:
  0.0 230.9 jit_solution(2095496452193883992)
XLA Ops:
  0.0 0.8 select_reduce_fusion
  0.8 0.1 broadcast_in_dim.12
  0.9 0.1 broadcast_in_dim.26
  1.0 0.9 mul.16.visc
  1.9 1.2 fusion.8
  3.1 3.1 %collective-permute-start = (f32[5,10,16,128]{3,2,1,0:T(8,128)S(1)}, f32[5,10,16,128]{3,2,1,0:T(8,128)S(1)}, u32[]{:S(2)}, u32[]{:S(2)}) collective-permute-start(f32[5,10,16,128]{3,2,1,0:T(8,128)S(1)} %pad_maximum_fusion), channel_id=1, source_target_pairs={{0,128},{128,256},{256,384},{384,512},{512,640},{640,768},{768,896... | collective-permute-start | bytes 1228808 | tf_op jit(solution)/shard_map/ppermute | solution.py:501
  6.3 2.2 collective-permute-start.1
  8.5 6.9 %collective-permute-done.xlo = f32[5,10,16,128]{3,2,1,0:T(8,128)S(1)} collective-permute-done((f32[5,10,16,128]{3,2,1,0:T(8,128)S(1)}, f32[5,10,16,128]{3,2,1,0:T(8,128)S(1)}, u32[]{:S(2)}, u32[]{:S(2)}) %collective-permute-start) | collective-permute-done | bytes 409632 | tf_op jit(solution)/shard_map/ppermute | solution.py:501
  15.4 4.1 %collective-permute-done.1.xhi = f32[5,10,16,128]{3,2,1,0:T(8,128)S(1)} collective-permute-done((f32[5,10,16,128]{3,2,1,0:T(8,128)S(1)}, f32[5,10,16,128]{3,2,1,0:T(8,128)S(1)}, u32[]{:S(2)}, u32[]{:S(2)}) %collective-permute-start.1) | collective-permute-done | bytes 409632 | tf_op jit(solution)/shard_map/ppermute | solution.py:502
  19.5 0.8 copy-done.5
  20.3 3.1 %shard_map.145 = (f32[36,112,128]{2,1,0:T(8,128)}, f32[36,16,128]{2,1,0:T(8,128)}, f32[36,16,128]{2,1,0:T(8,128)}) custom-call(f32[5,10,16,128]{3,2,1,0:T(8,128)} %copy-done.4, f32[4,16,16,128]{3,2,1,0:T(8,128)} %source.1, f32[16,16,128]{2,1,0:T(8,128)} %copy-done.1, f32[5,10,16,128]{3,2,1,0:T(8,128)} %copy-done.5), custom_call_target="tpu_custom_call" | custom-call | tf_op jit(solution)/shard_map/pallas_call | solution.py:489
  23.4 3.3 %collective-permute-start.2 = (f32[36,16,128]{2,1,0:T(8,128)}, f32[36,16,128]{2,1,0:T(8,128)S(1)}, u32[]{:S(2)}, u32[]{:S(2)}) collective-permute-start(f32[36,16,128]{2,1,0:T(8,128)} %get-tuple-element.32), channel_id=1, source_target_pairs={{0,16},{16,32},{32,48},{48,64},{64,80},{80,96},{96,112},{1,17},{17... | collective-permute-start | bytes 884744 | tf_op jit(solution)/shard_map/ppermute | solution.py:501
  26.7 1.3 collective-permute-start.3
  28.0 3.7 %collective-permute-done.2.ylo = f32[36,16,128]{2,1,0:T(8,128)S(1)} collective-permute-done((f32[36,16,128]{2,1,0:T(8,128)}, f32[36,16,128]{2,1,0:T(8,128)S(1)}, u32[]{:S(2)}, u32[]{:S(2)}) %collective-permute-start.2) | collective-permute-done | bytes 294944 | tf_op jit(solution)/shard_map/ppermute | solution.py:501
  31.7 3.7 %collective-permute-done.3.yhi = f32[36,16,128]{2,1,0:T(8,128)S(1)} collective-permute-done((f32[36,16,128]{2,1,0:T(8,128)}, f32[36,16,128]{2,1,0:T(8,128)S(1)}, u32[]{:S(2)}, u32[]{:S(2)}) %collective-permute-start.3) | collective-permute-done | bytes 294944 | tf_op jit(solution)/shard_map/ppermute | solution.py:502
  35.5 0.7 copy-done.9
  36.2 7.2 %shard_map.146 = (f32[36,128,128]{2,1,0:T(8,128)}, f32[36,16,128]{2,1,0:T(8,128)}, f32[36,16,128]{2,1,0:T(8,128)}) custom-call(f32[36,112,128]{2,1,0:T(8,128)} %get-tuple-element.31.rows, f32[36,16,128]{2,1,0:T(8,128)} %copy-done.8, f32[36,16,128]{2,1,0:T(8,128)} %copy-done.9), custom_call_target="tpu_custom_call" | custom-call | tf_op jit(solution)/shard_map/pallas_call | solution.py:489
  43.4 7.5 %collective-permute-start.4 = (f32[36,16,128]{2,1,0:T(8,128)}, f32[36,16,128]{2,1,0:T(8,128)S(1)}, u32[]{:S(2)}, u32[]{:S(2)}) collective-permute-start(f32[36,16,128]{2,1,0:T(8,128)} %get-tuple-element.35), channel_id=1, source_target_pairs={{0,1},{1,2},{2,3},{3,4},{4,5},{5,6},{6,7},{7,8},{8,9},{9,10},{10,1... | collective-permute-start | bytes 884744 | tf_op jit(solution)/shard_map/ppermute | solution.py:501
  50.9 1.9 collective-permute-start.5
  52.9 2.0 collective-permute-done.4.zlo
  54.9 4.3 %collective-permute-done.5.zhi = f32[36,16,128]{2,1,0:T(8,128)S(1)} collective-permute-done((f32[36,16,128]{2,1,0:T(8,128)}, f32[36,16,128]{2,1,0:T(8,128)S(1)}, u32[]{:S(2)}, u32[]{:S(2)}) %collective-permute-start.5) | collective-permute-done | bytes 294944 | tf_op jit(solution)/shard_map/ppermute | solution.py:502
  59.2 0.7 copy-done.7
  59.9 22.5 %shard_map.147 = (f32[16,48,128]{2,1,0:T(8,128)}, f32[16,24,128]{2,1,0:T(8,128)}, f32[16,24,128]{2,1,0:T(8,128)}, f32[20,144,128]{2,1,0:T(8,128)}, f32[20,144,128]{2,1,0:T(8,128)}, /*index=5*/f32[20,144,128]{2,1,0:T(8,128)}) custom-call(f32[36,128,128]{2,1,0:T(8,128)} %get-tuple-element.34.turned, f32[36,16,128]{2,1,0:T(8,128)} %copy-done.6, ...), custom_call_target="tpu_custom_call" | custom-call | tf_op jit(solution)/shard_map/pallas_call | solution.py:489
  82.4 3.3 %collective-permute-start.6 = (f32[16,24,128]{2,1,0:T(8,128)}, f32[16,24,128]{2,1,0:T(8,128)S(1)}, u32[]{:S(2)}, u32[]{:S(2)}) collective-permute-start(f32[16,24,128]{2,1,0:T(8,128)} %get-tuple-element.38), channel_id=1, source_target_pairs={{0,16},{16,32},{32,48},{48,64},{64,80},{80,96},{96,112},{1,17},{17... | collective-permute-start | bytes 589832 | tf_op jit(solution)/shard_map/ppermute | solution.py:501
  85.7 1.3 collective-permute-start.7
  87.0 1.6 collective-permute-done.6.ylo
  88.6 4.8 %collective-permute-done.7.yhi = f32[16,24,128]{2,1,0:T(8,128)S(1)} collective-permute-done((f32[16,24,128]{2,1,0:T(8,128)}, f32[16,24,128]{2,1,0:T(8,128)S(1)}, u32[]{:S(2)}, u32[]{:S(2)}) %collective-permute-start.7) | collective-permute-done | bytes 196640 | tf_op jit(solution)/shard_map/ppermute | solution.py:502
  93.5 0.7 copy-done.11
  94.1 7.3 %shard_map.148 = (f32[24,128]{1,0:T(8,128)}, f32[16,96,128]{2,1,0:T(8,128)}, f32[16,96,128]{2,1,0:T(8,128)}, f32[16,80,128]{2,1,0:T(8,128)}) custom-call(f32[16,48,128]{2,1,0:T(8,128)} %get-tuple-element.37.own, f32[16,24,128]{2,1,0:T(8,128)} %copy-done.10, f32[16,24,128]{2,1,0:T(8,128)} %copy-done.11, f32[128,128]{1,0:T(8,128)} %constant.86.clone.qb, ...), custom_call_target="tpu_custom_call" | custom-call | tf_op jit(solution)/shard_map/pallas_call | solution.py:489
  101.4 1.6 broadcast_in_dim.30
  103.1 10.8 %all-to-all-start = ((f32[64,24,128]{2,1,0:T(8,128)}), f32[64,24,128]{2,1,0:T(8,128)S(1)}, u32[]{:S(2)}, u32[]{:S(2)}) async-start(f32[64,24,128]{2,1,0:T(8,128)} %broadcast_in_dim.30), calls=%async_computation | async-start | bytes 1572864 | tf_op jit(solution)/shard_map/all_to_all | solution.py:554
  113.9 24.3 %all-to-all-done.got = f32[64,24,128]{2,1,0:T(8,128)S(1)} async-done(((f32[64,24,128]{2,1,0:T(8,128)}), f32[64,24,128]{2,1,0:T(8,128)S(1)}, u32[]{:S(2)}, u32[]{:S(2)}) %all-to-all-start) | async-done | bytes 786464 | tf_op jit(solution)/shard_map/all_to_all | solution.py:554
  138.2 0.9 copy-done
  139.1 3.9 %shard_map.149 = (f32[32,32,128]{2,1,0:T(8,128)}, f32[32,32,128]{2,1,0:T(8,128)}, f32[2,32,10,128]{3,2,1,0:T(8,128)}, f32[2,32,10,128]{3,2,1,0:T(8,128)}) custom-call(f32[64,24,128]{2,1,0:T(8,128)} %copy-done), custom_call_target="tpu_custom_call" | custom-call | tf_op jit(solution)/shard_map/pallas_call | solution.py:489
  143.0 1.9 collective-permute-start.8
  144.9 2.4 %collective-permute-start.9 = (f32[2,32,10,128]{3,2,1,0:T(8,128)}, f32[2,32,10,128]{3,2,1,0:T(8,128)S(1)}, u32[]{:S(2)}, u32[]{:S(2)}) collective-permute-start(f32[2,32,10,128]{3,2,1,0:T(8,128)} %get-tuple-element.44), channel_id=1, source_target_pairs={{1,0},{2,1},{3,2},{4,3},{5,4},{6,5},{7,6},{8,7},{9,8},{10,9},{11,1... | collective-permute-start | bytes 983048 | tf_op jit(solution)/shard_map/ppermute | solution.py:502
  147.4 4.0 %collective-permute-done.8.zlo = f32[2,32,10,128]{3,2,1,0:T(8,128)S(1)} collective-permute-done((f32[2,32,10,128]{3,2,1,0:T(8,128)}, f32[2,32,10,128]{3,2,1,0:T(8,128)S(1)}, u32[]{:S(2)}, u32[]{:S(2)}) %collective-permute-start.8) | collective-permute-done | bytes 327712 | tf_op jit(solution)/shard_map/ppermute | solution.py:501
  151.4 6.1 %collective-permute-done.9.zhi = f32[2,32,10,128]{3,2,1,0:T(8,128)S(1)} collective-permute-done((f32[2,32,10,128]{3,2,1,0:T(8,128)}, f32[2,32,10,128]{3,2,1,0:T(8,128)S(1)}, u32[]{:S(2)}, u32[]{:S(2)}) %collective-permute-start.9) | collective-permute-done | bytes 327712 | tf_op jit(solution)/shard_map/ppermute | solution.py:502
  157.4 0.8 copy-done.3
  158.2 12.6 %shard_map.150 = (f32[16,32,128]{2,1,0:T(8,128)}, f32[16,20,128]{2,1,0:T(8,128)}, f32[16,20,128]{2,1,0:T(8,128)}, f32[34,80,128]{2,1,0:T(8,128)}, f32[34,80,128]{2,1,0:T(8,128)}, /*index=5*/f32[32,64,128]{2,1,0:T(8,128)}) custom-call(f32[32,32,128]{2,1,0:T(8,128)} %get-tuple-element.41.b, f32[32,32,128]{2,1,0:T(8,128)} %get-tuple-element.42.c, ...), custom_call_target="tpu_custom_call" | custom-call | tf_op jit(solution)/shard_map/pallas_call | solution.py:489
  170.9 3.0 %collective-permute-start.10 = (f32[16,20,128]{2,1,0:T(8,128)}, f32[16,20,128]{2,1,0:T(8,128)S(1)}, u32[]{:S(2)}, u32[]{:S(2)}) collective-permute-start(f32[16,20,128]{2,1,0:T(8,128)} %get-tuple-element.46), channel_id=1, source_target_pairs={{0,1},{1,2},{2,3},{3,4},{4,5},{5,6},{6,7},{7,8},{8,9},{9,10},{10,1... | collective-permute-start | bytes 491528 | tf_op jit(solution)/shard_map/ppermute | solution.py:501
  173.8 1.9 collective-permute-start.11
  175.8 0.6 fusion.7.u2
  176.4 0.3 collective-permute-done.10.zlo
  176.7 11.0 %collective-permute-done.11.zhi = f32[16,20,128]{2,1,0:T(8,128)S(1)} collective-permute-done((f32[16,20,128]{2,1,0:T(8,128)}, f32[16,20,128]{2,1,0:T(8,128)S(1)}, u32[]{:S(2)}, u32[]{:S(2)}) %collective-permute-start.11) | collective-permute-done | bytes 163872 | tf_op jit(solution)/shard_map/ppermute | solution.py:502
  187.7 0.7 copy-done.13
  188.4 27.6 %shard_map.151.e2 = f32[36,40,128]{2,1,0:T(8,128)} custom-call(f32[16,32,128]{2,1,0:T(8,128)} %get-tuple-element.45.own, f32[16,20,128]{2,1,0:T(8,128)} %copy-done.12, f32[16,20,128]{2,1,0:T(8,128)} %copy-done.13, f32[34,80,128]{2,1,0:T(8,128)} %get-tuple-element.48.w2, f32[34,80,128]{2,1,0:T(8,128)} %get-tuple-element.49.beta2, ...), custom_call_target="tpu_custom_call" | custom-call | tf_op jit(solution)/shard_map/pallas_call | solution.py:489
  216.0 14.9 %shard_map.152 = f32[4,16,16,128]{3,2,1,0:T(8,128)} custom-call(s32[1]{0:T(128)} %bitcast.place, f32[36,40,128]{2,1,0:T(8,128)} %shard_map.151.e2, f32[16,96,128]{2,1,0:T(8,128)} %get-tuple-element.51.w1, f32[16,96,128]{2,1,0:T(8,128)} %get-tuple-element.52.beta1, f32[16,80,128]{2,1,0:T(8,128)} %get-tuple-element.53.root1, ...), custom_call_target="tpu_custom_call" | custom-call | tf_op jit(solution)/shard_map/pallas_call | solution.py:489
  (29 shorter events, 0.1 us)
Async XLA Ops:
  1.9 4.4 %copy-start.1 = (f32[16,16,128]{2,1,0:T(8,128)}, f32[16,16,128]{2,1,0:T(8,128)S(1)}, u32[]{:S(2)}) copy-start(f32[16,16,128]{2,1,0:T(8,128)S(1)} %mul.16.visc) | copy-start | bytes 393220
  3.1 12.2 %collective-permute-start = (f32[5,10,16,128]{3,2,1,0:T(8,128)S(1)}, f32[5,10,16,128]{3,2,1,0:T(8,128)S(1)}, u32[]{:S(2)}, u32[]{:S(2)}) collective-permute-start(f32[5,10,16,128]{3,2,1,0:T(8,128)S(1)} %pad_maximum_fusion), channel_id=1, source_target_pairs={{0,128},{128,256},{256,384},{384,512},{512,640},{640,768},{768,896... | collective-permute-start | bytes 1228808 | tf_op jit(solution)/shard_map/ppermute | solution.py:501
  6.3 13.2 %collective-permute-start.1 = (f32[5,10,16,128]{3,2,1,0:T(8,128)S(1)}, f32[5,10,16,128]{3,2,1,0:T(8,128)S(1)}, u32[]{:S(2)}, u32[]{:S(2)}) collective-permute-start(f32[5,10,16,128]{3,2,1,0:T(8,128)S(1)} %pad_maximum_fusion.1), channel_id=1, source_target_pairs={{128,0},{256,128},{384,256},{512,384},{640,512},{768,640},{896,768... | collective-permute-start | bytes 1228808 | tf_op jit(solution)/shard_map/ppermute | solution.py:502
  15.4 4.1 %copy-start.4 = (f32[5,10,16,128]{3,2,1,0:T(8,128)}, f32[5,10,16,128]{3,2,1,0:T(8,128)S(1)}, u32[]{:S(2)}) copy-start(f32[5,10,16,128]{3,2,1,0:T(8,128)S(1)} %collective-permute-done.xlo) | copy-start | bytes 1228804
  19.5 0.8 copy-start.5
  23.4 8.4 %collective-permute-start.2 = (f32[36,16,128]{2,1,0:T(8,128)}, f32[36,16,128]{2,1,0:T(8,128)S(1)}, u32[]{:S(2)}, u32[]{:S(2)}) collective-permute-start(f32[36,16,128]{2,1,0:T(8,128)} %get-tuple-element.32), channel_id=1, source_target_pairs={{0,16},{16,32},{32,48},{48,64},{64,80},{80,96},{96,112},{1,17},{17... | collective-permute-start | bytes 884744 | tf_op jit(solution)/shard_map/ppermute | solution.py:501
  26.7 8.8 %collective-permute-start.3 = (f32[36,16,128]{2,1,0:T(8,128)}, f32[36,16,128]{2,1,0:T(8,128)S(1)}, u32[]{:S(2)}, u32[]{:S(2)}) collective-permute-start(f32[36,16,128]{2,1,0:T(8,128)} %get-tuple-element.33), channel_id=1, source_target_pairs={{16,0},{32,16},{48,32},{64,48},{80,64},{96,80},{112,96},{17,1},{33... | collective-permute-start | bytes 884744 | tf_op jit(solution)/shard_map/ppermute | solution.py:502
  31.7 3.7 %copy-start.8 = (f32[36,16,128]{2,1,0:T(8,128)}, f32[36,16,128]{2,1,0:T(8,128)S(1)}, u32[]{:S(2)}) copy-start(f32[36,16,128]{2,1,0:T(8,128)S(1)} %collective-permute-done.2.ylo) | copy-start | bytes 884740
  35.5 0.7 copy-start.9
  43.4 11.5 %collective-permute-start.4 = (f32[36,16,128]{2,1,0:T(8,128)}, f32[36,16,128]{2,1,0:T(8,128)S(1)}, u32[]{:S(2)}, u32[]{:S(2)}) collective-permute-start(f32[36,16,128]{2,1,0:T(8,128)} %get-tuple-element.35), channel_id=1, source_target_pairs={{0,1},{1,2},{2,3},{3,4},{4,5},{5,6},{6,7},{7,8},{8,9},{9,10},{10,1... | collective-permute-start | bytes 884744 | tf_op jit(solution)/shard_map/ppermute | solution.py:501
  50.9 8.3 %collective-permute-start.5 = (f32[36,16,128]{2,1,0:T(8,128)}, f32[36,16,128]{2,1,0:T(8,128)S(1)}, u32[]{:S(2)}, u32[]{:S(2)}) collective-permute-start(f32[36,16,128]{2,1,0:T(8,128)} %get-tuple-element.36), channel_id=1, source_target_pairs={{1,0},{2,1},{3,2},{4,3},{5,4},{6,5},{7,6},{8,7},{9,8},{10,9},{11,1... | collective-permute-start | bytes 884744 | tf_op jit(solution)/shard_map/ppermute | solution.py:502
  54.9 4.3 %copy-start.6 = (f32[36,16,128]{2,1,0:T(8,128)}, f32[36,16,128]{2,1,0:T(8,128)S(1)}, u32[]{:S(2)}) copy-start(f32[36,16,128]{2,1,0:T(8,128)S(1)} %collective-permute-done.4.zlo) | copy-start | bytes 884740
  59.2 0.7 copy-start.7
  82.4 6.2 %collective-permute-start.6 = (f32[16,24,128]{2,1,0:T(8,128)}, f32[16,24,128]{2,1,0:T(8,128)S(1)}, u32[]{:S(2)}, u32[]{:S(2)}) collective-permute-start(f32[16,24,128]{2,1,0:T(8,128)} %get-tuple-element.38), channel_id=1, source_target_pairs={{0,16},{16,32},{32,48},{48,64},{64,80},{80,96},{96,112},{1,17},{17... | collective-permute-start | bytes 589832 | tf_op jit(solution)/shard_map/ppermute | solution.py:501
  85.7 7.7 %collective-permute-start.7 = (f32[16,24,128]{2,1,0:T(8,128)}, f32[16,24,128]{2,1,0:T(8,128)S(1)}, u32[]{:S(2)}, u32[]{:S(2)}) collective-permute-start(f32[16,24,128]{2,1,0:T(8,128)} %get-tuple-element.39), channel_id=1, source_target_pairs={{16,0},{32,16},{48,32},{64,48},{80,64},{96,80},{112,96},{17,1},{33... | collective-permute-start | bytes 589832 | tf_op jit(solution)/shard_map/ppermute | solution.py:502
  88.6 4.8 %copy-start.10 = (f32[16,24,128]{2,1,0:T(8,128)}, f32[16,24,128]{2,1,0:T(8,128)S(1)}, u32[]{:S(2)}) copy-start(f32[16,24,128]{2,1,0:T(8,128)S(1)} %collective-permute-done.6.ylo) | copy-start | bytes 589828
  93.5 0.7 copy-start.11
  103.1 35.1 %all-to-all-start = ((f32[64,24,128]{2,1,0:T(8,128)}), f32[64,24,128]{2,1,0:T(8,128)S(1)}, u32[]{:S(2)}, u32[]{:S(2)}) async-start(f32[64,24,128]{2,1,0:T(8,128)} %broadcast_in_dim.30), calls=%async_computation | async-start | bytes 1572864 | tf_op jit(solution)/shard_map/all_to_all | solution.py:554
  138.2 0.9 copy-start
  143.0 8.3 %collective-permute-start.8 = (f32[2,32,10,128]{3,2,1,0:T(8,128)}, f32[2,32,10,128]{3,2,1,0:T(8,128)S(1)}, u32[]{:S(2)}, u32[]{:S(2)}) collective-permute-start(f32[2,32,10,128]{3,2,1,0:T(8,128)} %get-tuple-element.43), channel_id=1, source_target_pairs={{0,1},{1,2},{2,3},{3,4},{4,5},{5,6},{6,7},{7,8},{8,9},{9,10},{10,1... | collective-permute-start | bytes 983048 | tf_op jit(solution)/shard_map/ppermute | solution.py:501
  144.9 12.5 %collective-permute-start.9 = (f32[2,32,10,128]{3,2,1,0:T(8,128)}, f32[2,32,10,128]{3,2,1,0:T(8,128)S(1)}, u32[]{:S(2)}, u32[]{:S(2)}) collective-permute-start(f32[2,32,10,128]{3,2,1,0:T(8,128)} %get-tuple-element.44), channel_id=1, source_target_pairs={{1,0},{2,1},{3,2},{4,3},{5,4},{6,5},{7,6},{8,7},{9,8},{10,9},{11,1... | collective-permute-start | bytes 983048 | tf_op jit(solution)/shard_map/ppermute | solution.py:502
  151.4 6.1 %copy-start.2 = (f32[2,32,10,128]{3,2,1,0:T(8,128)}, f32[2,32,10,128]{3,2,1,0:T(8,128)S(1)}, u32[]{:S(2)}) copy-start(f32[2,32,10,128]{3,2,1,0:T(8,128)S(1)} %collective-permute-done.8.zlo) | copy-start | bytes 983044
  157.4 0.8 copy-start.3
  170.9 5.9 %collective-permute-start.10 = (f32[16,20,128]{2,1,0:T(8,128)}, f32[16,20,128]{2,1,0:T(8,128)S(1)}, u32[]{:S(2)}, u32[]{:S(2)}) collective-permute-start(f32[16,20,128]{2,1,0:T(8,128)} %get-tuple-element.46), channel_id=1, source_target_pairs={{0,1},{1,2},{2,3},{3,4},{4,5},{5,6},{6,7},{7,8},{8,9},{9,10},{10,1... | collective-permute-start | bytes 491528 | tf_op jit(solution)/shard_map/ppermute | solution.py:501
  173.8 13.9 %collective-permute-start.11 = (f32[16,20,128]{2,1,0:T(8,128)}, f32[16,20,128]{2,1,0:T(8,128)S(1)}, u32[]{:S(2)}, u32[]{:S(2)}) collective-permute-start(f32[16,20,128]{2,1,0:T(8,128)} %get-tuple-element.47), channel_id=1, source_target_pairs={{1,0},{2,1},{3,2},{4,3},{5,4},{6,5},{7,6},{8,7},{9,8},{10,9},{11,1... | collective-permute-start | bytes 491528 | tf_op jit(solution)/shard_map/ppermute | solution.py:502
  176.7 11.0 %copy-start.12 = (f32[16,20,128]{2,1,0:T(8,128)}, f32[16,20,128]{2,1,0:T(8,128)S(1)}, u32[]{:S(2)}) copy-start(f32[16,20,128]{2,1,0:T(8,128)S(1)} %collective-permute-done.10.zlo) | copy-start | bytes 491524
  187.7 0.7 copy-start.13

commit v2 on v0

v2 whole, which is shorter than its diff:
```python
import functools

import jax
import jax.numpy as jnp
import numpy as np
from jax import lax
from jax.experimental import pallas as pl
from jax.experimental.pallas import tpu as pltpu
from jax.sharding import PartitionSpec as P

F32 = jnp.float32
COARSE_ITERS = 8
TAU = 0.8 / 6.0
LANES = 128
HX0, HY0, HZ0 = 3, 3, 16
Y0 = 16 + 2 * HY0
Y1 = 16
HZ2 = 10
HZ3 = 20
OFF2, OFF3 = 4, 2


def halves(a):
    high = a.astype(jnp.bfloat16)
    return [high, (a - high.astype(F32)).astype(jnp.bfloat16)]


def mm(pairs):
    left, right = [], []
    for a, m in pairs:
        left += halves(a)
        right += [m, m]
    return jnp.dot(jnp.concatenate(left, axis=1), jnp.concatenate(right, axis=0), preferred_element_type=F32)


def lane_of(n):
    return lax.broadcasted_iota(jnp.int32, (n, LANES), 1)


def lane_roll(x, shift):
    return pltpu.roll(x, shift % LANES, 1) if shift % LANES else x


def around(ref, x, row, n):
    mid = ref[x, pl.ds(row, n), :]
    total = ref[x - 1, pl.ds(row, n), :] + ref[x + 1, pl.ds(row, n), :]
    total = total + (ref[x, pl.ds(row - 1, n), :] + ref[x, pl.ds(row + 1, n), :])
    return mid, total + (lane_roll(mid, 1) + lane_roll(mid, -1))


def around_whole(ref, x, row, n, width):
    mid = ref[x, pl.ds(row, n), :]
    total = ref[x - 1, pl.ds(row, n), :] + ref[x + 1, pl.ds(row, n), :]
    total = total + (ref[x, pl.ds(row - 1, n), :] + ref[x, pl.ds(row + 1, n), :])
    place = lane_of(n) & (width - 1)
    total = total + jnp.where(place == 0, 0.0, lane_roll(mid, 1))
    return mid, total + jnp.where(place == width - 1, 0.0, lane_roll(mid, -1))


def chunks(n, size):
    return [(r, min(size, n - r)) for r in range(0, n, size)]


def roots_of(c):
    live = c > 0.0
    inv = lax.rsqrt(jnp.where(live, c, 1.0))
    return jnp.where(live, c * inv, 0.0), jnp.where(live, inv, 0.0)


def inverse(root):
    live = root > 0.0
    return jnp.where(live, 1.0 / jnp.where(live, root, 1.0), 0.0)


def jacobi(live, mid, beta, total):
    return jnp.where(live, 0.2 * mid + beta + TAU * total, 0.0)


def pair_lanes(width, start, fields, out_width, out_start, scale):
    m = np.zeros((LANES, LANES), jnp.bfloat16)
    for k, f in enumerate(fields):
        for j in range(out_width):
            for i in range(2):
                m[f * width + start + 2 * j + i, out_start + k * out_width + j] = scale
    return m


def repeat_lanes(width, shift, out_width, out_shift):
    m = np.zeros((LANES, LANES), jnp.bfloat16)
    for f in range(4):
        for j in range(out_width):
            i = shift + (j - out_shift) // 2
            if 0 <= i < width:
                m[f * width + i, f * out_width + j] = 1.0
    return m


def residual(w, beta, root, x, row, n, mid_total):
    mid, total = mid_total
    root_x = root[x, pl.ds(row - 8, n), :]
    return root_x * ((1.0 / TAU) * beta[x, pl.ds(row, n), :] - 6.0 * mid + total), root_x * root_x


def loop(begin, end, body, unroll=1):
    def step(i, carry):
        body(i)
        return carry

    lax.fori_loop(begin, end, step, 0, unroll=unroll)


def fold_rows(ref, k, n):
    return ref[k, pl.ds(0, n, stride=2), :] + ref[k, pl.ds(1, n, stride=2), :]


def unfold_rows(ref, k, n, value):
    ref[k, pl.ds(0, n, stride=2), :] = value
    ref[k, pl.ds(1, n, stride=2), :] = value


def prepare_kernel(table, ids, spread, source, roughness, visc, low, high):
    blocks = jnp.concatenate([ids[0], ids[1]], axis=0)
    found = jnp.zeros(blocks.shape, F32)
    for k in range(table.shape[0]):
        found = found + jnp.where(blocks == k, table[k], 0.0)
    along_z = jnp.dot(found, spread[...], precision=lax.Precision.HIGHEST, preferred_element_type=F32)
    for x in range(16):
        for j in range(2):
            row = 2 * (x // 8) + j
            visc[x, pl.ds(8 * j, 8), :] = roughness[x, pl.ds(8 * j, 8), :] * along_z[row : row + 1]
    for x in range(HX0):
        for f in range(4):
            low[f, x] = source[f, x]
            high[f, x] = source[f, 16 - HX0 + x]
        low[4, x] = visc[x]
        high[4, x] = visc[16 - HX0 + x]


def edge_kernel(xlo, source, visc, xhi, ylo, yhi):
    def put(x, f, plane):
        ylo[x, pl.ds(f * HY0, HY0), :] = plane[0:HY0]
        yhi[x, pl.ds(f * HY0, HY0), :] = plane[16 - HY0 : 16]

    for x in range(HX0):
        for f in range(5):
            put(x, f, xlo[f, x])
            put(x + HX0 + 16, f, xhi[f, x])

    def own(x):
        for f in range(4):
            put(x + HX0, f, source[f, x])
        put(x + HX0, 4, visc[x])

    loop(0, 16, own, 16)


def turn_kernel(xlo, source, visc, xhi, ylo, yhi, turned, zlo, zhi, stage):
    stage[...] = jnp.zeros_like(stage)

    def turn(x, slot, planes):
        for f in range(5):
            stage[slot, pl.ds(f * Y0 + HY0, 16), :] = planes[f]
            stage[slot, pl.ds(f * Y0, HY0), :] = ylo[x, pl.ds(f * HY0, HY0), :]
            stage[slot, pl.ds(f * Y0 + HY0 + 16, HY0), :] = yhi[x, pl.ds(f * HY0, HY0), :]
        t = stage[slot].T
        turned[x] = t
        zlo[x] = t[0:HZ0]
        zhi[x] = t[128 - HZ0 : 128]

    for x in range(HX0):
        turn(x, 0, [xlo[f, x] for f in range(5)])
        turn(x + HX0 + 16, 1, [xhi[f, x] for f in range(5)])

    def own(k):
        for slot in range(4):
            x = 4 * k + slot
            turn(x + HX0, slot, [source[f, x] for f in range(4)] + [visc[x]])

    loop(0, 4, own, 2)


def down0_kernel(turned, zlo, zhi, qb, qc, out, ylo, yhi, w, beta, root, rsum, csum, rz, cz, stage):
    planes = 16 + 2 * HX0
    depth = 128 + 2 * HZ0
    half = depth // 2

    def prepare(x, t, row, n):
        lane = lane_of(n)
        v = lane_roll(jnp.where(lane < 4 * Y0, 0.0, t), -4 * Y0)
        v = v + lane_roll(v, Y0)
        v = v + lane_roll(v, 2 * Y0)
        root_v, inv_v = roots_of(v)
        pressure = lane >= 3 * Y0
        root[x, pl.ds(row, n), :] = jnp.where(pressure, inv_v, root_v)
        beta[x, pl.ds(8 + row, n), :] = TAU * t * jnp.where(pressure, root_v, inv_v)

    def setup(x):
        for ref in (beta, w):
            ref[x, pl.ds(0, 8), :] = jnp.zeros((8, LANES), F32)
            ref[x, pl.ds(8 + depth, 8), :] = jnp.zeros((8, LANES), F32)
        prepare(x, zlo[x], 0, HZ0)
        for r, n in chunks(128, 32):
            prepare(x, turned[x, pl.ds(r, n), :], HZ0 + r, n)
        prepare(x, zhi[x], HZ0 + 128, HZ0)

    loop(0, planes, setup, 2)

    def smooth(x):
        for r, n in chunks(depth, 32):
            mid, total = around(beta, x, 8 + r, n)
            w[x, pl.ds(8 + r, n), :] = jnp.where(root[x, pl.ds(r, n), :] > 0.0, 1.2 * mid + TAU * total, 0.0)

    loop(1, planes - 1, smooth, 10)

    def restrict(k):
        for r, n in chunks(depth, 32):
            x = HX0 + 2 * k
            res_a, coef_a = residual(w, beta, root, x, 8 + r, n, around(w, x, 8 + r, n))
            res_b, coef_b = residual(w, beta, root, x + 1, 8 + r, n, around(w, x + 1, 8 + r, n))
            rsum[k, pl.ds(r, n), :] = res_a + res_b
            csum[k, pl.ds(r, n), :] = coef_a + coef_b

    loop(0, 8, restrict, 4)

    def fold(k):
        rz[pl.ds(k * half, half), :] = fold_rows(rsum, k, half)
        cz[pl.ds(k * half, half), :] = fold_rows(csum, k, half)

    for k in range(8):
        fold(k)
    stage[...] = jnp.zeros_like(stage)
    for k in range(0, 8, 2):
        both = mm(((rz[pl.ds(k * half, 2 * half), :], qb[...]), (cz[pl.ds(k * half, 2 * half), :], qc[...])))
        for i in range(2):
            stage[k + i, pl.ds(0, half), :] = both[i * half : (i + 1) * half]
    for k in range(8):
        t = stage[k].T
        out[k] = t[0:48]
        for a in range(6):
            ylo[k, pl.ds(a * 4, 4), :] = t[a * 8 : a * 8 + 4]
            yhi[k, pl.ds(a * 4, 4), :] = t[a * 8 + 4 : a * 8 + 8]


def join_kernel(own, ylo, yhi, low, high):
    for ref, first in ((low, 0), (high, 4)):
        for x in range(4):
            ref[x, pl.ds(0, 48), :] = own[first + x]
            ref[x, pl.ds(48, 24), :] = ylo[first + x]
            ref[x, pl.ds(72, 24), :] = yhi[first + x]


def down1_kernel(own, ylo, yhi, xlo, xhi, qb, qc, block, w, beta, root, stage, rsum, csum, rz, cz):
    stage[...] = jnp.zeros_like(stage)

    def prepare(x, slot, mine, lo, hi):
        for a in range(6):
            stage[slot, pl.ds(a * Y1 + 4, 8), :] = mine(a * 8, 8)
            stage[slot, pl.ds(a * Y1, 4), :] = lo(a * 4, 4)
            stage[slot, pl.ds(a * Y1 + 12, 4), :] = hi(a * 4, 4)
        t = stage[slot].T[0:80]
        lane = lane_of(80)
        c = jnp.where(lane < Y1, lane_roll(t, 64), jnp.where(lane < 2 * Y1, lane_roll(t, 80), lane_roll(t, 96)))
        root_x, inv_x = roots_of(jnp.where(lane < 4 * Y1, c, 0.0))
        root[x] = root_x
        beta[x, pl.ds(8, 80), :] = TAU * t * inv_x
        for ref in (beta, w):
            ref[x, pl.ds(0, 8), :] = jnp.zeros((8, LANES), F32)
            ref[x, pl.ds(88, 8), :] = jnp.zeros((8, LANES), F32)

    for x in range(4):
        for slot, side in ((0, xlo), (1, xhi)):
            prepare(
                x + 12 * slot,
                2 * (x % 2) + slot,
                lambda r, n: side[x, pl.ds(r, n), :],
                lambda r, n: side[x, pl.ds(48 + r, n), :],
                lambda r, n: side[x, pl.ds(72 + r, n), :],
            )
    for x in range(8):
        prepare(
            x + 4,
            x % 4,
            lambda r, n: own[x, pl.ds(r, n), :],
            lambda r, n: ylo[x, pl.ds(r, n), :],
            lambda r, n: yhi[x, pl.ds(r, n), :],
        )

    def smooth(x):
        for r, n in chunks(80, 40):
            mid, total = around(beta, x, 8 + r, n)
            w[x, pl.ds(8 + r, n), :] = jnp.where(root[x, pl.ds(r, n), :] > 0.0, 1.2 * mid + TAU * total, 0.0)

    loop(1, 15, smooth, 14)
    for k in range(4):
        for r, n in chunks(64, 32):
            x = 4 + 2 * k
            res_a, coef_a = residual(w, beta, root, x, 16 + r, n, around(w, x, 16 + r, n))
            res_b, coef_b = residual(w, beta, root, x + 1, 16 + r, n, around(w, x + 1, 16 + r, n))
            rsum[k, pl.ds(r, n), :] = res_a + res_b
            csum[k, pl.ds(r, n), :] = coef_a + coef_b
    for k in range(4):
        rz[pl.ds(k * 32, 32), :] = fold_rows(rsum, k, 32)
        cz[pl.ds(k * 32, 32), :] = fold_rows(csum, k, 32)
    t = mm(((rz[...], qb[...]), (cz[...], qc[...]))).T[0:24]

    def copy(i):
        block[i] = t

    loop(0, block.shape[0], copy, 8 if block.shape[0] % 8 == 0 else 1)


def plane_kernel(gx, gy, got, b, c, zlo, zhi, stage_b, stage_c):
    width = 4 * gy
    stage_b[...] = jnp.zeros_like(stage_b)
    stage_c[...] = jnp.zeros_like(stage_c)

    def one(i, slot):
        for j in range(gy):
            for a in range(4):
                stage_b[slot, pl.ds(a * width + 4 * j, 4), :] = got[i * gy + j, pl.ds(4 * a, 4), :]
            for a in range(2):
                stage_c[slot, pl.ds(a * width + 4 * j, 4), :] = got[i * gy + j, pl.ds(16 + 4 * a, 4), :]
        tb = stage_b[slot].T
        tc = stage_c[slot].T
        for x in range(4):
            at = 4 * i + x
            b[at] = tb[x * 32 : (x + 1) * 32]
            c[at] = tc[x * 32 : (x + 1) * 32]
            for ref, first in ((zlo, x * 32), (zhi, (x + 1) * 32 - HZ2)):
                ref[at, pl.ds(0, HZ2), :] = tb[first : first + HZ2]
                ref[at, pl.ds(HZ2, 5), :] = jnp.where(
                    lane_of(5) < 64, tc[first : first + 5], lane_roll(tc[first + 5 : first + 10], 64)
                )
                ref[at, pl.ds(HZ2 + 5, 1), :] = jnp.zeros((1, LANES), F32)

    def body(k):
        one(2 * k, 0)
        one(2 * k + 1, 1)

    loop(0, gx // 2, body)


def down2_kernel(gx, gy, b, c, zlo, zhi, qb, qc, out, zup, zdown, w, beta, root, rsum, csum, rz, cz):
    size_x, width = 4 * gx, 4 * gy

    def prepare(x, row, t, tc):
        n = t.shape[0]
        lane = lane_of(n)
        c_all = jnp.where(lane < width, tc, jnp.where(lane < 2 * width, lane_roll(tc, width), lane_roll(tc, 2 * width)))
        root_x, inv_x = roots_of(jnp.where(lane < 4 * width, c_all, 0.0))
        root[x + OFF2, pl.ds(row, n), :] = root_x
        beta[x + OFF2, pl.ds(8 + row, n), :] = TAU * t * inv_x

    for x in list(range(OFF2)) + list(range(OFF2 + size_x, 2 * OFF2 + size_x)):
        for ref in (beta, w, root):
            ref[x] = jnp.zeros(ref.shape[1:], F32)

    def setup(x):
        for ref in (beta, w):
            ref[x + OFF2, pl.ds(0, 16), :] = jnp.zeros((16, LANES), F32)
            ref[x + OFF2, pl.ds(64, 16), :] = jnp.zeros((16, LANES), F32)
        root[x + OFF2, pl.ds(0, 8), :] = jnp.zeros((8, LANES), F32)
        root[x + OFF2, pl.ds(56, 8), :] = jnp.zeros((8, LANES), F32)
        prepare(x, 16, b[x], c[x])
        for ref, row in ((zlo, 16 - HZ2), (zhi, 48)):
            packed = ref[x, pl.ds(HZ2, 5), :]
            prepare(x, row, ref[x, pl.ds(0, 5), :], jnp.where(lane_of(5) < 64, packed, 0.0))
            prepare(x, row + 5, ref[x, pl.ds(5, 5), :], jnp.where(lane_of(5) < 64, lane_roll(packed, 64), 0.0))

    loop(0, size_x, setup, 8)

    def smooth(x):
        for r, n in chunks(64, 32):
            mid, total = around_whole(beta, x, 8 + r, n, width)
            w[x, pl.ds(8 + r, n), :] = jnp.where(root[x, pl.ds(r, n), :] > 0.0, 1.2 * mid + TAU * total, 0.0)

    loop(OFF2, size_x + OFF2, smooth, 8)
    restrict_whole(size_x, OFF2, width, w, beta, root, rsum, csum, rz, cz)
    for k in range(0, size_x // 2, 4):
        rows = pl.ds(k * 32, 128)
        t = mm(((rz[rows, :], qb[...]), (cz[rows, :], qc[...])))
        for i in range(4):
            out[k + i] = t[i * 32 : (i + 1) * 32]
            zup[k + i] = t[i * 32 + 24 - HZ3 : i * 32 + 24]
            zdown[k + i] = t[i * 32 + 8 : i * 32 + 8 + HZ3]


def restrict_whole(size_x, off, width, w, beta, root, rsum, csum, rz, cz):
    def body(k):
        for r, n in chunks(64, 32):
            x = 2 * k + off
            res_a, coef_a = residual(w, beta, root, x, 8 + r, n, around_whole(w, x, 8 + r, n, width))
            res_b, coef_b = residual(w, beta, root, x + 1, 8 + r, n, around_whole(w, x + 1, 8 + r, n, width))
            rsum[k, pl.ds(r, n), :] = res_a + res_b
            csum[k, pl.ds(r, n), :] = coef_a + coef_b

    loop(0, size_x // 2, body, 4 if size_x % 8 == 0 else 2)
    for k in range(size_x // 2):
        rz[pl.ds(k * 32, 32), :] = fold_rows(rsum, k, 32)
        cz[pl.ds(k * 32, 32), :] = fold_rows(csum, k, 32)


def relax_whole(first, planes, begin, depth, width, src, dst, beta, root, unroll, shift=0):
    def body(x):
        for r, n in chunks(depth, 32):
            r = r + begin
            mid, total = around_whole(src, x, 8 + r, n, width)
            live = root[x + shift, pl.ds(r, n), :] > 0.0
            dst[x, pl.ds(8 + r, n), :] = jacobi(live, mid, beta[x + shift, pl.ds(8 + r, n), :], total)

    loop(first, first + planes, body, unroll)


def coarse_kernel(gx, gy, place, own, zlo, zhi, w2, beta2, root2, q3b, q3c, u4, u3, e2, beta3, w3, v3, root3, beta4, w4, v4, root4, rsum, csum, rz, cz, v2, w2b, fine3, fine2):
    size_x, width = 2 * gx, 2 * gy
    for ref in (beta3, w3, v3, root3, beta4, w4, v4):
        ref[...] = jnp.zeros_like(ref)

    def prepare(x, row, t):
        n = t.shape[0]
        root_x, inv_x = roots_of(jnp.where(lane_of(n) < 4 * width, lane_roll(t, 64), 0.0))
        root3[x + OFF3, pl.ds(row, n), :] = root_x
        beta3[x + OFF3, pl.ds(8 + row, n), :] = TAU * t * inv_x

    def setup(x):
        prepare(x, 24 - HZ3, zlo[x])
        prepare(x, 24, own[x, pl.ds(8, 16), :])
        prepare(x, 40, zhi[x])

    loop(0, size_x, setup, 4)

    def smooth(x):
        for r, n in chunks(64, 32):
            mid, total = around_whole(beta3, x, 8 + r, n, width)
            w3[x, pl.ds(8 + r, n), :] = jnp.where(root3[x, pl.ds(r, n), :] > 0.0, 1.2 * mid + TAU * total, 0.0)

    loop(OFF3, size_x + OFF3, smooth, 4)
    restrict_whole(size_x, OFF3, width, w3, beta3, root3, rsum, csum, rz, cz)
    t = mm(((rz[...], q3b[...]), (cz[...], q3c[...])))
    for x in range(gx):
        t_x = t[x * 32 : (x + 1) * 32]
        root_x, inv_x = roots_of(jnp.where(lane_of(32) < 4 * gy, lane_roll(t_x, 64), 0.0))
        root4[x + 1] = root_x
        beta4[x + 1, pl.ds(8, 32), :] = TAU * t_x * inv_x
        w4[x + 1, pl.ds(8, 32), :] = TAU * t_x * inv_x
    here, there = w4, v4
    for step in range(COARSE_ITERS - 1):
        relax_whole(1, gx, 0, 32, gy, here, there, beta4, root4, gx)
        here, there = there, here

    e4 = [here[x + 1, pl.ds(16, 16), :] * inverse(root4[x + 1, pl.ds(8, 16), :]) for x in range(gx)]
    e4 = mm(((jnp.concatenate(e4, axis=0), u4[...]),))
    for x in range(gx):
        unfold_rows(fine3, x, 16, e4[x * 16 : (x + 1) * 16])
        for i in range(2):
            at = 2 * x + i + OFF3
            w3[at, pl.ds(24, 32), :] = w3[at, pl.ds(24, 32), :] + root3[at, pl.ds(16, 32), :] * fine3[x]
    relax_whole(OFF3, size_x, 16, 32, width, w3, v3, beta3, root3, 4)
    relax_whole(OFF3, size_x, 16, 32, width, v3, w3, beta3, root3, 4)

    first3 = 2 * place[0] - 2 + OFF3
    first2 = 4 * place[0] - 4 + OFF2
    e3 = [w3[first3 + k, pl.ds(28, 24), :] * inverse(root3[first3 + k, pl.ds(20, 24), :]) for k in range(6)]
    e3 = mm(((jnp.concatenate(e3, axis=0), u3[...]),))
    for k in range(6):
        unfold_rows(fine2, k, 24, e3[k * 24 : (k + 1) * 24])
    for p in range(12):
        add = root2[first2 + p, pl.ds(8, 48), :] * fine2[p // 2]
        w2b[p, pl.ds(16, 48), :] = w2[first2 + p, pl.ds(16, 48), :] + add
        for ref in (w2b, v2):
            ref[p, pl.ds(8, 8), :] = jnp.zeros((8, LANES), F32)
            ref[p, pl.ds(64, 8), :] = jnp.zeros((8, LANES), F32)
    relax_whole(1, 10, 8, 48, 2 * width, w2b, v2, beta2, root2, 10, first2)
    relax_whole(2, 8, 8, 48, 2 * width, v2, w2b, beta2, root2, 8, first2)
    for k in range(8):
        e2[k] = w2b[k + 2, pl.ds(20, 40), :] * inverse(root2[first2 + k + 2, pl.ds(12, 40), :])


def up_kernel(gy, place, e2, w1, beta1, root1, w0, beta0, root0, u1, out, w1b, v1, w0b, v0, fine1, fine0, turned):
    width = 4 * gy
    source_lane = lax.broadcasted_iota(jnp.int32, (LANES, LANES), 0)
    target_lane = lane_of(LANES)
    wanted_y = 4 * place[0] - 2 + ((target_lane & (Y1 - 1)) >> 1)
    wanted = (target_lane >> 4) * width + wanted_y
    valid = (source_lane == wanted) & (wanted_y >= 0) & (wanted_y < width) & (target_lane < 4 * Y1)
    u2 = jnp.where(valid, 1.0, 0.0).astype(jnp.bfloat16)
    for ref in (w1b, v1):
        for row in (0, 88):
            ref[:, pl.ds(row, 8), :] = jnp.zeros((16, 8, LANES), F32)
    for ref in (w0b, v0):
        for row in (0, 152):
            ref[:, pl.ds(row, 8), :] = jnp.zeros((20, 8, LANES), F32)
    for k in range(0, 8, 4):
        e = mm(((jnp.concatenate([e2[k + i] for i in range(4)], axis=0), u2),))
        for i in range(4):
            unfold_rows(fine1, k + i, 40, e[i * 40 : (i + 1) * 40])
    for x in range(1, 15):
        w1b[x, pl.ds(8, 80), :] = w1[x, pl.ds(8, 80), :] + root1[x] * fine1[x // 2]

    def relax1(src, dst, begin, end):
        def body(x):
            for r, n in chunks(80, 40):
                mid, total = around(src, x, 8 + r, n)
                live = root1[x, pl.ds(r, n), :] > 0.0
                dst[x, pl.ds(8 + r, n), :] = jacobi(live, mid, beta1[x, pl.ds(8 + r, n), :], total)

        loop(begin, end, body, end - begin)

    relax1(w1b, v1, 2, 14)
    relax1(v1, w1b, 3, 13)

    for k in range(0, 10, 2):
        e = [w1b[x, pl.ds(12, 72), :] * inverse(root1[x, pl.ds(4, 72), :]) for x in (k + 3, k + 4)]
        e = mm(((jnp.concatenate(e, axis=0), u1[...]),))
        for i in range(2):
            unfold_rows(fine0, k + i, 72, e[i * 72 : (i + 1) * 72])

    def up0(k):
        for i in range(2):
            x = 2 * k + i
            for r, n in chunks(144, 48):
                add = root0[x + 1, pl.ds(8 + r, n), :] * fine0[k, pl.ds(r, n), :]
                w0b[x, pl.ds(8 + r, n), :] = w0[x + 1, pl.ds(16 + r, n), :] + add

    loop(0, 10, up0, 10)

    def first0(x):
        for r, n in chunks(144, 24):
            mid, total = around(w0b, x, 8 + r, n)
            live = root0[x + 1, pl.ds(8 + r, n), :] > 0.0
            v0[x, pl.ds(8 + r, n), :] = jacobi(live, mid, beta0[x + 1, pl.ds(16 + r, n), :], total)

    loop(1, 19, first0, 9)

    def last0(j):
        for slot in range(4):
            k = 4 * j + slot
            x = k + 2
            for r, n in chunks(128, 32):
                mid, total = around(v0, x, 16 + r, n)
                root_x = root0[x + 1, pl.ds(16 + r, n), :]
                new = jacobi(root_x > 0.0, mid, beta0[x + 1, pl.ds(24 + r, n), :], total)
                turned[slot, pl.ds(r, n), :] = new * inverse(root_x)
        for slot in range(4):
            t = turned[slot].T
            for f in range(4):
                out[f, 4 * j + slot] = t[f * Y0 + HY0 : f * Y0 + HY0 + 16]

    loop(0, 4, last0)


def call(kernel, args, outs, scratch, smem=0):
    vmem = pl.BlockSpec(memory_space=pltpu.VMEM)
    scalar = pl.BlockSpec(memory_space=pltpu.SMEM)
    return pl.pallas_call(
        kernel,
        out_shape=[jax.ShapeDtypeStruct(s, F32) for s in outs],
        in_specs=[scalar] * smem + [vmem] * (len(args) - smem),
        out_specs=[vmem] * len(outs),
        scratch_shapes=[pltpu.VMEM(s, F32) for s in scratch],
        compiler_params=pltpu.CompilerParams(vmem_limit_bytes=16 * 1024 * 1024),
    )(*args)


def swap(to_up, to_down, axis):
    n = lax.axis_size(axis)
    from_below = lax.ppermute(to_up, axis, [(i, i + 1) for i in range(n - 1)])
    from_above = lax.ppermute(to_down, axis, [(i + 1, i) for i in range(n - 1)])
    return from_below, from_above


def whole_plane(block):
    return lax.all_to_all(block, ("gx", "gy"), 0, 0, tiled=True)


def position(axis):
    return lax.axis_index(axis).astype(jnp.int32)


def shards(gx, gy, source, material_ids, material_table, roughness):
    spread = np.repeat(np.eye(16, dtype=np.float32), 8, axis=1)
    visc, low, high = call(
        prepare_kernel,
        (material_table, material_ids, spread, source, roughness),
        [(16, 16, LANES)] + [(5, HX0, 16, LANES)] * 2,
        [],
        smem=1,
    )
    xlo, xhi = swap(high, low, "gx")
    planes = 16 + 2 * HX0
    ysend_lo, ysend_hi = call(edge_kernel, (xlo, source, visc, xhi), [(planes, 15, LANES)] * 2, [])
    ylo, yhi = swap(ysend_hi, ysend_lo, "gy")
    turned, zsend_lo, zsend_hi = call(
        turn_kernel,
        (xlo, source, visc, xhi, ylo, yhi),
        [(planes, 128, LANES)] + [(planes, HZ0, LANES)] * 2,
        [(4, LANES, LANES)],
    )
    zlo, zhi = swap(zsend_hi, zsend_lo, "gz")

    q0b = pair_lanes(Y0, HY0, (0, 1, 2, 3), 8, 0, 0.5)
    q0c = pair_lanes(Y0, HY0, (0, 3), 8, 32, 0.125)
    depth = 128 + 2 * HZ0
    own1, ysend_lo, ysend_hi, w0, beta0, root0 = call(
        down0_kernel,
        (turned, zlo, zhi, q0b, q0c),
        [(8, 48, LANES)] + [(8, 24, LANES)] * 2 + [(planes, depth + 16, LANES)] * 2 + [(planes, depth, LANES)],
        [(8, depth, LANES)] * 2 + [(4 * depth, LANES)] * 2 + [(8, LANES, LANES)],
    )
    ylo, yhi = swap(ysend_hi, ysend_lo, "gy")
    low, high = call(join_kernel, (own1, ylo, yhi), [(4, 96, LANES)] * 2, [])
    xlo, xhi = swap(high, low, "gx")

    q1b = pair_lanes(Y1, 4, (0, 1, 2, 3), 4, 0, 0.5)
    q1c = pair_lanes(Y1, 4, (0, 3), 4, 16, 0.125)
    block, w1, beta1, root1 = call(
        down1_kernel,
        (own1, ylo, yhi, xlo, xhi, q1b, q1c),
        [(gx * gy, 24, LANES), (16, 96, LANES), (16, 96, LANES), (16, 80, LANES)],
        [(4, LANES, LANES)] + [(4, 64, LANES)] * 2 + [(LANES, LANES)] * 2,
    )
    got = whole_plane(block)

    x2, x3 = 4 * gx, 2 * gx
    b2, c2, zsend_lo, zsend_hi = call(
        functools.partial(plane_kernel, gx, gy),
        (got,),
        [(x2, 32, LANES)] * 2 + [(x2, 16, LANES)] * 2,
        [(2, LANES, LANES)] * 2,
    )
    zlo, zhi = swap(zsend_hi, zsend_lo, "gz")

    q2b = pair_lanes(4 * gy, 0, (0, 1, 2, 3), 2 * gy, 0, 0.5)
    q2c = pair_lanes(4 * gy, 0, (0, 1, 2, 3), 2 * gy, 64, 0.125)
    own3, zsend_up, zsend_down, w2, beta2, root2 = call(
        functools.partial(down2_kernel, gx, gy),
        (b2, c2, zlo, zhi, q2b, q2c),
        [(x3, 32, LANES)] + [(x3, HZ3, LANES)] * 2 + [(x2 + 2 * OFF2, 80, LANES)] * 2 + [(x2 + 2 * OFF2, 64, LANES)],
        [(x3, 64, LANES)] * 2 + [(x3 * 32, LANES)] * 2,
    )
    zlo, zhi = swap(zsend_up, zsend_down, "gz")

    q3b = pair_lanes(2 * gy, 0, (0, 1, 2, 3), gy, 0, 0.5)
    q3c = pair_lanes(2 * gy, 0, (0, 1, 2, 3), gy, 64, 0.125)
    u4 = repeat_lanes(gy, 0, 2 * gy, 0)
    u3 = repeat_lanes(2 * gy, 0, 4 * gy, 0)
    (e2,) = call(
        functools.partial(coarse_kernel, gx, gy),
        (position("gx").reshape(1), own3, zlo, zhi, w2, beta2, root2, q3b, q3c, u4, u3),
        [(8, 40, LANES)],
        [(x3 + 2 * OFF3, 80, LANES)] * 3
        + [(x3 + 2 * OFF3, 64, LANES)]
        + [(gx + 2, 48, LANES)] * 3
        + [(gx + 2, 32, LANES)]
        + [(gx, 64, LANES)] * 2
        + [(gx * 32, LANES)] * 2
        + [(12, 80, LANES)] * 2
        + [(gx, 32, LANES), (6, 48, LANES)],
        smem=1,
    )

    u1 = repeat_lanes(Y1, 4, Y0, HY0)
    (correction,) = call(
        functools.partial(up_kernel, gy),
        (position("gy").reshape(1), e2, w1, beta1, root1, w0, beta0, root0, u1),
        [(4, 16, 16, LANES)],
        [(16, 96, LANES)] * 2
        + [(20, 160, LANES)] * 2
        + [(8, 80, LANES), (10, 144, LANES), (4, LANES, LANES)],
        smem=1,
    )
    return correction


def solution(mesh):
    return jax.shard_map(
        functools.partial(shards, mesh.shape["gx"], mesh.shape["gy"]),
        mesh=mesh,
        in_specs=(P(None, "gx", "gy", "gz"), P("gx", "gy", "gz"), P(), P("gx", "gy", "gz")),
        out_specs=P(None, "gx", "gy", "gz"),
        check_vma=False,
    )
```

time: 711 us -> 159 us (0.22)
  the two profiles are of different devices: /device:TPU:479 before, /device:TPU:261 now
where the time goes in v2:
time: 159 us; the launch traced here: 158 us
  starting transfers between devices  42 us (26%)
  waiting for transfers between devices  41.3 us (26%)
  blocking collectives  34.5 us (22%)
  Pallas kernels  22.9 us (14%)
  local copies, waits for them, and re-layouts  16.7 us (11%)
    ppermute x7, waiting for transfers between devices, swap(): from_above = lax.ppermute(to_down, axis, [(i + 1, i) for i in range(n - 1)])  35 us
    all_to_all x1, blocking collectives, whole_plane(): return lax.all_to_all(block, ('gx', 'gy'), 0, 0, tiled=True)  34.5 us
    ppermute x7, starting transfers between devices, swap(): from_below = lax.ppermute(to_up, axis, [(i, i + 1) for i in range(n - 1)])  29.6 us
    pallas_call x10, Pallas kernels, call(): pl.pallas_call(kernel, out_shape=[jax.ShapeDtypeStruct(s, F32) for s in o...  22.9 us
    unnamed x62, local copies, waits for them, and re-layouts  16.7 us
    ppermute x7, starting transfers between devices, swap(): from_above = lax.ppermute(to_down, axis, [(i + 1, i) for i in range(n - 1)])  12.4 us
    ppermute x7, waiting for transfers between devices, swap(): from_below = lax.ppermute(to_up, axis, [(i, i + 1) for i in range(n - 1)])  6.35 us
  transfers between devices with their start and end apart: 14, of which 14 were waited for; matrix products, arithmetic and copies ran while one was open for 0% of the time, Pallas kernels for 0%

profile of v2, /device:TPU:261, one launch (start us, length us, event | category | flops | bytes accessed | tf_op | source)
XLA Modules:
  0.0 157.7 jit_solution(11514910987660374879)
XLA Ops:
  0.0 1.0 copy-done
  1.0 0.9 copy-done.16
  1.9 0.7 copy-done.28
  4.7 3.1 %collective-permute-start = (f32[5,3,16,128]{3,2,1,0:T(8,128)S(1)}, f32[5,3,16,128]{3,2,1,0:T(8,128)S(1)}, u32[]{:S(2)}, u32[]{:S(2)}) collective-permute-start(f32[5,3,16,128]{3,2,1,0:T(8,128)S(1)} %get-tuple-element.35), channel_id=1, source_target_pairs={{0,128},{128,256},{256,384},{384,512},{512,640},{640,768},{768,896... | collective-permute-start | bytes 368648 | tf_op jit(solution)/shard_map/ppermute | solution.py:567
  7.8 2.2 %collective-permute-start.1 = (f32[5,3,16,128]{3,2,1,0:T(8,128)S(1)}, f32[5,3,16,128]{3,2,1,0:T(8,128)S(1)}, u32[]{:S(2)}, u32[]{:S(2)}) collective-permute-start(f32[5,3,16,128]{3,2,1,0:T(8,128)S(1)} %get-tuple-element.37), channel_id=1, source_target_pairs={{128,0},{256,128},{384,256},{512,384},{640,512},{768,640},{896,768... | collective-permute-start | bytes 368648 | tf_op jit(solution)/shard_map/ppermute | solution.py:568
  10.0 0.8 collective-permute-done.xlo
  10.8 4.1 %collective-permute-done.1.xhi = f32[5,3,16,128]{3,2,1,0:T(8,128)S(1)} collective-permute-done((f32[5,3,16,128]{3,2,1,0:T(8,128)S(1)}, f32[5,3,16,128]{3,2,1,0:T(8,128)S(1)}, u32[]{:S(2)}, u32[]{:S(2)}) %collective-permute-start.1) | collective-permute-done | bytes 122912 | tf_op jit(solution)/shard_map/ppermute | solution.py:568
  14.9 1.0 copy-done.1
  16.0 3.3 %collective-permute-start.2 = (f32[22,15,128]{2,1,0:T(8,128)S(1)}, f32[22,15,128]{2,1,0:T(8,128)S(1)}, u32[]{:S(2)}, u32[]{:S(2)}) collective-permute-start(f32[22,15,128]{2,1,0:T(8,128)S(1)} %get-tuple-element.38), channel_id=1, source_target_pairs={{0,16},{16,32},{32,48},{48,64},{64,80},{80,96},{96,112},{1,17},{17... | collective-permute-start | bytes 506888 | tf_op jit(solution)/shard_map/ppermute | solution.py:567
  19.3 1.3 collective-permute-start.3
  20.6 1.1 collective-permute-done.2.ylo
  21.7 3.9 %collective-permute-done.3.yhi = f32[22,15,128]{2,1,0:T(8,128)S(1)} collective-permute-done((f32[22,15,128]{2,1,0:T(8,128)S(1)}, f32[22,15,128]{2,1,0:T(8,128)S(1)}, u32[]{:S(2)}, u32[]{:S(2)}) %collective-permute-start.3) | collective-permute-done | bytes 168992 | tf_op jit(solution)/shard_map/ppermute | solution.py:568
  26.2 7.8 %collective-permute-start.4 = (f32[22,16,128]{2,1,0:T(8,128)S(1)}, f32[22,16,128]{2,1,0:T(8,128)S(1)}, u32[]{:S(2)}, u32[]{:S(2)}) collective-permute-start(f32[22,16,128]{2,1,0:T(8,128)S(1)} %get-tuple-element.41), channel_id=1, source_target_pairs={{0,1},{1,2},{2,3},{3,4},{4,5},{5,6},{6,7},{7,8},{8,9},{9,10},{10,1... | collective-permute-start | bytes 540680 | tf_op jit(solution)/shard_map/ppermute | solution.py:567
  34.0 1.9 %collective-permute-start.5 = (f32[22,16,128]{2,1,0:T(8,128)S(1)}, f32[22,16,128]{2,1,0:T(8,128)S(1)}, u32[]{:S(2)}, u32[]{:S(2)}) collective-permute-start(f32[22,16,128]{2,1,0:T(8,128)S(1)} %get-tuple-element.42), channel_id=1, source_target_pairs={{1,0},{2,1},{3,2},{4,3},{5,4},{6,5},{7,6},{8,7},{9,8},{10,9},{11,1... | collective-permute-start | bytes 540680 | tf_op jit(solution)/shard_map/ppermute | solution.py:568
  36.4 4.4 %collective-permute-done.5.zhi = f32[22,16,128]{2,1,0:T(8,128)S(1)} collective-permute-done((f32[22,16,128]{2,1,0:T(8,128)S(1)}, f32[22,16,128]{2,1,0:T(8,128)S(1)}, u32[]{:S(2)}, u32[]{:S(2)}) %collective-permute-start.5) | collective-permute-done | bytes 180256 | tf_op jit(solution)/shard_map/ppermute | solution.py:568
  40.8 5.3 %shard_map.157 = (f32[8,48,128]{2,1,0:T(8,128)S(1)}, f32[8,24,128]{2,1,0:T(8,128)S(1)}, f32[8,24,128]{2,1,0:T(8,128)S(1)}, f32[22,176,128]{2,1,0:T(8,128)S(1)}, ...) custom-call(f32[22,128,128]{2,1,0:T(8,128)S(1)} %get-tuple-element.40.turned, ...), custom_call_target="tpu_custom_call" | custom-call | tf_op jit(solution)/shard_map/pallas_call | solution.py:555
  46.1 1.3 copy-done.2
  47.5 3.3 %collective-permute-start.6 = (f32[8,24,128]{2,1,0:T(8,128)S(1)}, f32[8,24,128]{2,1,0:T(8,128)S(1)}, u32[]{:S(2)}, u32[]{:S(2)}) collective-permute-start(f32[8,24,128]{2,1,0:T(8,128)S(1)} %get-tuple-element.44), channel_id=1, source_target_pairs={{0,16},{16,32},{32,48},{48,64},{64,80},{80,96},{96,112},{1,17},{17... | collective-permute-start | bytes 294920 | tf_op jit(solution)/shard_map/ppermute | solution.py:567
  50.8 1.3 collective-permute-start.7
  52.4 4.6 %collective-permute-done.7.yhi = f32[8,24,128]{2,1,0:T(8,128)S(1)} collective-permute-done((f32[8,24,128]{2,1,0:T(8,128)S(1)}, f32[8,24,128]{2,1,0:T(8,128)S(1)}, u32[]{:S(2)}, u32[]{:S(2)}) %collective-permute-start.7) | collective-permute-done | bytes 98336 | tf_op jit(solution)/shard_map/ppermute | solution.py:568
  57.0 4.7 %collective-permute-start.8 = (f32[4,96,128]{2,1,0:T(8,128)S(1)}, f32[4,96,128]{2,1,0:T(8,128)S(1)}, u32[]{:S(2)}, u32[]{:S(2)}) collective-permute-start(f32[4,96,128]{2,1,0:T(8,128)S(1)} %get-tuple-element.46), channel_id=1, source_target_pairs={{0,128},{128,256},{256,384},{384,512},{512,640},{640,768},{768,896... | collective-permute-start | bytes 589832 | tf_op jit(solution)/shard_map/ppermute | solution.py:567
  61.7 1.9 %collective-permute-start.9 = (f32[4,96,128]{2,1,0:T(8,128)S(1)}, f32[4,96,128]{2,1,0:T(8,128)S(1)}, u32[]{:S(2)}, u32[]{:S(2)}) collective-permute-start(f32[4,96,128]{2,1,0:T(8,128)S(1)} %get-tuple-element.47), channel_id=1, source_target_pairs={{128,0},{256,128},{384,256},{512,384},{640,512},{768,640},{896,768... | collective-permute-start | bytes 589832 | tf_op jit(solution)/shard_map/ppermute | solution.py:568
  63.6 1.3 collective-permute-done.8.xlo
  65.0 4.1 %collective-permute-done.9.xhi = f32[4,96,128]{2,1,0:T(8,128)S(1)} collective-permute-done((f32[4,96,128]{2,1,0:T(8,128)S(1)}, f32[4,96,128]{2,1,0:T(8,128)S(1)}, u32[]{:S(2)}, u32[]{:S(2)}) %collective-permute-start.9) | collective-permute-done | bytes 196640 | tf_op jit(solution)/shard_map/ppermute | solution.py:568
  69.1 1.6 %shard_map.159 = (f32[64,24,128]{2,1,0:T(8,128)S(1)}, f32[16,96,128]{2,1,0:T(8,128)S(1)}, f32[16,96,128]{2,1,0:T(8,128)S(1)}, f32[16,80,128]{2,1,0:T(8,128)S(1)}) custom-call(f32[8,48,128]{2,1,0:T(8,128)S(1)} %get-tuple-element.43.own, f32[8,24,128]{2,1,0:T(8,128)S(1)} %collective-permute-done.6.ylo, f32[8,24,128]{2,1,0:T(8,128)S(1)} %collective-permute-done.7.yhi, ...), custom_call_target="tpu_custom_call" | custom-call | tf_op jit(solution)/shard_map/pallas_call | solution.py:555
  70.7 1.0 copy-done.10
  71.6 34.5 %all_to_all.5.got = f32[64,24,128]{2,1,0:T(8,128)S(1)} all-to-all(f32[64,24,128]{2,1,0:T(8,128)S(1)} %get-tuple-element.48), channel_id=1, replica_groups=mesh['gx'=8,'gy'=8,'gz'=16] {'gx','gy'}, dimensions={0} | all-to-all | bytes 1572864 | tf_op jit(solution)/shard_map/all_to_all | solution.py:573
  106.1 1.0 shard_map.160
  107.2 3.2 %collective-permute-start.10 = (f32[32,16,128]{2,1,0:T(8,128)S(1)}, f32[32,16,128]{2,1,0:T(8,128)S(1)}, u32[]{:S(2)}, u32[]{:S(2)}) collective-permute-start(f32[32,16,128]{2,1,0:T(8,128)S(1)} %get-tuple-element.51), channel_id=1, source_target_pairs={{0,1},{1,2},{2,3},{3,4},{4,5},{5,6},{6,7},{7,8},{8,9},{9,10},{10,1... | collective-permute-start | bytes 786440 | tf_op jit(solution)/shard_map/ppermute | solution.py:567
  110.4 1.9 %collective-permute-start.11 = (f32[32,16,128]{2,1,0:T(8,128)S(1)}, f32[32,16,128]{2,1,0:T(8,128)S(1)}, u32[]{:S(2)}, u32[]{:S(2)}) collective-permute-start(f32[32,16,128]{2,1,0:T(8,128)S(1)} %get-tuple-element.52), channel_id=1, source_target_pairs={{1,0},{2,1},{3,2},{4,3},{5,4},{6,5},{7,6},{8,7},{9,8},{10,9},{11,1... | collective-permute-start | bytes 786440 | tf_op jit(solution)/shard_map/ppermute | solution.py:568
  112.3 1.4 collective-permute-done.10.zlo
  113.7 5.3 %collective-permute-done.11.zhi = f32[32,16,128]{2,1,0:T(8,128)S(1)} collective-permute-done((f32[32,16,128]{2,1,0:T(8,128)S(1)}, f32[32,16,128]{2,1,0:T(8,128)S(1)}, u32[]{:S(2)}, u32[]{:S(2)}) %collective-permute-start.11) | collective-permute-done | bytes 262176 | tf_op jit(solution)/shard_map/ppermute | solution.py:568
  119.0 4.2 %shard_map.161 = (f32[16,32,128]{2,1,0:T(8,128)S(1)}, f32[16,20,128]{2,1,0:T(8,128)}, f32[16,20,128]{2,1,0:T(8,128)}, f32[40,80,128]{2,1,0:T(8,128)S(1)}, f32[40...) custom-call(f32[32,32,128]{2,1,0:T(8,128)S(1)} %get-tuple-element.49.b, f32[32,32,128]{2,1,0:T(8,128)S(1)} %get-tuple-element.50.c, ...), custom_call_target="tpu_custom_call" | custom-call | tf_op jit(solution)/shard_map/pallas_call | solution.py:555
  123.2 1.2 copy-done.6
  124.4 1.2 copy-done.8
  125.5 4.2 %collective-permute-start.12 = (f32[16,20,128]{2,1,0:T(8,128)}, f32[16,20,128]{2,1,0:T(8,128)}, u32[]{:S(2)}, u32[]{:S(2)}) collective-permute-start(f32[16,20,128]{2,1,0:T(8,128)} %get-tuple-element.54), channel_id=1, source_target_pairs={{0,1},{1,2},{2,3},{3,4},{4,5},{5,6},{6,7},{7,8},{8,9},{9,10},{10,1... | collective-permute-start | bytes 491528 | tf_op jit(solution)/shard_map/ppermute | solution.py:567
  129.7 1.9 %collective-permute-start.13 = (f32[16,20,128]{2,1,0:T(8,128)}, f32[16,20,128]{2,1,0:T(8,128)}, u32[]{:S(2)}, u32[]{:S(2)}) collective-permute-start(f32[16,20,128]{2,1,0:T(8,128)} %get-tuple-element.55), channel_id=1, source_target_pairs={{1,0},{2,1},{3,2},{4,3},{5,4},{6,5},{7,6},{8,7},{9,8},{10,9},{11,1... | collective-permute-start | bytes 491528 | tf_op jit(solution)/shard_map/ppermute | solution.py:568
  131.7 1.0 collective-permute-done.12.zlo
  132.6 8.6 %collective-permute-done.13.zhi = f32[16,20,128]{2,1,0:T(8,128)} collective-permute-done((f32[16,20,128]{2,1,0:T(8,128)}, f32[16,20,128]{2,1,0:T(8,128)}, u32[]{:S(2)}, u32[]{:S(2)}) %collective-permute-start.13) | collective-permute-done | bytes 163872 | tf_op jit(solution)/shard_map/ppermute | solution.py:568
  141.3 1.4 copy-done.7
  142.7 1.4 copy-done.9
  144.2 0.8 copy-done.18
  144.9 0.8 copy-done.19
  145.7 0.8 copy-done.20
  146.4 0.8 copy-done.21
  147.2 5.1 %shard_map.162.e2 = f32[8,40,128]{2,1,0:T(8,128)S(1)} custom-call(s32[1]{0:T(128)} %bitcast.1.place, f32[16,32,128]{2,1,0:T(8,128)S(1)} %get-tuple-element.53.own, f32[16,20,128]{2,1,0:T(8,128)} %collective-permute-done.12.zlo, f32[16,20,128]{2,1,0:T(8,128)} %collective-permute-done.13.zhi, f32[40,80,128]{2,1,0:T(8,128)S(1)} %copy-done.7, ...), custom_call_target="tpu_custom_call" | custom-call | tf_op jit(solution)/shard_map/pallas_call | solution.py:555
  152.4 1.1 copy-done.15
  153.5 4.2 %shard_map.163 = f32[4,16,16,128]{3,2,1,0:T(8,128)} custom-call(s32[1]{0:T(128)} %bitcast.place, f32[8,40,128]{2,1,0:T(8,128)S(1)} %shard_map.162.e2, f32[16,96,128]{2,1,0:T(8,128)S(1)} %copy-done.11, f32[16,96,128]{2,1,0:T(8,128)S(1)} %copy-done.13, f32[16,80,128]{2,1,0:T(8,128)S(1)} %copy-done.15, f32[22,176,128]{2,1,0:T(8,128)S(1)} %get-tuple-element.62.w0, ...), custom_call_target="tpu_custom_call" | custom-call | tf_op jit(solution)/shard_map/pallas_call | solution.py:555
  (53 shorter events, 3.7 us)
Async XLA Ops:
  0.0 1.0 copy-start
  1.0 0.9 copy-start.16
  1.9 0.7 copy-start.28
  2.6 0.7 copy-start.29
  3.3 0.7 copy-start.30
  4.0 36.9 %copy-start.22 = (bf16[128,128]{1,0:T(8,128)(2,1)S(1)}, bf16[128,128]{1,0:T(8,128)(2,1)}, u32[]{:S(2)}) copy-start(bf16[128,128]{1,0:T(8,128)(2,1)} %constant.34.clone.qb) | copy-start | bytes 98308
  4.0 36.9 %copy-start.23 = (bf16[128,128]{1,0:T(8,128)(2,1)S(1)}, bf16[128,128]{1,0:T(8,128)(2,1)}, u32[]{:S(2)}) copy-start(bf16[128,128]{1,0:T(8,128)(2,1)} %constant.35.clone.qc) | copy-start | bytes 98308
  4.7 6.1 %collective-permute-start = (f32[5,3,16,128]{3,2,1,0:T(8,128)S(1)}, f32[5,3,16,128]{3,2,1,0:T(8,128)S(1)}, u32[]{:S(2)}, u32[]{:S(2)}) collective-permute-start(f32[5,3,16,128]{3,2,1,0:T(8,128)S(1)} %get-tuple-element.35), channel_id=1, source_target_pairs={{0,128},{128,256},{256,384},{384,512},{512,640},{640,768},{768,896... | collective-permute-start | bytes 368648 | tf_op jit(solution)/shard_map/ppermute | solution.py:567
  7.8 7.1 %collective-permute-start.1 = (f32[5,3,16,128]{3,2,1,0:T(8,128)S(1)}, f32[5,3,16,128]{3,2,1,0:T(8,128)S(1)}, u32[]{:S(2)}, u32[]{:S(2)}) collective-permute-start(f32[5,3,16,128]{3,2,1,0:T(8,128)S(1)} %get-tuple-element.37), channel_id=1, source_target_pairs={{128,0},{256,128},{384,256},{512,384},{640,512},{768,640},{896,768... | collective-permute-start | bytes 368648 | tf_op jit(solution)/shard_map/ppermute | solution.py:568
  14.9 1.0 copy-start.1
  16.0 5.7 %collective-permute-start.2 = (f32[22,15,128]{2,1,0:T(8,128)S(1)}, f32[22,15,128]{2,1,0:T(8,128)S(1)}, u32[]{:S(2)}, u32[]{:S(2)}) collective-permute-start(f32[22,15,128]{2,1,0:T(8,128)S(1)} %get-tuple-element.38), channel_id=1, source_target_pairs={{0,16},{16,32},{32,48},{48,64},{64,80},{80,96},{96,112},{1,17},{17... | collective-permute-start | bytes 506888 | tf_op jit(solution)/shard_map/ppermute | solution.py:567
  19.3 49.8 %copy-start.26 = (bf16[128,128]{1,0:T(8,128)(2,1)S(1)}, bf16[128,128]{1,0:T(8,128)(2,1)}, u32[]{:S(2)}) copy-start(bf16[128,128]{1,0:T(8,128)(2,1)} %constant.36.clone.qb) | copy-start | bytes 98308
  19.3 49.8 %copy-start.27 = (bf16[128,128]{1,0:T(8,128)(2,1)S(1)}, bf16[128,128]{1,0:T(8,128)(2,1)}, u32[]{:S(2)}) copy-start(bf16[128,128]{1,0:T(8,128)(2,1)} %constant.37.clone.qc) | copy-start | bytes 98308
  19.3 6.2 %collective-permute-start.3 = (f32[22,15,128]{2,1,0:T(8,128)S(1)}, f32[22,15,128]{2,1,0:T(8,128)S(1)}, u32[]{:S(2)}, u32[]{:S(2)}) collective-permute-start(f32[22,15,128]{2,1,0:T(8,128)S(1)} %get-tuple-element.39), channel_id=1, source_target_pairs={{16,0},{32,16},{48,32},{64,48},{80,64},{96,80},{112,96},{17,1},{33... | collective-permute-start | bytes 506888 | tf_op jit(solution)/shard_map/ppermute | solution.py:568
  26.2 10.2 %collective-permute-start.4 = (f32[22,16,128]{2,1,0:T(8,128)S(1)}, f32[22,16,128]{2,1,0:T(8,128)S(1)}, u32[]{:S(2)}, u32[]{:S(2)}) collective-permute-start(f32[22,16,128]{2,1,0:T(8,128)S(1)} %get-tuple-element.41), channel_id=1, source_target_pairs={{0,1},{1,2},{2,3},{3,4},{4,5},{5,6},{6,7},{7,8},{8,9},{9,10},{10,1... | collective-permute-start | bytes 540680 | tf_op jit(solution)/shard_map/ppermute | solution.py:567
  34.0 6.8 %collective-permute-start.5 = (f32[22,16,128]{2,1,0:T(8,128)S(1)}, f32[22,16,128]{2,1,0:T(8,128)S(1)}, u32[]{:S(2)}, u32[]{:S(2)}) collective-permute-start(f32[22,16,128]{2,1,0:T(8,128)S(1)} %get-tuple-element.42), channel_id=1, source_target_pairs={{1,0},{2,1},{3,2},{4,3},{5,4},{6,5},{7,6},{8,7},{9,8},{10,9},{11,1... | collective-permute-start | bytes 540680 | tf_op jit(solution)/shard_map/ppermute | solution.py:568
  46.1 1.3 copy-start.2
  47.5 59.7 %copy-start.4 = (f32[22,160,128]{2,1,0:T(8,128)}, f32[22,160,128]{2,1,0:T(8,128)S(1)}, u32[]{:S(2)}) copy-start(f32[22,160,128]{2,1,0:T(8,128)S(1)} %get-tuple-element.64.root0) | copy-start | bytes 5406724
  47.5 4.9 %collective-permute-start.6 = (f32[8,24,128]{2,1,0:T(8,128)S(1)}, f32[8,24,128]{2,1,0:T(8,128)S(1)}, u32[]{:S(2)}, u32[]{:S(2)}) collective-permute-start(f32[8,24,128]{2,1,0:T(8,128)S(1)} %get-tuple-element.44), channel_id=1, source_target_pairs={{0,16},{16,32},{32,48},{48,64},{64,80},{80,96},{96,112},{1,17},{17... | collective-permute-start | bytes 294920 | tf_op jit(solution)/shard_map/ppermute | solution.py:567
  50.8 6.2 %collective-permute-start.7 = (f32[8,24,128]{2,1,0:T(8,128)S(1)}, f32[8,24,128]{2,1,0:T(8,128)S(1)}, u32[]{:S(2)}, u32[]{:S(2)}) collective-permute-start(f32[8,24,128]{2,1,0:T(8,128)S(1)} %get-tuple-element.45), channel_id=1, source_target_pairs={{16,0},{32,16},{48,32},{64,48},{80,64},{96,80},{112,96},{17,1},{33... | collective-permute-start | bytes 294920 | tf_op jit(solution)/shard_map/ppermute | solution.py:568
  57.0 62.0 %copy-start.24 = (bf16[128,128]{1,0:T(8,128)(2,1)S(1)}, bf16[128,128]{1,0:T(8,128)(2,1)}, u32[]{:S(2)}) copy-start(bf16[128,128]{1,0:T(8,128)(2,1)} %constant.38.clone.qb) | copy-start | bytes 98308
  57.0 62.0 %copy-start.25 = (bf16[128,128]{1,0:T(8,128)(2,1)S(1)}, bf16[128,128]{1,0:T(8,128)(2,1)}, u32[]{:S(2)}) copy-start(bf16[128,128]{1,0:T(8,128)(2,1)} %constant.39.clone.qc) | copy-start | bytes 98308
  57.0 7.9 %collective-permute-start.8 = (f32[4,96,128]{2,1,0:T(8,128)S(1)}, f32[4,96,128]{2,1,0:T(8,128)S(1)}, u32[]{:S(2)}, u32[]{:S(2)}) collective-permute-start(f32[4,96,128]{2,1,0:T(8,128)S(1)} %get-tuple-element.46), channel_id=1, source_target_pairs={{0,128},{128,256},{256,384},{384,512},{512,640},{640,768},{768,896... | collective-permute-start | bytes 589832 | tf_op jit(solution)/shard_map/ppermute | solution.py:567
  61.7 7.4 %collective-permute-start.9 = (f32[4,96,128]{2,1,0:T(8,128)S(1)}, f32[4,96,128]{2,1,0:T(8,128)S(1)}, u32[]{:S(2)}, u32[]{:S(2)}) collective-permute-start(f32[4,96,128]{2,1,0:T(8,128)S(1)} %get-tuple-element.47), channel_id=1, source_target_pairs={{128,0},{256,128},{384,256},{512,384},{640,512},{768,640},{896,768... | collective-permute-start | bytes 589832 | tf_op jit(solution)/shard_map/ppermute | solution.py:568
  70.7 1.0 copy-start.10
  71.6 47.4 %copy-start.12 = (f32[16,96,128]{2,1,0:T(8,128)}, f32[16,96,128]{2,1,0:T(8,128)S(1)}, u32[]{:S(2)}) copy-start(f32[16,96,128]{2,1,0:T(8,128)S(1)} %get-tuple-element.60.beta1) | copy-start | bytes 2359300
  71.6 47.4 %copy-start.14 = (f32[16,80,128]{2,1,0:T(8,128)}, f32[16,80,128]{2,1,0:T(8,128)S(1)}, u32[]{:S(2)}) copy-start(f32[16,80,128]{2,1,0:T(8,128)S(1)} %get-tuple-element.61.root1) | copy-start | bytes 1966084
  107.2 6.5 %collective-permute-start.10 = (f32[32,16,128]{2,1,0:T(8,128)S(1)}, f32[32,16,128]{2,1,0:T(8,128)S(1)}, u32[]{:S(2)}, u32[]{:S(2)}) collective-permute-start(f32[32,16,128]{2,1,0:T(8,128)S(1)} %get-tuple-element.51), channel_id=1, source_target_pairs={{0,1},{1,2},{2,3},{3,4},{4,5},{5,6},{6,7},{7,8},{8,9},{9,10},{10,1... | collective-permute-start | bytes 786440 | tf_op jit(solution)/shard_map/ppermute | solution.py:567
  110.4 8.6 %collective-permute-start.11 = (f32[32,16,128]{2,1,0:T(8,128)S(1)}, f32[32,16,128]{2,1,0:T(8,128)S(1)}, u32[]{:S(2)}, u32[]{:S(2)}) collective-permute-start(f32[32,16,128]{2,1,0:T(8,128)S(1)} %get-tuple-element.52), channel_id=1, source_target_pairs={{1,0},{2,1},{3,2},{4,3},{5,4},{6,5},{7,6},{8,7},{9,8},{10,9},{11,1... | collective-permute-start | bytes 786440 | tf_op jit(solution)/shard_map/ppermute | solution.py:568
  123.2 1.2 copy-start.6
  124.4 1.2 copy-start.8
  125.5 7.1 %collective-permute-start.12 = (f32[16,20,128]{2,1,0:T(8,128)}, f32[16,20,128]{2,1,0:T(8,128)}, u32[]{:S(2)}, u32[]{:S(2)}) collective-permute-start(f32[16,20,128]{2,1,0:T(8,128)} %get-tuple-element.54), channel_id=1, source_target_pairs={{0,1},{1,2},{2,3},{3,4},{4,5},{5,6},{6,7},{7,8},{8,9},{9,10},{10,1... | collective-permute-start | bytes 491528 | tf_op jit(solution)/shard_map/ppermute | solution.py:567
  129.7 11.6 %collective-permute-start.13 = (f32[16,20,128]{2,1,0:T(8,128)}, f32[16,20,128]{2,1,0:T(8,128)}, u32[]{:S(2)}, u32[]{:S(2)}) collective-permute-start(f32[16,20,128]{2,1,0:T(8,128)} %get-tuple-element.55), channel_id=1, source_target_pairs={{1,0},{2,1},{3,2},{4,3},{5,4},{6,5},{7,6},{8,7},{9,8},{10,9},{11,1... | collective-permute-start | bytes 491528 | tf_op jit(solution)/shard_map/ppermute | solution.py:568
  141.3 1.4 copy-start.7
  142.7 1.4 copy-start.9
  144.2 0.8 copy-start.18
  144.9 0.8 copy-start.19
  145.7 0.8 copy-start.20
  146.4 0.8 copy-start.21
  147.2 5.2 %copy-start.3 = (f32[22,176,128]{2,1,0:T(8,128)S(1)}, f32[22,176,128]{2,1,0:T(8,128)}, u32[]{:S(2)}) copy-start(f32[22,176,128]{2,1,0:T(8,128)} %copy-done.2) | copy-start | bytes 5947396
  147.2 5.2 %copy-start.5 = (f32[22,160,128]{2,1,0:T(8,128)S(1)}, f32[22,160,128]{2,1,0:T(8,128)}, u32[]{:S(2)}) copy-start(f32[22,160,128]{2,1,0:T(8,128)} %copy-done.4) | copy-start | bytes 5406724
  147.2 5.2 %copy-start.11 = (f32[16,96,128]{2,1,0:T(8,128)S(1)}, f32[16,96,128]{2,1,0:T(8,128)}, u32[]{:S(2)}) copy-start(f32[16,96,128]{2,1,0:T(8,128)} %copy-done.10) | copy-start | bytes 2359300
  147.2 5.2 %copy-start.13 = (f32[16,96,128]{2,1,0:T(8,128)S(1)}, f32[16,96,128]{2,1,0:T(8,128)}, u32[]{:S(2)}) copy-start(f32[16,96,128]{2,1,0:T(8,128)} %copy-done.12) | copy-start | bytes 2359300
  147.2 5.2 %copy-start.17 = (bf16[128,128]{1,0:T(8,128)(2,1)S(1)}, bf16[128,128]{1,0:T(8,128)(2,1)}, u32[]{:S(2)}) copy-start(bf16[128,128]{1,0:T(8,128)(2,1)} %constant.44.clone.u1) | copy-start | bytes 98308
  152.4 1.1 copy-start.15

commit v3 on v2

--- a/solution.py
+++ b/solution.py
@@ -1,8 +1,8 @@
 import functools
+import math
 
 import jax
 import jax.numpy as jnp
-import numpy as np
 from jax import lax
 from jax.experimental import pallas as pl
 from jax.experimental.pallas import tpu as pltpu
@@ -76,23 +76,32 @@
     return jnp.where(live, 0.2 * mid + beta + TAU * total, 0.0)
 
 
-def pair_lanes(width, start, fields, out_width, out_start, scale):
-    m = np.zeros((LANES, LANES), jnp.bfloat16)
-    for k, f in enumerate(fields):
-        for j in range(out_width):
-            for i in range(2):
-                m[f * width + start + 2 * j + i, out_start + k * out_width + j] = scale
-    return m
-
-
-def repeat_lanes(width, shift, out_width, out_shift):
-    m = np.zeros((LANES, LANES), jnp.bfloat16)
-    for f in range(4):
-        for j in range(out_width):
-            i = shift + (j - out_shift) // 2
-            if 0 <= i < width:
-                m[f * width + i, f * out_width + j] = 1.0
-    return m
+def bits(mask):
+    return jnp.where(mask, 1.0, 0.0)
+
+
+def pair_lanes(width, start, out_width, out_start, scale, fields=4, step=1):
+    source = lax.broadcasted_iota(jnp.int32, (LANES, LANES), 0)
+    out = lane_of(LANES) - out_start
+    shift = out_width.bit_length() - 1
+    first = (out >> shift) * (step * width) + start + 2 * (out & (out_width - 1))
+    hit = ((source == first) | (source == first + 1)) & (out >= 0) & (out < fields * out_width)
+    return (scale * bits(hit)).astype(jnp.bfloat16)
+
+
+def repeat_lanes(width, out_width):
+    source = lax.broadcasted_iota(jnp.int32, (LANES, LANES), 0)
+    out = lane_of(LANES)
+    return bits((source == out >> 1) & (out < 4 * out_width)).astype(jnp.bfloat16)
+
+
+def repeat_to_level0():
+    source = lax.broadcasted_iota(jnp.int32, (LANES, LANES), 0)
+    out = lane_of(LANES)
+    field = bits(out >= Y0) + bits(out >= 2 * Y0) + bits(out >= 3 * Y0)
+    field = field.astype(jnp.int32)
+    wanted = field * Y1 + 4 + ((out - field * Y0 - HY0) >> 1)
+    return bits((source == wanted) & (out < 4 * Y0)).astype(jnp.bfloat16)
 
 
 def residual(w, beta, root, x, row, n, mid_total):
@@ -118,25 +127,33 @@
     ref[k, pl.ds(1, n, stride=2), :] = value
 
 
-def prepare_kernel(table, ids, spread, source, roughness, visc, low, high):
-    blocks = jnp.concatenate([ids[0], ids[1]], axis=0)
-    found = jnp.zeros(blocks.shape, F32)
-    for k in range(table.shape[0]):
-        found = found + jnp.where(blocks == k, table[k], 0.0)
-    along_z = jnp.dot(found, spread[...], precision=lax.Precision.HIGHEST, preferred_element_type=F32)
-    for x in range(16):
+def prepare_kernel(table_any, ids_any, source_any, roughness_any, full, low, high, table, ids, roughness, sems):
+    copies = [
+        pltpu.make_async_copy(table_any, table, sems.at[0]),
+        pltpu.make_async_copy(ids_any, ids, sems.at[1]),
+        pltpu.make_async_copy(roughness_any, roughness, sems.at[2]),
+        pltpu.make_async_copy(source_any, full.at[pl.ds(0, 4)], sems.at[3]),
+    ]
+    for copy in copies:
+        copy.start()
+    for copy in copies[:3]:
+        copy.wait()
+    block = lane_of(8) >> 3
+    for i in range(2):
         for j in range(2):
-            row = 2 * (x // 8) + j
-            visc[x, pl.ds(8 * j, 8), :] = roughness[x, pl.ds(8 * j, 8), :] * along_z[row : row + 1]
+            along_z = jnp.zeros((8, LANES), F32)
+            for k in range(16):
+                along_z = jnp.where(block == k, table[ids[i, j, k]], along_z)
+            for x in range(8 * i, 8 * i + 8):
+                full[4, x, pl.ds(8 * j, 8), :] = roughness[x, pl.ds(8 * j, 8), :] * along_z
+    copies[3].wait()
     for x in range(HX0):
-        for f in range(4):
-            low[f, x] = source[f, x]
-            high[f, x] = source[f, 16 - HX0 + x]
-        low[4, x] = visc[x]
-        high[4, x] = visc[16 - HX0 + x]
-
-
-def edge_kernel(xlo, source, visc, xhi, ylo, yhi):
+        for f in range(5):
+            low[f, x] = full[f, x]
+            high[f, x] = full[f, 16 - HX0 + x]
+
+
+def edge_kernel(xlo, full, xhi, ylo, yhi):
     def put(x, f, plane):
         ylo[x, pl.ds(f * HY0, HY0), :] = plane[0:HY0]
         yhi[x, pl.ds(f * HY0, HY0), :] = plane[16 - HY0 : 16]
@@ -147,14 +164,13 @@
             put(x + HX0 + 16, f, xhi[f, x])
 
     def own(x):
-        for f in range(4):
-            put(x + HX0, f, source[f, x])
-        put(x + HX0, 4, visc[x])
+        for f in range(5):
+            put(x + HX0, f, full[f, x])
 
     loop(0, 16, own, 16)
 
 
-def turn_kernel(xlo, source, visc, xhi, ylo, yhi, turned, zlo, zhi, stage):
+def turn_kernel(xlo, full, xhi, ylo, yhi, turned, zlo, zhi, stage):
     stage[...] = jnp.zeros_like(stage)
 
     def turn(x, slot, planes):
@@ -174,15 +190,17 @@
     def own(k):
         for slot in range(4):
             x = 4 * k + slot
-            turn(x + HX0, slot, [source[f, x] for f in range(4)] + [visc[x]])
+            turn(x + HX0, slot, [full[f, x] for f in range(5)])
 
     loop(0, 4, own, 2)
 
 
-def down0_kernel(turned, zlo, zhi, qb, qc, out, ylo, yhi, w, beta, root, rsum, csum, rz, cz, stage):
+def down0_kernel(turned, zlo, zhi, out, ylo, yhi, w, beta, root, rsum, csum, rz, cz, stage):
     planes = 16 + 2 * HX0
     depth = 128 + 2 * HZ0
     half = depth // 2
+    qb = pair_lanes(Y0, HY0, 8, 0, 0.5)
+    qc = pair_lanes(Y0, HY0, 8, 32, 0.125, 2, 3)
 
     def prepare(x, t, row, n):
         lane = lane_of(n)
@@ -230,7 +248,7 @@
         fold(k)
     stage[...] = jnp.zeros_like(stage)
     for k in range(0, 8, 2):
-        both = mm(((rz[pl.ds(k * half, 2 * half), :], qb[...]), (cz[pl.ds(k * half, 2 * half), :], qc[...])))
+        both = mm(((rz[pl.ds(k * half, 2 * half), :], qb), (cz[pl.ds(k * half, 2 * half), :], qc)))
         for i in range(2):
             stage[k + i, pl.ds(0, half), :] = both[i * half : (i + 1) * half]
     for k in range(8):
@@ -249,7 +267,7 @@
             ref[x, pl.ds(72, 24), :] = yhi[first + x]
 
 
-def down1_kernel(own, ylo, yhi, xlo, xhi, qb, qc, block, w, beta, root, stage, rsum, csum, rz, cz):
+def down1_kernel(own, ylo, yhi, xlo, xhi, block, w, beta, root, stage, rsum, csum, rz, cz):
     stage[...] = jnp.zeros_like(stage)
 
     def prepare(x, slot, mine, lo, hi):
@@ -301,7 +319,9 @@
     for k in range(4):
         rz[pl.ds(k * 32, 32), :] = fold_rows(rsum, k, 32)
         cz[pl.ds(k * 32, 32), :] = fold_rows(csum, k, 32)
-    t = mm(((rz[...], qb[...]), (cz[...], qc[...]))).T[0:24]
+    qb = pair_lanes(Y1, 4, 4, 0, 0.5)
+    qc = pair_lanes(Y1, 4, 4, 16, 0.125, 2, 3)
+    t = mm(((rz[...], qb), (cz[...], qc))).T[0:24]
 
     def copy(i):
         block[i] = t
@@ -340,7 +360,7 @@
     loop(0, gx // 2, body)
 
 
-def down2_kernel(gx, gy, b, c, zlo, zhi, qb, qc, out, zup, zdown, w, beta, root, rsum, csum, rz, cz):
+def down2_kernel(gx, gy, place, b, c, zlo, zhi, out, zup, zdown, w_kept, beta_kept, root_kept, w, beta, root, rsum, csum, rz, cz):
     size_x, width = 4 * gx, 4 * gy
 
     def prepare(x, row, t, tc):
@@ -376,9 +396,16 @@
 
     loop(OFF2, size_x + OFF2, smooth, 8)
     restrict_whole(size_x, OFF2, width, w, beta, root, rsum, csum, rz, cz)
+    qb = pair_lanes(width, 0, width // 2, 0, 0.5)
+    qc = pair_lanes(width, 0, width // 2, 64, 0.125)
+    first = 4 * place[0] - 4 + OFF2
+    for p in range(12):
+        w_kept[p] = w[first + p, pl.ds(16, 48), :]
+        beta_kept[p] = beta[first + p, pl.ds(16, 48), :]
+        root_kept[p] = root[first + p, pl.ds(8, 48), :]
     for k in range(0, size_x // 2, 4):
         rows = pl.ds(k * 32, 128)
-        t = mm(((rz[rows, :], qb[...]), (cz[rows, :], qc[...])))
+        t = mm(((rz[rows, :], qb), (cz[rows, :], qc)))
         for i in range(4):
             out[k + i] = t[i * 32 : (i + 1) * 32]
             zup[k + i] = t[i * 32 + 24 - HZ3 : i * 32 + 24]
@@ -400,18 +427,27 @@
         cz[pl.ds(k * 32, 32), :] = fold_rows(csum, k, 32)
 
 
-def relax_whole(first, planes, begin, depth, width, src, dst, beta, root, unroll, shift=0):
+def relax_whole(first, planes, begin, depth, width, src, dst, beta, root, unroll):
     def body(x):
         for r, n in chunks(depth, 32):
             r = r + begin
             mid, total = around_whole(src, x, 8 + r, n, width)
-            live = root[x + shift, pl.ds(r, n), :] > 0.0
-            dst[x, pl.ds(8 + r, n), :] = jacobi(live, mid, beta[x + shift, pl.ds(8 + r, n), :], total)
+            live = root[x, pl.ds(r, n), :] > 0.0
+            dst[x, pl.ds(8 + r, n), :] = jacobi(live, mid, beta[x, pl.ds(8 + r, n), :], total)
 
     loop(first, first + planes, body, unroll)
 
 
-def coarse_kernel(gx, gy, place, own, zlo, zhi, w2, beta2, root2, q3b, q3c, u4, u3, e2, beta3, w3, v3, root3, beta4, w4, v4, root4, rsum, csum, rz, cz, v2, w2b, fine3, fine2):
+def relax_kept(first, planes, width, src, dst, beta, root):
+    def body(x):
+        for r, n in chunks(48, 24):
+            mid, total = around_whole(src, x, 8 + r, n, width)
+            dst[x, pl.ds(8 + r, n), :] = jacobi(root[x, pl.ds(r, n), :] > 0.0, mid, beta[x, pl.ds(r, n), :], total)
+
+    loop(first, first + planes, body, planes)
+
+
+def coarse_kernel(gx, gy, place, own, zlo, zhi, w2, beta2, root2, e2, beta3, w3, v3, root3, beta4, w4, v4, root4, rsum, csum, rz, cz, v2, w2b, fine3, fine2):
     size_x, width = 2 * gx, 2 * gy
     for ref in (beta3, w3, v3, root3, beta4, w4, v4):
         ref[...] = jnp.zeros_like(ref)
@@ -436,7 +472,7 @@
 
     loop(OFF3, size_x + OFF3, smooth, 4)
     restrict_whole(size_x, OFF3, width, w3, beta3, root3, rsum, csum, rz, cz)
-    t = mm(((rz[...], q3b[...]), (cz[...], q3c[...])))
+    t = mm(((rz[...], pair_lanes(width, 0, gy, 0, 0.5)), (cz[...], pair_lanes(width, 0, gy, 64, 0.125))))
     for x in range(gx):
         t_x = t[x * 32 : (x + 1) * 32]
         root_x, inv_x = roots_of(jnp.where(lane_of(32) < 4 * gy, lane_roll(t_x, 64), 0.0))
@@ -449,7 +485,7 @@
         here, there = there, here
 
     e4 = [here[x + 1, pl.ds(16, 16), :] * inverse(root4[x + 1, pl.ds(8, 16), :]) for x in range(gx)]
-    e4 = mm(((jnp.concatenate(e4, axis=0), u4[...]),))
+    e4 = mm(((jnp.concatenate(e4, axis=0), repeat_lanes(gy, width)),))
     for x in range(gx):
         unfold_rows(fine3, x, 16, e4[x * 16 : (x + 1) * 16])
         for i in range(2):
@@ -459,24 +495,22 @@
     relax_whole(OFF3, size_x, 16, 32, width, v3, w3, beta3, root3, 4)
 
     first3 = 2 * place[0] - 2 + OFF3
-    first2 = 4 * place[0] - 4 + OFF2
     e3 = [w3[first3 + k, pl.ds(28, 24), :] * inverse(root3[first3 + k, pl.ds(20, 24), :]) for k in range(6)]
-    e3 = mm(((jnp.concatenate(e3, axis=0), u3[...]),))
+    e3 = mm(((jnp.concatenate(e3, axis=0), repeat_lanes(width, 2 * width)),))
     for k in range(6):
         unfold_rows(fine2, k, 24, e3[k * 24 : (k + 1) * 24])
     for p in range(12):
-        add = root2[first2 + p, pl.ds(8, 48), :] * fine2[p // 2]
-        w2b[p, pl.ds(16, 48), :] = w2[first2 + p, pl.ds(16, 48), :] + add
+        w2b[p, pl.ds(8, 48), :] = w2[p] + root2[p] * fine2[p // 2]
         for ref in (w2b, v2):
-            ref[p, pl.ds(8, 8), :] = jnp.zeros((8, LANES), F32)
-            ref[p, pl.ds(64, 8), :] = jnp.zeros((8, LANES), F32)
-    relax_whole(1, 10, 8, 48, 2 * width, w2b, v2, beta2, root2, 10, first2)
-    relax_whole(2, 8, 8, 48, 2 * width, v2, w2b, beta2, root2, 8, first2)
+            ref[p, pl.ds(0, 8), :] = jnp.zeros((8, LANES), F32)
+            ref[p, pl.ds(56, 8), :] = jnp.zeros((8, LANES), F32)
+    relax_kept(1, 10, 2 * width, w2b, v2, beta2, root2)
+    relax_kept(2, 8, 2 * width, v2, w2b, beta2, root2)
     for k in range(8):
-        e2[k] = w2b[k + 2, pl.ds(20, 40), :] * inverse(root2[first2 + k + 2, pl.ds(12, 40), :])
-
-
-def up_kernel(gy, place, e2, w1, beta1, root1, w0, beta0, root0, u1, out, w1b, v1, w0b, v0, fine1, fine0, turned):
+        e2[k] = w2b[k + 2, pl.ds(12, 40), :] * inverse(root2[k + 2, pl.ds(4, 40), :])
+
+
+def up_kernel(gy, place, e2, w1, beta1, root1, w0, beta0, root0, out, w1b, v1, w0b, v0, fine1, fine0, turned):
     width = 4 * gy
     source_lane = lax.broadcasted_iota(jnp.int32, (LANES, LANES), 0)
     target_lane = lane_of(LANES)
@@ -509,9 +543,10 @@
     relax1(w1b, v1, 2, 14)
     relax1(v1, w1b, 3, 13)
 
+    u1 = repeat_to_level0()
     for k in range(0, 10, 2):
         e = [w1b[x, pl.ds(12, 72), :] * inverse(root1[x, pl.ds(4, 72), :]) for x in (k + 3, k + 4)]
-        e = mm(((jnp.concatenate(e, axis=0), u1[...]),))
+        e = mm(((jnp.concatenate(e, axis=0), u1),))
         for i in range(2):
             unfold_rows(fine0, k + i, 72, e[i * 72 : (i + 1) * 72])
 
@@ -552,13 +587,15 @@
 def call(kernel, args, outs, scratch, smem=0):
     vmem = pl.BlockSpec(memory_space=pltpu.VMEM)
     scalar = pl.BlockSpec(memory_space=pltpu.SMEM)
+    sizes = [a.shape for a in args] + outs + scratch
+    held = sum(4 * math.prod(s[:-2]) * -(-s[-2] // 8) * 8 * LANES for s in sizes if len(s) > 1)
     return pl.pallas_call(
         kernel,
         out_shape=[jax.ShapeDtypeStruct(s, F32) for s in outs],
         in_specs=[scalar] * smem + [vmem] * (len(args) - smem),
         out_specs=[vmem] * len(outs),
         scratch_shapes=[pltpu.VMEM(s, F32) for s in scratch],
-        compiler_params=pltpu.CompilerParams(vmem_limit_bytes=16 * 1024 * 1024),
+        compiler_params=pltpu.CompilerParams(vmem_limit_bytes=held + 2 * 1024 * 1024),
     )(*args)
 
 
@@ -578,32 +615,36 @@
 
 
 def shards(gx, gy, source, material_ids, material_table, roughness):
-    spread = np.repeat(np.eye(16, dtype=np.float32), 8, axis=1)
-    visc, low, high = call(
+    anywhere = pl.BlockSpec(memory_space=pltpu.HBM)
+    full, low, high = pl.pallas_call(
         prepare_kernel,
-        (material_table, material_ids, spread, source, roughness),
-        [(16, 16, LANES)] + [(5, HX0, 16, LANES)] * 2,
-        [],
-        smem=1,
-    )
+        out_shape=[jax.ShapeDtypeStruct((5, n, 16, LANES), F32) for n in (16, HX0, HX0)],
+        in_specs=[anywhere] * 4,
+        out_specs=[pl.BlockSpec(memory_space=pltpu.VMEM)] * 3,
+        scratch_shapes=[
+            pltpu.SMEM(material_table.shape, F32),
+            pltpu.SMEM(material_ids.shape, jnp.int32),
+            pltpu.VMEM(roughness.shape, F32),
+            pltpu.SemaphoreType.DMA((4,)),
+        ],
+        compiler_params=pltpu.CompilerParams(vmem_limit_bytes=4 * 1024 * 1024),
+    )(material_table, material_ids, source, roughness)
     xlo, xhi = swap(high, low, "gx")
     planes = 16 + 2 * HX0
-    ysend_lo, ysend_hi = call(edge_kernel, (xlo, source, visc, xhi), [(planes, 15, LANES)] * 2, [])
+    ysend_lo, ysend_hi = call(edge_kernel, (xlo, full, xhi), [(planes, 15, LANES)] * 2, [])
     ylo, yhi = swap(ysend_hi, ysend_lo, "gy")
     turned, zsend_lo, zsend_hi = call(
         turn_kernel,
-        (xlo, source, visc, xhi, ylo, yhi),
+        (xlo, full, xhi, ylo, yhi),
         [(planes, 128, LANES)] + [(planes, HZ0, LANES)] * 2,
         [(4, LANES, LANES)],
     )
     zlo, zhi = swap(zsend_hi, zsend_lo, "gz")
 
-    q0b = pair_lanes(Y0, HY0, (0, 1, 2, 3), 8, 0, 0.5)
-    q0c = pair_lanes(Y0, HY0, (0, 3), 8, 32, 0.125)
     depth = 128 + 2 * HZ0
     own1, ysend_lo, ysend_hi, w0, beta0, root0 = call(
         down0_kernel,
-        (turned, zlo, zhi, q0b, q0c),
+        (turned, zlo, zhi),
         [(8, 48, LANES)] + [(8, 24, LANES)] * 2 + [(planes, depth + 16, LANES)] * 2 + [(planes, depth, LANES)],
         [(8, depth, LANES)] * 2 + [(4 * depth, LANES)] * 2 + [(8, LANES, LANES)],
     )
@@ -611,11 +652,9 @@
     low, high = call(join_kernel, (own1, ylo, yhi), [(4, 96, LANES)] * 2, [])
     xlo, xhi = swap(high, low, "gx")
 
-    q1b = pair_lanes(Y1, 4, (0, 1, 2, 3), 4, 0, 0.5)
-    q1c = pair_lanes(Y1, 4, (0, 3), 4, 16, 0.125)
     block, w1, beta1, root1 = call(
         down1_kernel,
-        (own1, ylo, yhi, xlo, xhi, q1b, q1c),
+        (own1, ylo, yhi, xlo, xhi),
         [(gx * gy, 24, LANES), (16, 96, LANES), (16, 96, LANES), (16, 80, LANES)],
         [(4, LANES, LANES)] + [(4, 64, LANES)] * 2 + [(LANES, LANES)] * 2,
     )
@@ -630,23 +669,21 @@
     )
     zlo, zhi = swap(zsend_hi, zsend_lo, "gz")
 
-    q2b = pair_lanes(4 * gy, 0, (0, 1, 2, 3), 2 * gy, 0, 0.5)
-    q2c = pair_lanes(4 * gy, 0, (0, 1, 2, 3), 2 * gy, 64, 0.125)
     own3, zsend_up, zsend_down, w2, beta2, root2 = call(
         functools.partial(down2_kernel, gx, gy),
-        (b2, c2, zlo, zhi, q2b, q2c),
-        [(x3, 32, LANES)] + [(x3, HZ3, LANES)] * 2 + [(x2 + 2 * OFF2, 80, LANES)] * 2 + [(x2 + 2 * OFF2, 64, LANES)],
-        [(x3, 64, LANES)] * 2 + [(x3 * 32, LANES)] * 2,
+        (position("gx").reshape(1), b2, c2, zlo, zhi),
+        [(x3, 32, LANES)] + [(x3, HZ3, LANES)] * 2 + [(12, 48, LANES)] * 3,
+        [(x2 + 2 * OFF2, 80, LANES)] * 2
+        + [(x2 + 2 * OFF2, 64, LANES)]
+        + [(x3, 64, LANES)] * 2
+        + [(x3 * 32, LANES)] * 2,
+        smem=1,
     )
     zlo, zhi = swap(zsend_up, zsend_down, "gz")
 
-    q3b = pair_lanes(2 * gy, 0, (0, 1, 2, 3), gy, 0, 0.5)
-    q3c = pair_lanes(2 * gy, 0, (0, 1, 2, 3), gy, 64, 0.125)
-    u4 = repeat_lanes(gy, 0, 2 * gy, 0)
-    u3 = repeat_lanes(2 * gy, 0, 4 * gy, 0)
     (e2,) = call(
         functools.partial(coarse_kernel, gx, gy),
-        (position("gx").reshape(1), own3, zlo, zhi, w2, beta2, root2, q3b, q3c, u4, u3),
+        (position("gx").reshape(1), own3, zlo, zhi, w2, beta2, root2),
         [(8, 40, LANES)],
         [(x3 + 2 * OFF3, 80, LANES)] * 3
         + [(x3 + 2 * OFF3, 64, LANES)]
@@ -654,15 +691,14 @@
         + [(gx + 2, 32, LANES)]
         + [(gx, 64, LANES)] * 2
         + [(gx * 32, LANES)] * 2
-        + [(12, 80, LANES)] * 2
+        + [(12, 64, LANES)] * 2
         + [(gx, 32, LANES), (6, 48, LANES)],
         smem=1,
     )
 
-    u1 = repeat_lanes(Y1, 4, Y0, HY0)
     (correction,) = call(
         functools.partial(up_kernel, gy),
-        (position("gy").reshape(1), e2, w1, beta1, root1, w0, beta0, root0, u1),
+        (position("gy").reshape(1), e2, w1, beta1, root1, w0, beta0, root0),
         [(4, 16, 16, LANES)],
         [(16, 96, LANES)] * 2
         + [(20, 160, LANES)] * 2

time: 159 us -> 162 us (1.019)
    unnamed x62 -> x44, local copies, waits for them, and re-layouts: 16.7 us -> 17.9 us
    pallas_call x10 -> x9, Pallas kernels: 22.9 us -> 23.8 us  [call(): pl.pallas_call(kernel, out_shape=[jax.ShapeDtypeStruct(s, F32) for s in o...]
where the time goes in v3:
time: 162 us; the launch traced here: 161 us
  starting transfers between devices  42.1 us (26%)
  waiting for transfers between devices  41.6 us (26%)
  blocking collectives  34.5 us (21%)
  Pallas kernels  24.4 us (15%)
  local copies, waits for them, and re-layouts  17.9 us (11%)
    ppermute x7, waiting for transfers between devices, swap(): from_above = lax.ppermute(to_down, axis, [(i + 1, i) for i in range(n - 1)])  34.9 us
    all_to_all x1, blocking collectives, whole_plane(): return lax.all_to_all(block, ('gx', 'gy'), 0, 0, tiled=True)  34.5 us
    ppermute x7, starting transfers between devices, swap(): from_below = lax.ppermute(to_up, axis, [(i, i + 1) for i in range(n - 1)])  29.7 us
    pallas_call x9, Pallas kernels, call(): pl.pallas_call(kernel, out_shape=[jax.ShapeDtypeStruct(s, F32) for s in o...  23.8 us
    unnamed x44, local copies, waits for them, and re-layouts  17.9 us
    ppermute x7, starting transfers between devices, swap(): from_above = lax.ppermute(to_down, axis, [(i + 1, i) for i in range(n - 1)])  12.4 us
    ppermute x7, waiting for transfers between devices, swap(): from_below = lax.ppermute(to_up, axis, [(i, i + 1) for i in range(n - 1)])  6.67 us
  transfers between devices with their start and end apart: 14, of which 14 were waited for; matrix products, arithmetic and copies ran while one was open for 0% of the time, Pallas kernels for 0%

profile of v3, /device:TPU:261, one launch (start us, length us, event | category | flops | bytes accessed | tf_op | source)
XLA Modules:
  0.0 160.7 jit_solution(77118554852972729)
XLA Ops:
  0.0 1.0 copy-done.6
  1.0 0.9 copy-done.19
  4.0 3.1 %collective-permute-start = (f32[5,3,16,128]{3,2,1,0:T(8,128)S(1)}, f32[5,3,16,128]{3,2,1,0:T(8,128)S(1)}, u32[]{:S(2)}, u32[]{:S(2)}) collective-permute-start(f32[5,3,16,128]{3,2,1,0:T(8,128)S(1)} %get-tuple-element.35), channel_id=1, source_target_pairs={{0,128},{128,256},{256,384},{384,512},{512,640},{640,768},{768,896... | collective-permute-start | bytes 368648 | tf_op jit(solution)/shard_map/ppermute | solution.py:604
  7.1 2.2 %collective-permute-start.1 = (f32[5,3,16,128]{3,2,1,0:T(8,128)S(1)}, f32[5,3,16,128]{3,2,1,0:T(8,128)S(1)}, u32[]{:S(2)}, u32[]{:S(2)}) collective-permute-start(f32[5,3,16,128]{3,2,1,0:T(8,128)S(1)} %get-tuple-element.37), channel_id=1, source_target_pairs={{128,0},{256,128},{384,256},{512,384},{640,512},{768,640},{896,768... | collective-permute-start | bytes 368648 | tf_op jit(solution)/shard_map/ppermute | solution.py:605
  9.3 0.8 collective-permute-done.xlo
  10.1 4.1 %collective-permute-done.1.xhi = f32[5,3,16,128]{3,2,1,0:T(8,128)S(1)} collective-permute-done((f32[5,3,16,128]{3,2,1,0:T(8,128)S(1)}, f32[5,3,16,128]{3,2,1,0:T(8,128)S(1)}, u32[]{:S(2)}, u32[]{:S(2)}) %collective-permute-start.1) | collective-permute-done | bytes 122912 | tf_op jit(solution)/shard_map/ppermute | solution.py:605
  14.2 3.3 %collective-permute-start.2 = (f32[22,15,128]{2,1,0:T(8,128)S(1)}, f32[22,15,128]{2,1,0:T(8,128)S(1)}, u32[]{:S(2)}, u32[]{:S(2)}) collective-permute-start(f32[22,15,128]{2,1,0:T(8,128)S(1)} %get-tuple-element.38), channel_id=1, source_target_pairs={{0,16},{16,32},{32,48},{48,64},{64,80},{80,96},{96,112},{1,17},{17... | collective-permute-start | bytes 506888 | tf_op jit(solution)/shard_map/ppermute | solution.py:604
  17.5 1.3 collective-permute-start.3
  18.8 1.1 collective-permute-done.2.ylo
  20.0 3.8 %collective-permute-done.3.yhi = f32[22,15,128]{2,1,0:T(8,128)S(1)} collective-permute-done((f32[22,15,128]{2,1,0:T(8,128)S(1)}, f32[22,15,128]{2,1,0:T(8,128)S(1)}, u32[]{:S(2)}, u32[]{:S(2)}) %collective-permute-start.3) | collective-permute-done | bytes 168992 | tf_op jit(solution)/shard_map/ppermute | solution.py:605
  24.5 7.8 %collective-permute-start.4 = (f32[22,16,128]{2,1,0:T(8,128)S(1)}, f32[22,16,128]{2,1,0:T(8,128)S(1)}, u32[]{:S(2)}, u32[]{:S(2)}) collective-permute-start(f32[22,16,128]{2,1,0:T(8,128)S(1)} %get-tuple-element.41), channel_id=1, source_target_pairs={{0,1},{1,2},{2,3},{3,4},{4,5},{5,6},{6,7},{7,8},{8,9},{9,10},{10,1... | collective-permute-start | bytes 540680 | tf_op jit(solution)/shard_map/ppermute | solution.py:604
  32.2 1.9 %collective-permute-start.5 = (f32[22,16,128]{2,1,0:T(8,128)S(1)}, f32[22,16,128]{2,1,0:T(8,128)S(1)}, u32[]{:S(2)}, u32[]{:S(2)}) collective-permute-start(f32[22,16,128]{2,1,0:T(8,128)S(1)} %get-tuple-element.42), channel_id=1, source_target_pairs={{1,0},{2,1},{3,2},{4,3},{5,4},{6,5},{7,6},{8,7},{9,8},{10,9},{11,1... | collective-permute-start | bytes 540680 | tf_op jit(solution)/shard_map/ppermute | solution.py:605
  34.7 4.4 %collective-permute-done.5.zhi = f32[22,16,128]{2,1,0:T(8,128)S(1)} collective-permute-done((f32[22,16,128]{2,1,0:T(8,128)S(1)}, f32[22,16,128]{2,1,0:T(8,128)S(1)}, u32[]{:S(2)}, u32[]{:S(2)}) %collective-permute-start.5) | collective-permute-done | bytes 180256 | tf_op jit(solution)/shard_map/ppermute | solution.py:605
  39.1 5.3 %shard_map.49 = (f32[8,48,128]{2,1,0:T(8,128)S(1)}, f32[8,24,128]{2,1,0:T(8,128)S(1)}, f32[8,24,128]{2,1,0:T(8,128)S(1)}, f32[22,176,128]{2,1,0:T(8,128)S(1)}, f...) custom-call(f32[22,128,128]{2,1,0:T(8,128)S(1)} %get-tuple-element.40.turned, ...), custom_call_target="tpu_custom_call" | custom-call | tf_op jit(solution)/shard_map/pallas_call | solution.py:592
  44.4 1.2 copy-done.2
  45.6 3.3 %collective-permute-start.6 = (f32[8,24,128]{2,1,0:T(8,128)S(1)}, f32[8,24,128]{2,1,0:T(8,128)S(1)}, u32[]{:S(2)}, u32[]{:S(2)}) collective-permute-start(f32[8,24,128]{2,1,0:T(8,128)S(1)} %get-tuple-element.44), channel_id=1, source_target_pairs={{0,16},{16,32},{32,48},{48,64},{64,80},{80,96},{96,112},{1,17},{17... | collective-permute-start | bytes 294920 | tf_op jit(solution)/shard_map/ppermute | solution.py:604
  48.9 1.3 collective-permute-start.7
  50.5 4.6 %collective-permute-done.7.yhi = f32[8,24,128]{2,1,0:T(8,128)S(1)} collective-permute-done((f32[8,24,128]{2,1,0:T(8,128)S(1)}, f32[8,24,128]{2,1,0:T(8,128)S(1)}, u32[]{:S(2)}, u32[]{:S(2)}) %collective-permute-start.7) | collective-permute-done | bytes 98336 | tf_op jit(solution)/shard_map/ppermute | solution.py:605
  55.2 4.7 %collective-permute-start.8 = (f32[4,96,128]{2,1,0:T(8,128)S(1)}, f32[4,96,128]{2,1,0:T(8,128)S(1)}, u32[]{:S(2)}, u32[]{:S(2)}) collective-permute-start(f32[4,96,128]{2,1,0:T(8,128)S(1)} %get-tuple-element.46), channel_id=1, source_target_pairs={{0,128},{128,256},{256,384},{384,512},{512,640},{640,768},{768,896... | collective-permute-start | bytes 589832 | tf_op jit(solution)/shard_map/ppermute | solution.py:604
  59.8 1.9 %collective-permute-start.9 = (f32[4,96,128]{2,1,0:T(8,128)S(1)}, f32[4,96,128]{2,1,0:T(8,128)S(1)}, u32[]{:S(2)}, u32[]{:S(2)}) collective-permute-start(f32[4,96,128]{2,1,0:T(8,128)S(1)} %get-tuple-element.47), channel_id=1, source_target_pairs={{128,0},{256,128},{384,256},{512,384},{640,512},{768,640},{896,768... | collective-permute-start | bytes 589832 | tf_op jit(solution)/shard_map/ppermute | solution.py:605
  61.8 1.3 collective-permute-done.8.xlo
  63.1 4.1 %collective-permute-done.9.xhi = f32[4,96,128]{2,1,0:T(8,128)S(1)} collective-permute-done((f32[4,96,128]{2,1,0:T(8,128)S(1)}, f32[4,96,128]{2,1,0:T(8,128)S(1)}, u32[]{:S(2)}, u32[]{:S(2)}) %collective-permute-start.9) | collective-permute-done | bytes 196640 | tf_op jit(solution)/shard_map/ppermute | solution.py:605
  67.2 1.6 shard_map.51
  68.8 34.5 %all_to_all.5.got = f32[64,24,128]{2,1,0:T(8,128)S(1)} all-to-all(f32[64,24,128]{2,1,0:T(8,128)S(1)} %get-tuple-element.48), channel_id=1, replica_groups=mesh['gx'=8,'gy'=8,'gz'=16] {'gx','gy'}, dimensions={0} | all-to-all | bytes 1572864 | tf_op jit(solution)/shard_map/all_to_all | solution.py:610
  103.3 1.9 %shard_map.52 = (f32[32,32,128]{2,1,0:T(8,128)S(1)}, f32[32,32,128]{2,1,0:T(8,128)S(1)}, f32[32,16,128]{2,1,0:T(8,128)}, f32[32,16,128]{2,1,0:T(8,128)}) custom-call(f32[64,24,128]{2,1,0:T(8,128)S(1)} %all_to_all.5.got), custom_call_target="tpu_custom_call" | custom-call | tf_op jit(solution)/shard_map/pallas_call | solution.py:592
  105.1 0.8 copy-done.7
  105.9 0.8 copy-done.9
  106.7 3.2 %collective-permute-start.10 = (f32[32,16,128]{2,1,0:T(8,128)}, f32[32,16,128]{2,1,0:T(8,128)}, u32[]{:S(2)}, u32[]{:S(2)}) collective-permute-start(f32[32,16,128]{2,1,0:T(8,128)} %get-tuple-element.51), channel_id=1, source_target_pairs={{0,1},{1,2},{2,3},{3,4},{4,5},{5,6},{6,7},{7,8},{8,9},{9,10},{10,1... | collective-permute-start | bytes 786440 | tf_op jit(solution)/shard_map/ppermute | solution.py:604
  110.0 1.9 %collective-permute-start.11 = (f32[32,16,128]{2,1,0:T(8,128)}, f32[32,16,128]{2,1,0:T(8,128)}, u32[]{:S(2)}, u32[]{:S(2)}) collective-permute-start(f32[32,16,128]{2,1,0:T(8,128)} %get-tuple-element.52), channel_id=1, source_target_pairs={{1,0},{2,1},{3,2},{4,3},{5,4},{6,5},{7,6},{8,7},{9,8},{10,9},{11,1... | collective-permute-start | bytes 786440 | tf_op jit(solution)/shard_map/ppermute | solution.py:605
  111.9 1.7 %collective-permute-done.10.zlo = f32[32,16,128]{2,1,0:T(8,128)} collective-permute-done((f32[32,16,128]{2,1,0:T(8,128)}, f32[32,16,128]{2,1,0:T(8,128)}, u32[]{:S(2)}, u32[]{:S(2)}) %collective-permute-start.10) | collective-permute-done | bytes 262176 | tf_op jit(solution)/shard_map/ppermute | solution.py:604
  113.6 5.3 %collective-permute-done.11.zhi = f32[32,16,128]{2,1,0:T(8,128)} collective-permute-done((f32[32,16,128]{2,1,0:T(8,128)}, f32[32,16,128]{2,1,0:T(8,128)}, u32[]{:S(2)}, u32[]{:S(2)}) %collective-permute-start.11) | collective-permute-done | bytes 262176 | tf_op jit(solution)/shard_map/ppermute | solution.py:605
  118.9 1.0 copy-done.8
  120.0 1.0 copy-done.10
  121.0 5.3 %shard_map.53 = (f32[16,32,128]{2,1,0:T(8,128)S(1)}, f32[16,20,128]{2,1,0:T(8,128)}, f32[16,20,128]{2,1,0:T(8,128)}, f32[12,48,128]{2,1,0:T(8,128)S(1)}, f32[12,...) custom-call(s32[1]{0:T(128)} %bitcast.1.place, f32[32,32,128]{2,1,0:T(8,128)S(1)} %copy-done.8, ...), custom_call_target="tpu_custom_call" | custom-call | tf_op jit(solution)/shard_map/pallas_call | solution.py:592
  126.3 0.7 copy-done.11
  127.7 0.7 copy-done.15
  129.1 4.2 %collective-permute-start.12 = (f32[16,20,128]{2,1,0:T(8,128)}, f32[16,20,128]{2,1,0:T(8,128)}, u32[]{:S(2)}, u32[]{:S(2)}) collective-permute-start(f32[16,20,128]{2,1,0:T(8,128)} %get-tuple-element.54), channel_id=1, source_target_pairs={{0,1},{1,2},{2,3},{3,4},{4,5},{5,6},{6,7},{7,8},{8,9},{9,10},{10,1... | collective-permute-start | bytes 491528 | tf_op jit(solution)/shard_map/ppermute | solution.py:604
  133.4 1.9 %collective-permute-start.13 = (f32[16,20,128]{2,1,0:T(8,128)}, f32[16,20,128]{2,1,0:T(8,128)}, u32[]{:S(2)}, u32[]{:S(2)}) collective-permute-start(f32[16,20,128]{2,1,0:T(8,128)} %get-tuple-element.55), channel_id=1, source_target_pairs={{1,0},{2,1},{3,2},{4,3},{5,4},{6,5},{7,6},{8,7},{9,8},{10,9},{11,1... | collective-permute-start | bytes 491528 | tf_op jit(solution)/shard_map/ppermute | solution.py:605
  135.3 1.0 collective-permute-done.12.zlo
  136.3 8.6 %collective-permute-done.13.zhi = f32[16,20,128]{2,1,0:T(8,128)} collective-permute-done((f32[16,20,128]{2,1,0:T(8,128)}, f32[16,20,128]{2,1,0:T(8,128)}, u32[]{:S(2)}, u32[]{:S(2)}) %collective-permute-start.13) | collective-permute-done | bytes 163872 | tf_op jit(solution)/shard_map/ppermute | solution.py:605
  144.9 1.0 copy-done.12
  145.9 1.0 copy-done.14
  146.8 1.0 copy-done.16
  147.8 0.9 copy-done.18
  148.7 5.1 %shard_map.54.e2 = f32[8,40,128]{2,1,0:T(8,128)S(1)} custom-call(s32[1]{0:T(128)} %bitcast.1.place, f32[16,32,128]{2,1,0:T(8,128)S(1)} %copy-done.18, f32[16,20,128]{2,1,0:T(8,128)} %collective-permute-done.12.zlo, f32[16,20,128]{2,1,0:T(8,128)} %collective-permute-done.13.zhi, f32[12,48,128]{2,1,0:T(8,128)S(1)} %copy-done.12, ...), custom_call_target="tpu_custom_call" | custom-call | tf_op jit(solution)/shard_map/pallas_call | solution.py:592
  153.8 1.5 copy-done.1
  155.4 1.5 copy-done.3
  156.8 3.9 %shard_map.55 = f32[4,16,16,128]{3,2,1,0:T(8,128)} custom-call(s32[1]{0:T(128)} %bitcast.place, f32[8,40,128]{2,1,0:T(8,128)S(1)} %shard_map.54.e2, f32[16,96,128]{2,1,0:T(8,128)S(1)} %get-tuple-element.59.w1, f32[16,96,128]{2,1,0:T(8,128)S(1)} %get-tuple-element.60.beta1, f32[16,80,128]{2,1,0:T(8,128)S(1)} %copy-done.5, ...), custom_call_target="tpu_custom_call" | custom-call | tf_op jit(solution)/shard_map/pallas_call | solution.py:592
  (35 shorter events, 5.0 us)
Async XLA Ops:
  0.0 1.0 copy-start.6
  1.0 0.9 copy-start.19
  1.9 0.7 copy-start.20
  2.6 0.7 copy-start.21
  4.0 6.1 %collective-permute-start = (f32[5,3,16,128]{3,2,1,0:T(8,128)S(1)}, f32[5,3,16,128]{3,2,1,0:T(8,128)S(1)}, u32[]{:S(2)}, u32[]{:S(2)}) collective-permute-start(f32[5,3,16,128]{3,2,1,0:T(8,128)S(1)} %get-tuple-element.35), channel_id=1, source_target_pairs={{0,128},{128,256},{256,384},{384,512},{512,640},{640,768},{768,896... | collective-permute-start | bytes 368648 | tf_op jit(solution)/shard_map/ppermute | solution.py:604
  7.1 7.1 %collective-permute-start.1 = (f32[5,3,16,128]{3,2,1,0:T(8,128)S(1)}, f32[5,3,16,128]{3,2,1,0:T(8,128)S(1)}, u32[]{:S(2)}, u32[]{:S(2)}) collective-permute-start(f32[5,3,16,128]{3,2,1,0:T(8,128)S(1)} %get-tuple-element.37), channel_id=1, source_target_pairs={{128,0},{256,128},{384,256},{512,384},{640,512},{768,640},{896,768... | collective-permute-start | bytes 368648 | tf_op jit(solution)/shard_map/ppermute | solution.py:605
  14.2 5.7 %collective-permute-start.2 = (f32[22,15,128]{2,1,0:T(8,128)S(1)}, f32[22,15,128]{2,1,0:T(8,128)S(1)}, u32[]{:S(2)}, u32[]{:S(2)}) collective-permute-start(f32[22,15,128]{2,1,0:T(8,128)S(1)} %get-tuple-element.38), channel_id=1, source_target_pairs={{0,16},{16,32},{32,48},{48,64},{64,80},{80,96},{96,112},{1,17},{17... | collective-permute-start | bytes 506888 | tf_op jit(solution)/shard_map/ppermute | solution.py:604
  17.5 6.2 %collective-permute-start.3 = (f32[22,15,128]{2,1,0:T(8,128)S(1)}, f32[22,15,128]{2,1,0:T(8,128)S(1)}, u32[]{:S(2)}, u32[]{:S(2)}) collective-permute-start(f32[22,15,128]{2,1,0:T(8,128)S(1)} %get-tuple-element.39), channel_id=1, source_target_pairs={{16,0},{32,16},{48,32},{64,48},{80,64},{96,80},{112,96},{17,1},{33... | collective-permute-start | bytes 506888 | tf_op jit(solution)/shard_map/ppermute | solution.py:605
  24.5 10.2 %collective-permute-start.4 = (f32[22,16,128]{2,1,0:T(8,128)S(1)}, f32[22,16,128]{2,1,0:T(8,128)S(1)}, u32[]{:S(2)}, u32[]{:S(2)}) collective-permute-start(f32[22,16,128]{2,1,0:T(8,128)S(1)} %get-tuple-element.41), channel_id=1, source_target_pairs={{0,1},{1,2},{2,3},{3,4},{4,5},{5,6},{6,7},{7,8},{8,9},{9,10},{10,1... | collective-permute-start | bytes 540680 | tf_op jit(solution)/shard_map/ppermute | solution.py:604
  32.2 6.8 %collective-permute-start.5 = (f32[22,16,128]{2,1,0:T(8,128)S(1)}, f32[22,16,128]{2,1,0:T(8,128)S(1)}, u32[]{:S(2)}, u32[]{:S(2)}) collective-permute-start(f32[22,16,128]{2,1,0:T(8,128)S(1)} %get-tuple-element.42), channel_id=1, source_target_pairs={{1,0},{2,1},{3,2},{4,3},{5,4},{6,5},{7,6},{8,7},{9,8},{10,9},{11,1... | collective-permute-start | bytes 540680 | tf_op jit(solution)/shard_map/ppermute | solution.py:605
  44.4 1.2 copy-start.2
  45.6 59.5 %copy-start = (f32[22,176,128]{2,1,0:T(8,128)}, f32[22,176,128]{2,1,0:T(8,128)S(1)}, u32[]{:S(2)}) copy-start(f32[22,176,128]{2,1,0:T(8,128)S(1)} %get-tuple-element.63.beta0) | copy-start | bytes 5947396
  45.6 4.9 %collective-permute-start.6 = (f32[8,24,128]{2,1,0:T(8,128)S(1)}, f32[8,24,128]{2,1,0:T(8,128)S(1)}, u32[]{:S(2)}, u32[]{:S(2)}) collective-permute-start(f32[8,24,128]{2,1,0:T(8,128)S(1)} %get-tuple-element.44), channel_id=1, source_target_pairs={{0,16},{16,32},{32,48},{48,64},{64,80},{80,96},{96,112},{1,17},{17... | collective-permute-start | bytes 294920 | tf_op jit(solution)/shard_map/ppermute | solution.py:604
  48.9 6.2 %collective-permute-start.7 = (f32[8,24,128]{2,1,0:T(8,128)S(1)}, f32[8,24,128]{2,1,0:T(8,128)S(1)}, u32[]{:S(2)}, u32[]{:S(2)}) collective-permute-start(f32[8,24,128]{2,1,0:T(8,128)S(1)} %get-tuple-element.45), channel_id=1, source_target_pairs={{16,0},{32,16},{48,32},{64,48},{80,64},{96,80},{112,96},{17,1},{33... | collective-permute-start | bytes 294920 | tf_op jit(solution)/shard_map/ppermute | solution.py:605
  55.2 7.9 %collective-permute-start.8 = (f32[4,96,128]{2,1,0:T(8,128)S(1)}, f32[4,96,128]{2,1,0:T(8,128)S(1)}, u32[]{:S(2)}, u32[]{:S(2)}) collective-permute-start(f32[4,96,128]{2,1,0:T(8,128)S(1)} %get-tuple-element.46), channel_id=1, source_target_pairs={{0,128},{128,256},{256,384},{384,512},{512,640},{640,768},{768,896... | collective-permute-start | bytes 589832 | tf_op jit(solution)/shard_map/ppermute | solution.py:604
  59.8 7.4 %collective-permute-start.9 = (f32[4,96,128]{2,1,0:T(8,128)S(1)}, f32[4,96,128]{2,1,0:T(8,128)S(1)}, u32[]{:S(2)}, u32[]{:S(2)}) collective-permute-start(f32[4,96,128]{2,1,0:T(8,128)S(1)} %get-tuple-element.47), channel_id=1, source_target_pairs={{128,0},{256,128},{384,256},{512,384},{640,512},{768,640},{896,768... | collective-permute-start | bytes 589832 | tf_op jit(solution)/shard_map/ppermute | solution.py:605
  68.8 37.9 %copy-start.4 = (f32[16,80,128]{2,1,0:T(8,128)}, f32[16,80,128]{2,1,0:T(8,128)S(1)}, u32[]{:S(2)}) copy-start(f32[16,80,128]{2,1,0:T(8,128)S(1)} %get-tuple-element.61.root1) | copy-start | bytes 1966084
  105.1 0.8 copy-start.7
  105.9 0.8 copy-start.9
  106.7 6.9 %collective-permute-start.10 = (f32[32,16,128]{2,1,0:T(8,128)}, f32[32,16,128]{2,1,0:T(8,128)}, u32[]{:S(2)}, u32[]{:S(2)}) collective-permute-start(f32[32,16,128]{2,1,0:T(8,128)} %get-tuple-element.51), channel_id=1, source_target_pairs={{0,1},{1,2},{2,3},{3,4},{4,5},{5,6},{6,7},{7,8},{8,9},{9,10},{10,1... | collective-permute-start | bytes 786440 | tf_op jit(solution)/shard_map/ppermute | solution.py:604
  110.0 8.9 %collective-permute-start.11 = (f32[32,16,128]{2,1,0:T(8,128)}, f32[32,16,128]{2,1,0:T(8,128)}, u32[]{:S(2)}, u32[]{:S(2)}) collective-permute-start(f32[32,16,128]{2,1,0:T(8,128)} %get-tuple-element.52), channel_id=1, source_target_pairs={{1,0},{2,1},{3,2},{4,3},{5,4},{6,5},{7,6},{8,7},{9,8},{10,9},{11,1... | collective-permute-start | bytes 786440 | tf_op jit(solution)/shard_map/ppermute | solution.py:605
  118.9 1.0 copy-start.8
  120.0 1.0 copy-start.10
  126.3 0.7 copy-start.11
  127.0 0.7 copy-start.13
  127.7 0.7 copy-start.15
  128.4 0.7 copy-start.17
  129.1 7.2 %collective-permute-start.12 = (f32[16,20,128]{2,1,0:T(8,128)}, f32[16,20,128]{2,1,0:T(8,128)}, u32[]{:S(2)}, u32[]{:S(2)}) collective-permute-start(f32[16,20,128]{2,1,0:T(8,128)} %get-tuple-element.54), channel_id=1, source_target_pairs={{0,1},{1,2},{2,3},{3,4},{4,5},{5,6},{6,7},{7,8},{8,9},{9,10},{10,1... | collective-permute-start | bytes 491528 | tf_op jit(solution)/shard_map/ppermute | solution.py:604
  133.4 11.5 %collective-permute-start.13 = (f32[16,20,128]{2,1,0:T(8,128)}, f32[16,20,128]{2,1,0:T(8,128)}, u32[]{:S(2)}, u32[]{:S(2)}) collective-permute-start(f32[16,20,128]{2,1,0:T(8,128)} %get-tuple-element.55), channel_id=1, source_target_pairs={{1,0},{2,1},{3,2},{4,3},{5,4},{6,5},{7,6},{8,7},{9,8},{10,9},{11,1... | collective-permute-start | bytes 491528 | tf_op jit(solution)/shard_map/ppermute | solution.py:605
  135.3 18.5 %copy-start.5 = (f32[16,80,128]{2,1,0:T(8,128)S(1)}, f32[16,80,128]{2,1,0:T(8,128)}, u32[]{:S(2)}) copy-start(f32[16,80,128]{2,1,0:T(8,128)} %copy-done.4) | copy-start | bytes 1966084
  144.9 1.0 copy-start.12
  145.8 1.0 copy-start.14
  146.8 1.0 copy-start.16
  147.8 0.9 copy-start.18
  153.8 1.6 copy-start.1
  155.4 1.5 copy-start.3

commit v4 on v3

--- a/solution.py
+++ b/solution.py
@@ -360,7 +360,7 @@
     loop(0, gx // 2, body)
 
 
-def down2_kernel(gx, gy, place, b, c, zlo, zhi, out, zup, zdown, w_kept, beta_kept, root_kept, w, beta, root, rsum, csum, rz, cz):
+def down2_kernel(gx, gy, b, c, zlo, zhi, out, zup, zdown, w_kept, beta_kept, root_kept, w, beta, root, rsum, csum, rz, cz):
     size_x, width = 4 * gx, 4 * gy
 
     def prepare(x, row, t, tc):
@@ -398,7 +398,7 @@
     restrict_whole(size_x, OFF2, width, w, beta, root, rsum, csum, rz, cz)
     qb = pair_lanes(width, 0, width // 2, 0, 0.5)
     qc = pair_lanes(width, 0, width // 2, 64, 0.125)
-    first = 4 * place[0] - 4 + OFF2
+    first = 4 * position("gx") - 4 + OFF2
     for p in range(12):
         w_kept[p] = w[first + p, pl.ds(16, 48), :]
         beta_kept[p] = beta[first + p, pl.ds(16, 48), :]
@@ -447,7 +447,7 @@
     loop(first, first + planes, body, planes)
 
 
-def coarse_kernel(gx, gy, place, own, zlo, zhi, w2, beta2, root2, e2, beta3, w3, v3, root3, beta4, w4, v4, root4, rsum, csum, rz, cz, v2, w2b, fine3, fine2):
+def coarse_kernel(gx, gy, own, zlo, zhi, w2, beta2, root2, e2, beta3, w3, v3, root3, beta4, w4, v4, root4, rsum, csum, rz, cz, v2, w2b, fine3, fine2):
     size_x, width = 2 * gx, 2 * gy
     for ref in (beta3, w3, v3, root3, beta4, w4, v4):
         ref[...] = jnp.zeros_like(ref)
@@ -494,7 +494,7 @@
     relax_whole(OFF3, size_x, 16, 32, width, w3, v3, beta3, root3, 4)
     relax_whole(OFF3, size_x, 16, 32, width, v3, w3, beta3, root3, 4)
 
-    first3 = 2 * place[0] - 2 + OFF3
+    first3 = 2 * position("gx") - 2 + OFF3
     e3 = [w3[first3 + k, pl.ds(28, 24), :] * inverse(root3[first3 + k, pl.ds(20, 24), :]) for k in range(6)]
     e3 = mm(((jnp.concatenate(e3, axis=0), repeat_lanes(width, 2 * width)),))
     for k in range(6):
@@ -510,11 +510,11 @@
         e2[k] = w2b[k + 2, pl.ds(12, 40), :] * inverse(root2[k + 2, pl.ds(4, 40), :])
 
 
-def up_kernel(gy, place, e2, w1, beta1, root1, w0, beta0, root0, out, w1b, v1, w0b, v0, fine1, fine0, turned):
+def up_kernel(gy, e2, w1, beta1, root1, w0, beta0, root0, out, w1b, v1, w0b, v0, fine1, fine0, turned):
     width = 4 * gy
     source_lane = lax.broadcasted_iota(jnp.int32, (LANES, LANES), 0)
     target_lane = lane_of(LANES)
-    wanted_y = 4 * place[0] - 2 + ((target_lane & (Y1 - 1)) >> 1)
+    wanted_y = 4 * position("gy") - 2 + ((target_lane & (Y1 - 1)) >> 1)
     wanted = (target_lane >> 4) * width + wanted_y
     valid = (source_lane == wanted) & (wanted_y >= 0) & (wanted_y < width) & (target_lane < 4 * Y1)
     u2 = jnp.where(valid, 1.0, 0.0).astype(jnp.bfloat16)
@@ -584,15 +584,14 @@
     loop(0, 4, last0)
 
 
-def call(kernel, args, outs, scratch, smem=0):
+def call(kernel, args, outs, scratch):
     vmem = pl.BlockSpec(memory_space=pltpu.VMEM)
-    scalar = pl.BlockSpec(memory_space=pltpu.SMEM)
     sizes = [a.shape for a in args] + outs + scratch
     held = sum(4 * math.prod(s[:-2]) * -(-s[-2] // 8) * 8 * LANES for s in sizes if len(s) > 1)
     return pl.pallas_call(
         kernel,
         out_shape=[jax.ShapeDtypeStruct(s, F32) for s in outs],
-        in_specs=[scalar] * smem + [vmem] * (len(args) - smem),
+        in_specs=[vmem] * len(args),
         out_specs=[vmem] * len(outs),
         scratch_shapes=[pltpu.VMEM(s, F32) for s in scratch],
         compiler_params=pltpu.CompilerParams(vmem_limit_bytes=held + 2 * 1024 * 1024),
@@ -671,19 +670,18 @@
 
     own3, zsend_up, zsend_down, w2, beta2, root2 = call(
         functools.partial(down2_kernel, gx, gy),
-        (position("gx").reshape(1), b2, c2, zlo, zhi),
+        (b2, c2, zlo, zhi),
         [(x3, 32, LANES)] + [(x3, HZ3, LANES)] * 2 + [(12, 48, LANES)] * 3,
         [(x2 + 2 * OFF2, 80, LANES)] * 2
         + [(x2 + 2 * OFF2, 64, LANES)]
         + [(x3, 64, LANES)] * 2
         + [(x3 * 32, LANES)] * 2,
-        smem=1,
     )
     zlo, zhi = swap(zsend_up, zsend_down, "gz")
 
     (e2,) = call(
         functools.partial(coarse_kernel, gx, gy),
-        (position("gx").reshape(1), own3, zlo, zhi, w2, beta2, root2),
+        (own3, zlo, zhi, w2, beta2, root2),
         [(8, 40, LANES)],
         [(x3 + 2 * OFF3, 80, LANES)] * 3
         + [(x3 + 2 * OFF3, 64, LANES)]
@@ -693,17 +691,15 @@
         + [(gx * 32, LANES)] * 2
         + [(12, 64, LANES)] * 2
         + [(gx, 32, LANES), (6, 48, LANES)],
-        smem=1,
     )
 
     (correction,) = call(
         functools.partial(up_kernel, gy),
-        (position("gy").reshape(1), e2, w1, beta1, root1, w0, beta0, root0),
+        (e2, w1, beta1, root1, w0, beta0, root0),
         [(4, 16, 16, LANES)],
         [(16, 96, LANES)] * 2
         + [(20, 160, LANES)] * 2
         + [(8, 80, LANES), (10, 144, LANES), (4, LANES, LANES)],
-        smem=1,
     )
     return correction
 

time: 162 us -> 142 us (0.88)
  local copies, waits for them, and re-layouts: 17.9 us -> 3.28 us
  Pallas kernels: 24.4 us -> 20.8 us
    unnamed x44 -> x8, local copies, waits for them, and re-layouts: 17.9 us -> 3.28 us
    pallas_call x9, Pallas kernels: 23.8 us -> 20.1 us  [call(): pl.pallas_call(kernel, out_shape=[jax.ShapeDtypeStruct(s, F32) for s in o...]
where the time goes in v4:
time: 142 us
  starting transfers between devices  42.1 us (30%)
  waiting for transfers between devices  41 us (29%)
  blocking collectives  34.5 us (24%)
  Pallas kernels  20.8 us (15%)
  local copies, waits for them, and re-layouts  3.28 us (2%)
    ppermute x7, waiting for transfers between devices, swap(): from_above = lax.ppermute(to_down, axis, [(i + 1, i) for i in range(n - 1)])  34.9 us
    all_to_all x1, blocking collectives, whole_plane(): return lax.all_to_all(block, ('gx', 'gy'), 0, 0, tiled=True)  34.5 us
    ppermute x7, starting transfers between devices, swap(): from_below = lax.ppermute(to_up, axis, [(i, i + 1) for i in range(n - 1)])  29.7 us
    pallas_call x9, Pallas kernels, call(): pl.pallas_call(kernel, out_shape=[jax.ShapeDtypeStruct(s, F32) for s in o...  20.1 us
    ppermute x7, starting transfers between devices, swap(): from_above = lax.ppermute(to_down, axis, [(i + 1, i) for i in range(n - 1)])  12.4 us
    ppermute x7, waiting for transfers between devices, swap(): from_below = lax.ppermute(to_up, axis, [(i, i + 1) for i in range(n - 1)])  6.07 us
    unnamed x8, local copies, waits for them, and re-layouts  3.28 us
  transfers between devices with their start and end apart: 14, of which 14 were waited for; matrix products, arithmetic and copies ran while one was open for 0% of the time, Pallas kernels for 0%

profile of v4, /device:TPU:261, one launch (start us, length us, event | category | flops | bytes accessed | tf_op | source)
XLA Modules:
  0.0 141.8 jit_solution(4909012476822636089)
XLA Ops:
  0.0 0.0 copy-start
  0.0 1.0 copy-done
  1.0 0.0 copy-start.1
  1.0 0.9 copy-done.1
  1.9 0.0 copy-start.2
  1.9 0.7 copy-done.2
  2.6 0.0 copy-start.3
  2.6 0.7 copy-done.3
  3.3 0.7 shard_map.46
  4.0 3.1 %collective-permute-start = (f32[5,3,16,128]{3,2,1,0:T(8,128)S(1)}, f32[5,3,16,128]{3,2,1,0:T(8,128)S(1)}, u32[]{:S(2)}, u32[]{:S(2)}) collective-permute-start(f32[5,3,16,128]{3,2,1,0:T(8,128)S(1)} %get-tuple-element.35), channel_id=1, source_target_pairs={{0,128},{128,256},{256,384},{384,512},{512,640},{640,768},{768,896... | collective-permute-start | bytes 368648 | tf_op jit(solution)/shard_map/ppermute | solution.py:603
  7.1 2.2 %collective-permute-start.1 = (f32[5,3,16,128]{3,2,1,0:T(8,128)S(1)}, f32[5,3,16,128]{3,2,1,0:T(8,128)S(1)}, u32[]{:S(2)}, u32[]{:S(2)}) collective-permute-start(f32[5,3,16,128]{3,2,1,0:T(8,128)S(1)} %get-tuple-element.37), channel_id=1, source_target_pairs={{128,0},{256,128},{384,256},{512,384},{640,512},{768,640},{896,768... | collective-permute-start | bytes 368648 | tf_op jit(solution)/shard_map/ppermute | solution.py:604
  9.3 0.8 collective-permute-done.xlo
  10.1 4.1 %collective-permute-done.1.xhi = f32[5,3,16,128]{3,2,1,0:T(8,128)S(1)} collective-permute-done((f32[5,3,16,128]{3,2,1,0:T(8,128)S(1)}, f32[5,3,16,128]{3,2,1,0:T(8,128)S(1)}, u32[]{:S(2)}, u32[]{:S(2)}) %collective-permute-start.1) | collective-permute-done | bytes 122912 | tf_op jit(solution)/shard_map/ppermute | solution.py:604
  14.1 0.1 shard_map.47
  14.2 3.3 %collective-permute-start.2 = (f32[22,15,128]{2,1,0:T(8,128)S(1)}, f32[22,15,128]{2,1,0:T(8,128)S(1)}, u32[]{:S(2)}, u32[]{:S(2)}) collective-permute-start(f32[22,15,128]{2,1,0:T(8,128)S(1)} %get-tuple-element.38), channel_id=1, source_target_pairs={{0,16},{16,32},{32,48},{48,64},{64,80},{80,96},{96,112},{1,17},{17... | collective-permute-start | bytes 506888 | tf_op jit(solution)/shard_map/ppermute | solution.py:603
  17.5 1.3 collective-permute-start.3
  18.8 1.1 collective-permute-done.2.ylo
  20.0 3.8 %collective-permute-done.3.yhi = f32[22,15,128]{2,1,0:T(8,128)S(1)} collective-permute-done((f32[22,15,128]{2,1,0:T(8,128)S(1)}, f32[22,15,128]{2,1,0:T(8,128)S(1)}, u32[]{:S(2)}, u32[]{:S(2)}) %collective-permute-start.3) | collective-permute-done | bytes 168992 | tf_op jit(solution)/shard_map/ppermute | solution.py:604
  23.8 0.7 shard_map.48
  24.5 7.8 %collective-permute-start.4 = (f32[22,16,128]{2,1,0:T(8,128)S(1)}, f32[22,16,128]{2,1,0:T(8,128)S(1)}, u32[]{:S(2)}, u32[]{:S(2)}) collective-permute-start(f32[22,16,128]{2,1,0:T(8,128)S(1)} %get-tuple-element.41), channel_id=1, source_target_pairs={{0,1},{1,2},{2,3},{3,4},{4,5},{5,6},{6,7},{7,8},{8,9},{9,10},{10,1... | collective-permute-start | bytes 540680 | tf_op jit(solution)/shard_map/ppermute | solution.py:603
  32.2 1.9 %collective-permute-start.5 = (f32[22,16,128]{2,1,0:T(8,128)S(1)}, f32[22,16,128]{2,1,0:T(8,128)S(1)}, u32[]{:S(2)}, u32[]{:S(2)}) collective-permute-start(f32[22,16,128]{2,1,0:T(8,128)S(1)} %get-tuple-element.42), channel_id=1, source_target_pairs={{1,0},{2,1},{3,2},{4,3},{5,4},{6,5},{7,6},{8,7},{9,8},{10,9},{11,1... | collective-permute-start | bytes 540680 | tf_op jit(solution)/shard_map/ppermute | solution.py:604
  34.2 0.5 collective-permute-done.4.zlo
  34.7 4.4 %collective-permute-done.5.zhi = f32[22,16,128]{2,1,0:T(8,128)S(1)} collective-permute-done((f32[22,16,128]{2,1,0:T(8,128)S(1)}, f32[22,16,128]{2,1,0:T(8,128)S(1)}, u32[]{:S(2)}, u32[]{:S(2)}) %collective-permute-start.5) | collective-permute-done | bytes 180256 | tf_op jit(solution)/shard_map/ppermute | solution.py:604
  39.1 5.3 %shard_map.49 = (f32[8,48,128]{2,1,0:T(8,128)S(1)}, f32[8,24,128]{2,1,0:T(8,128)S(1)}, f32[8,24,128]{2,1,0:T(8,128)S(1)}, f32[22,176,128]{2,1,0:T(8,128)S(1)}, f...) custom-call(f32[22,128,128]{2,1,0:T(8,128)S(1)} %get-tuple-element.40.turned, ...), custom_call_target="tpu_custom_call" | custom-call | tf_op jit(solution)/shard_map/pallas_call | solution.py:591
  44.4 3.3 %collective-permute-start.6 = (f32[8,24,128]{2,1,0:T(8,128)S(1)}, f32[8,24,128]{2,1,0:T(8,128)S(1)}, u32[]{:S(2)}, u32[]{:S(2)}) collective-permute-start(f32[8,24,128]{2,1,0:T(8,128)S(1)} %get-tuple-element.44), channel_id=1, source_target_pairs={{0,16},{16,32},{32,48},{48,64},{64,80},{80,96},{96,112},{1,17},{17... | collective-permute-start | bytes 294920 | tf_op jit(solution)/shard_map/ppermute | solution.py:603
  47.7 1.3 collective-permute-start.7
  49.0 0.3 collective-permute-done.6.ylo
  49.3 4.6 %collective-permute-done.7.yhi = f32[8,24,128]{2,1,0:T(8,128)S(1)} collective-permute-done((f32[8,24,128]{2,1,0:T(8,128)S(1)}, f32[8,24,128]{2,1,0:T(8,128)S(1)}, u32[]{:S(2)}, u32[]{:S(2)}) %collective-permute-start.7) | collective-permute-done | bytes 98336 | tf_op jit(solution)/shard_map/ppermute | solution.py:604
  53.9 4.7 %collective-permute-start.8 = (f32[4,96,128]{2,1,0:T(8,128)S(1)}, f32[4,96,128]{2,1,0:T(8,128)S(1)}, u32[]{:S(2)}, u32[]{:S(2)}) collective-permute-start(f32[4,96,128]{2,1,0:T(8,128)S(1)} %get-tuple-element.46), channel_id=1, source_target_pairs={{0,128},{128,256},{256,384},{384,512},{512,640},{640,768},{768,896... | collective-permute-start | bytes 589832 | tf_op jit(solution)/shard_map/ppermute | solution.py:603
  58.6 1.9 %collective-permute-start.9 = (f32[4,96,128]{2,1,0:T(8,128)S(1)}, f32[4,96,128]{2,1,0:T(8,128)S(1)}, u32[]{:S(2)}, u32[]{:S(2)}) collective-permute-start(f32[4,96,128]{2,1,0:T(8,128)S(1)} %get-tuple-element.47), channel_id=1, source_target_pairs={{128,0},{256,128},{384,256},{512,384},{640,512},{768,640},{896,768... | collective-permute-start | bytes 589832 | tf_op jit(solution)/shard_map/ppermute | solution.py:604
  60.5 1.3 collective-permute-done.8.xlo
  61.9 4.1 %collective-permute-done.9.xhi = f32[4,96,128]{2,1,0:T(8,128)S(1)} collective-permute-done((f32[4,96,128]{2,1,0:T(8,128)S(1)}, f32[4,96,128]{2,1,0:T(8,128)S(1)}, u32[]{:S(2)}, u32[]{:S(2)}) %collective-permute-start.9) | collective-permute-done | bytes 196640 | tf_op jit(solution)/shard_map/ppermute | solution.py:604
  66.0 1.6 %shard_map.51 = (f32[64,24,128]{2,1,0:T(8,128)S(1)}, f32[16,96,128]{2,1,0:T(8,128)S(1)}, f32[16,96,128]{2,1,0:T(8,128)S(1)}, f32[16,80,128]{2,1,0:T(8,128)S(1)}) custom-call(f32[8,48,128]{2,1,0:T(8,128)S(1)} %get-tuple-element.43.own, f32[8,24,128]{2,1,0:T(8,128)S(1)} %collective-permute-done.6.ylo, f32[8,24,128]{2,1,0:T(8,128)S(1)} %collective-permute-done.7.yhi, ...), custom_call_target="tpu_custom_call" | custom-call | tf_op jit(solution)/shard_map/pallas_call | solution.py:591
  67.6 34.5 %all_to_all.5.got = f32[64,24,128]{2,1,0:T(8,128)S(1)} all-to-all(f32[64,24,128]{2,1,0:T(8,128)S(1)} %get-tuple-element.48), channel_id=1, replica_groups=mesh['gx'=8,'gy'=8,'gz'=16] {'gx','gy'}, dimensions={0} | all-to-all | bytes 1572864 | tf_op jit(solution)/shard_map/all_to_all | solution.py:609
  102.0 1.0 shard_map.52
  103.1 3.2 %collective-permute-start.10 = (f32[32,16,128]{2,1,0:T(8,128)S(1)}, f32[32,16,128]{2,1,0:T(8,128)S(1)}, u32[]{:S(2)}, u32[]{:S(2)}) collective-permute-start(f32[32,16,128]{2,1,0:T(8,128)S(1)} %get-tuple-element.51), channel_id=1, source_target_pairs={{0,1},{1,2},{2,3},{3,4},{4,5},{5,6},{6,7},{7,8},{8,9},{9,10},{10,1... | collective-permute-start | bytes 786440 | tf_op jit(solution)/shard_map/ppermute | solution.py:603
  106.4 1.9 %collective-permute-start.11 = (f32[32,16,128]{2,1,0:T(8,128)S(1)}, f32[32,16,128]{2,1,0:T(8,128)S(1)}, u32[]{:S(2)}, u32[]{:S(2)}) collective-permute-start(f32[32,16,128]{2,1,0:T(8,128)S(1)} %get-tuple-element.52), channel_id=1, source_target_pairs={{1,0},{2,1},{3,2},{4,3},{5,4},{6,5},{7,6},{8,7},{9,8},{10,9},{11,1... | collective-permute-start | bytes 786440 | tf_op jit(solution)/shard_map/ppermute | solution.py:604
  108.3 1.4 collective-permute-done.10.zlo
  109.6 5.3 %collective-permute-done.11.zhi = f32[32,16,128]{2,1,0:T(8,128)S(1)} collective-permute-done((f32[32,16,128]{2,1,0:T(8,128)S(1)}, f32[32,16,128]{2,1,0:T(8,128)S(1)}, u32[]{:S(2)}, u32[]{:S(2)}) %collective-permute-start.11) | collective-permute-done | bytes 262176 | tf_op jit(solution)/shard_map/ppermute | solution.py:604
  115.0 3.5 %shard_map.53 = (f32[16,32,128]{2,1,0:T(8,128)S(1)}, f32[16,20,128]{2,1,0:T(8,128)S(1)}, f32[16,20,128]{2,1,0:T(8,128)S(1)}, f32[12,48,128]{2,1,0:T(8,128)S(1)},...) custom-call(f32[32,32,128]{2,1,0:T(8,128)S(1)} %get-tuple-element.49.b, f32[32,32,128]{2,1,0:T(8,128)S(1)} %get-tuple-element.50.c, ...), custom_call_target="tpu_custom_call" | custom-call | tf_op jit(solution)/shard_map/pallas_call | solution.py:591
  118.4 4.2 %collective-permute-start.12 = (f32[16,20,128]{2,1,0:T(8,128)S(1)}, f32[16,20,128]{2,1,0:T(8,128)S(1)}, u32[]{:S(2)}, u32[]{:S(2)}) collective-permute-start(f32[16,20,128]{2,1,0:T(8,128)S(1)} %get-tuple-element.54), channel_id=1, source_target_pairs={{0,1},{1,2},{2,3},{3,4},{4,5},{5,6},{6,7},{7,8},{8,9},{9,10},{10,1... | collective-permute-start | bytes 491528 | tf_op jit(solution)/shard_map/ppermute | solution.py:603
  122.7 1.9 %collective-permute-start.13 = (f32[16,20,128]{2,1,0:T(8,128)S(1)}, f32[16,20,128]{2,1,0:T(8,128)S(1)}, u32[]{:S(2)}, u32[]{:S(2)}) collective-permute-start(f32[16,20,128]{2,1,0:T(8,128)S(1)} %get-tuple-element.55), channel_id=1, source_target_pairs={{1,0},{2,1},{3,2},{4,3},{5,4},{6,5},{7,6},{8,7},{9,8},{10,9},{11,1... | collective-permute-start | bytes 491528 | tf_op jit(solution)/shard_map/ppermute | solution.py:604
  124.6 0.7 collective-permute-done.12.zlo
  125.3 8.6 %collective-permute-done.13.zhi = f32[16,20,128]{2,1,0:T(8,128)S(1)} collective-permute-done((f32[16,20,128]{2,1,0:T(8,128)S(1)}, f32[16,20,128]{2,1,0:T(8,128)S(1)}, u32[]{:S(2)}, u32[]{:S(2)}) %collective-permute-start.13) | collective-permute-done | bytes 163872 | tf_op jit(solution)/shard_map/ppermute | solution.py:604
  133.9 4.0 %shard_map.54.e2 = f32[8,40,128]{2,1,0:T(8,128)S(1)} custom-call(f32[16,32,128]{2,1,0:T(8,128)S(1)} %get-tuple-element.53.own, f32[16,20,128]{2,1,0:T(8,128)S(1)} %collective-permute-done.12.zlo, f32[16,20,128]{2,1,0:T(8,128)S(1)} %collective-permute-done.13.zhi, f32[12,48,128]{2,1,0:T(8,128)S(1)} %get-tuple-element.56.w2, ...), custom_call_target="tpu_custom_call" | custom-call | tf_op jit(solution)/shard_map/pallas_call | solution.py:591
  137.9 3.9 %shard_map.55 = f32[4,16,16,128]{3,2,1,0:T(8,128)} custom-call(f32[8,40,128]{2,1,0:T(8,128)S(1)} %shard_map.54.e2, f32[16,96,128]{2,1,0:T(8,128)S(1)} %get-tuple-element.59.w1, f32[16,96,128]{2,1,0:T(8,128)S(1)} %get-tuple-element.60.beta1, f32[16,80,128]{2,1,0:T(8,128)S(1)} %get-tuple-element.61.root1, f32[22,176,128]{2,1,0:T(8,128)S(1)} %get-tuple-element.62.w0, ...), custom_call_target="tpu_custom_call" | custom-call | tf_op jit(solution)/shard_map/pallas_call | solution.py:591
  (1 shorter events, 0.0 us)
Async XLA Ops:
  0.0 1.0 copy-start
  1.0 0.9 copy-start.1
  1.9 0.7 copy-start.2
  2.6 0.7 copy-start.3
  4.0 6.1 %collective-permute-start = (f32[5,3,16,128]{3,2,1,0:T(8,128)S(1)}, f32[5,3,16,128]{3,2,1,0:T(8,128)S(1)}, u32[]{:S(2)}, u32[]{:S(2)}) collective-permute-start(f32[5,3,16,128]{3,2,1,0:T(8,128)S(1)} %get-tuple-element.35), channel_id=1, source_target_pairs={{0,128},{128,256},{256,384},{384,512},{512,640},{640,768},{768,896... | collective-permute-start | bytes 368648 | tf_op jit(solution)/shard_map/ppermute | solution.py:603
  7.1 7.1 %collective-permute-start.1 = (f32[5,3,16,128]{3,2,1,0:T(8,128)S(1)}, f32[5,3,16,128]{3,2,1,0:T(8,128)S(1)}, u32[]{:S(2)}, u32[]{:S(2)}) collective-permute-start(f32[5,3,16,128]{3,2,1,0:T(8,128)S(1)} %get-tuple-element.37), channel_id=1, source_target_pairs={{128,0},{256,128},{384,256},{512,384},{640,512},{768,640},{896,768... | collective-permute-start | bytes 368648 | tf_op jit(solution)/shard_map/ppermute | solution.py:604
  14.2 5.7 %collective-permute-start.2 = (f32[22,15,128]{2,1,0:T(8,128)S(1)}, f32[22,15,128]{2,1,0:T(8,128)S(1)}, u32[]{:S(2)}, u32[]{:S(2)}) collective-permute-start(f32[22,15,128]{2,1,0:T(8,128)S(1)} %get-tuple-element.38), channel_id=1, source_target_pairs={{0,16},{16,32},{32,48},{48,64},{64,80},{80,96},{96,112},{1,17},{17... | collective-permute-start | bytes 506888 | tf_op jit(solution)/shard_map/ppermute | solution.py:603
  17.5 6.2 %collective-permute-start.3 = (f32[22,15,128]{2,1,0:T(8,128)S(1)}, f32[22,15,128]{2,1,0:T(8,128)S(1)}, u32[]{:S(2)}, u32[]{:S(2)}) collective-permute-start(f32[22,15,128]{2,1,0:T(8,128)S(1)} %get-tuple-element.39), channel_id=1, source_target_pairs={{16,0},{32,16},{48,32},{64,48},{80,64},{96,80},{112,96},{17,1},{33... | collective-permute-start | bytes 506888 | tf_op jit(solution)/shard_map/ppermute | solution.py:604
  24.5 10.2 %collective-permute-start.4 = (f32[22,16,128]{2,1,0:T(8,128)S(1)}, f32[22,16,128]{2,1,0:T(8,128)S(1)}, u32[]{:S(2)}, u32[]{:S(2)}) collective-permute-start(f32[22,16,128]{2,1,0:T(8,128)S(1)} %get-tuple-element.41), channel_id=1, source_target_pairs={{0,1},{1,2},{2,3},{3,4},{4,5},{5,6},{6,7},{7,8},{8,9},{9,10},{10,1... | collective-permute-start | bytes 540680 | tf_op jit(solution)/shard_map/ppermute | solution.py:603
  32.2 6.8 %collective-permute-start.5 = (f32[22,16,128]{2,1,0:T(8,128)S(1)}, f32[22,16,128]{2,1,0:T(8,128)S(1)}, u32[]{:S(2)}, u32[]{:S(2)}) collective-permute-start(f32[22,16,128]{2,1,0:T(8,128)S(1)} %get-tuple-element.42), channel_id=1, source_target_pairs={{1,0},{2,1},{3,2},{4,3},{5,4},{6,5},{7,6},{8,7},{9,8},{10,9},{11,1... | collective-permute-start | bytes 540680 | tf_op jit(solution)/shard_map/ppermute | solution.py:604
  44.4 4.9 %collective-permute-start.6 = (f32[8,24,128]{2,1,0:T(8,128)S(1)}, f32[8,24,128]{2,1,0:T(8,128)S(1)}, u32[]{:S(2)}, u32[]{:S(2)}) collective-permute-start(f32[8,24,128]{2,1,0:T(8,128)S(1)} %get-tuple-element.44), channel_id=1, source_target_pairs={{0,16},{16,32},{32,48},{48,64},{64,80},{80,96},{96,112},{1,17},{17... | collective-permute-start | bytes 294920 | tf_op jit(solution)/shard_map/ppermute | solution.py:603
  47.7 6.2 %collective-permute-start.7 = (f32[8,24,128]{2,1,0:T(8,128)S(1)}, f32[8,24,128]{2,1,0:T(8,128)S(1)}, u32[]{:S(2)}, u32[]{:S(2)}) collective-permute-start(f32[8,24,128]{2,1,0:T(8,128)S(1)} %get-tuple-element.45), channel_id=1, source_target_pairs={{16,0},{32,16},{48,32},{64,48},{80,64},{96,80},{112,96},{17,1},{33... | collective-permute-start | bytes 294920 | tf_op jit(solution)/shard_map/ppermute | solution.py:604
  53.9 7.9 %collective-permute-start.8 = (f32[4,96,128]{2,1,0:T(8,128)S(1)}, f32[4,96,128]{2,1,0:T(8,128)S(1)}, u32[]{:S(2)}, u32[]{:S(2)}) collective-permute-start(f32[4,96,128]{2,1,0:T(8,128)S(1)} %get-tuple-element.46), channel_id=1, source_target_pairs={{0,128},{128,256},{256,384},{384,512},{512,640},{640,768},{768,896... | collective-permute-start | bytes 589832 | tf_op jit(solution)/shard_map/ppermute | solution.py:603
  58.6 7.4 %collective-permute-start.9 = (f32[4,96,128]{2,1,0:T(8,128)S(1)}, f32[4,96,128]{2,1,0:T(8,128)S(1)}, u32[]{:S(2)}, u32[]{:S(2)}) collective-permute-start(f32[4,96,128]{2,1,0:T(8,128)S(1)} %get-tuple-element.47), channel_id=1, source_target_pairs={{128,0},{256,128},{384,256},{512,384},{640,512},{768,640},{896,768... | collective-permute-start | bytes 589832 | tf_op jit(solution)/shard_map/ppermute | solution.py:604
  103.1 6.5 %collective-permute-start.10 = (f32[32,16,128]{2,1,0:T(8,128)S(1)}, f32[32,16,128]{2,1,0:T(8,128)S(1)}, u32[]{:S(2)}, u32[]{:S(2)}) collective-permute-start(f32[32,16,128]{2,1,0:T(8,128)S(1)} %get-tuple-element.51), channel_id=1, source_target_pairs={{0,1},{1,2},{2,3},{3,4},{4,5},{5,6},{6,7},{7,8},{8,9},{9,10},{10,1... | collective-permute-start | bytes 786440 | tf_op jit(solution)/shard_map/ppermute | solution.py:603
  106.4 8.6 %collective-permute-start.11 = (f32[32,16,128]{2,1,0:T(8,128)S(1)}, f32[32,16,128]{2,1,0:T(8,128)S(1)}, u32[]{:S(2)}, u32[]{:S(2)}) collective-permute-start(f32[32,16,128]{2,1,0:T(8,128)S(1)} %get-tuple-element.52), channel_id=1, source_target_pairs={{1,0},{2,1},{3,2},{4,3},{5,4},{6,5},{7,6},{8,7},{9,8},{10,9},{11,1... | collective-permute-start | bytes 786440 | tf_op jit(solution)/shard_map/ppermute | solution.py:604
  118.4 6.8 %collective-permute-start.12 = (f32[16,20,128]{2,1,0:T(8,128)S(1)}, f32[16,20,128]{2,1,0:T(8,128)S(1)}, u32[]{:S(2)}, u32[]{:S(2)}) collective-permute-start(f32[16,20,128]{2,1,0:T(8,128)S(1)} %get-tuple-element.54), channel_id=1, source_target_pairs={{0,1},{1,2},{2,3},{3,4},{4,5},{5,6},{6,7},{7,8},{8,9},{9,10},{10,1... | collective-permute-start | bytes 491528 | tf_op jit(solution)/shard_map/ppermute | solution.py:603
  122.7 11.2 %collective-permute-start.13 = (f32[16,20,128]{2,1,0:T(8,128)S(1)}, f32[16,20,128]{2,1,0:T(8,128)S(1)}, u32[]{:S(2)}, u32[]{:S(2)}) collective-permute-start(f32[16,20,128]{2,1,0:T(8,128)S(1)} %get-tuple-element.55), channel_id=1, source_target_pairs={{1,0},{2,1},{3,2},{4,3},{5,4},{6,5},{7,6},{8,7},{9,8},{10,9},{11,1... | collective-permute-start | bytes 491528 | tf_op jit(solution)/shard_map/ppermute | solution.py:604

commit v5 on v4

--- a/solution.py
+++ b/solution.py
@@ -14,10 +14,9 @@
 LANES = 128
 HX0, HY0, HZ0 = 3, 3, 16
 Y0 = 16 + 2 * HY0
-Y1 = 16
-HZ2 = 10
-HZ3 = 20
-OFF2, OFF3 = 4, 2
+H1, H2 = 6, 5
+Y1, Y2 = 8 + 2 * H1, 4 + 2 * H2
+OFF3 = 2
 
 
 def halves(a):
@@ -95,19 +94,32 @@
     return bits((source == out >> 1) & (out < 4 * out_width)).astype(jnp.bfloat16)
 
 
-def repeat_to_level0():
+def repeat_local(width, shift, out_width, out_start, fields=4):
     source = lax.broadcasted_iota(jnp.int32, (LANES, LANES), 0)
     out = lane_of(LANES)
-    field = bits(out >= Y0) + bits(out >= 2 * Y0) + bits(out >= 3 * Y0)
+    field = bits(out >= out_width) + bits(out >= 2 * out_width) + bits(out >= 3 * out_width)
     field = field.astype(jnp.int32)
-    wanted = field * Y1 + 4 + ((out - field * Y0 - HY0) >> 1)
-    return bits((source == wanted) & (out < 4 * Y0)).astype(jnp.bfloat16)
+    row = shift + ((out - field * out_width - out_start) >> 1)
+    hit = (source == field * width + row) & (row >= 0) & (row < width) & (out < fields * out_width)
+    return bits(hit).astype(jnp.bfloat16)
+
+
+def four_fields(t, width):
+    lane = lane_of(t.shape[0])
+    c = jnp.where(lane < 2 * width, lane_roll(t, -3 * width), lane_roll(t, -2 * width))
+    c = jnp.where(lane < width, lane_roll(t, -4 * width), c)
+    return jnp.where(lane < 4 * width, c, 0.0)
 
 
 def residual(w, beta, root, x, row, n, mid_total):
     mid, total = mid_total
     root_x = root[x, pl.ds(row - 8, n), :]
     return root_x * ((1.0 / TAU) * beta[x, pl.ds(row, n), :] - 6.0 * mid + total), root_x * root_x
+
+
+def thirds(ref):
+    n = ref.shape[0] // 3
+    return [ref.at[pl.ds(i * n, n)] for i in range(3)]
 
 
 def loop(begin, end, body, unroll=1):
@@ -195,10 +207,11 @@
     loop(0, 4, own, 2)
 
 
-def down0_kernel(turned, zlo, zhi, out, ylo, yhi, w, beta, root, rsum, csum, rz, cz, stage):
+def down0_kernel(turned, zlo, zhi, out, ylo, yhi, kept, rsum, csum, rz, cz, stage):
     planes = 16 + 2 * HX0
     depth = 128 + 2 * HZ0
     half = depth // 2
+    w, beta, root = thirds(kept)
     qb = pair_lanes(Y0, HY0, 8, 0, 0.5)
     qc = pair_lanes(Y0, HY0, 8, 32, 0.125, 2, 3)
 
@@ -255,161 +268,158 @@
         t = stage[k].T
         out[k] = t[0:48]
         for a in range(6):
-            ylo[k, pl.ds(a * 4, 4), :] = t[a * 8 : a * 8 + 4]
-            yhi[k, pl.ds(a * 4, 4), :] = t[a * 8 + 4 : a * 8 + 8]
-
-
-def join_kernel(own, ylo, yhi, low, high):
-    for ref, first in ((low, 0), (high, 4)):
-        for x in range(4):
-            ref[x, pl.ds(0, 48), :] = own[first + x]
-            ref[x, pl.ds(48, 24), :] = ylo[first + x]
-            ref[x, pl.ds(72, 24), :] = yhi[first + x]
-
-
-def down1_kernel(own, ylo, yhi, xlo, xhi, block, w, beta, root, stage, rsum, csum, rz, cz):
+            ylo[k, pl.ds(a * H1, H1), :] = t[a * 8 : a * 8 + H1]
+            yhi[k, pl.ds(a * H1, H1), :] = t[a * 8 + 8 - H1 : a * 8 + 8]
+
+
+def join1_kernel(own, ylo, yhi, turned, low, high, stage):
     stage[...] = jnp.zeros_like(stage)
-
-    def prepare(x, slot, mine, lo, hi):
+    for x in range(8):
+        slot = x % 4
         for a in range(6):
-            stage[slot, pl.ds(a * Y1 + 4, 8), :] = mine(a * 8, 8)
-            stage[slot, pl.ds(a * Y1, 4), :] = lo(a * 4, 4)
-            stage[slot, pl.ds(a * Y1 + 12, 4), :] = hi(a * 4, 4)
+            stage[slot, pl.ds(a * Y1 + H1, 8), :] = own[x, pl.ds(a * 8, 8), :]
+            stage[slot, pl.ds(a * Y1, H1), :] = ylo[x, pl.ds(a * H1, H1), :]
+            stage[slot, pl.ds(a * Y1 + H1 + 8, H1), :] = yhi[x, pl.ds(a * H1, H1), :]
         t = stage[slot].T[0:80]
-        lane = lane_of(80)
-        c = jnp.where(lane < Y1, lane_roll(t, 64), jnp.where(lane < 2 * Y1, lane_roll(t, 80), lane_roll(t, 96)))
-        root_x, inv_x = roots_of(jnp.where(lane < 4 * Y1, c, 0.0))
-        root[x] = root_x
+        turned[x] = t
+        if x < H1:
+            low[x] = t
+        if x >= 8 - H1:
+            high[x - 8 + H1] = t
+
+
+def down1_kernel(own, xlo, xhi, block, turned2, ylo2, yhi2, kept, rsum, csum, rz, cz, beta2, root2, w2, stage):
+    w, beta, root = thirds(kept)
+
+    def prepare(x, t):
+        root_x, inv_x = roots_of(four_fields(t, Y1))
+        root[x, pl.ds(0, 80), :] = root_x
         beta[x, pl.ds(8, 80), :] = TAU * t * inv_x
         for ref in (beta, w):
             ref[x, pl.ds(0, 8), :] = jnp.zeros((8, LANES), F32)
             ref[x, pl.ds(88, 8), :] = jnp.zeros((8, LANES), F32)
 
-    for x in range(4):
-        for slot, side in ((0, xlo), (1, xhi)):
-            prepare(
-                x + 12 * slot,
-                2 * (x % 2) + slot,
-                lambda r, n: side[x, pl.ds(r, n), :],
-                lambda r, n: side[x, pl.ds(48 + r, n), :],
-                lambda r, n: side[x, pl.ds(72 + r, n), :],
-            )
+    for x in range(H1):
+        prepare(x, xlo[x])
+        prepare(x + H1 + 8, xhi[x])
     for x in range(8):
-        prepare(
-            x + 4,
-            x % 4,
-            lambda r, n: own[x, pl.ds(r, n), :],
-            lambda r, n: ylo[x, pl.ds(r, n), :],
-            lambda r, n: yhi[x, pl.ds(r, n), :],
-        )
+        prepare(x + H1, own[x])
 
     def smooth(x):
         for r, n in chunks(80, 40):
             mid, total = around(beta, x, 8 + r, n)
             w[x, pl.ds(8 + r, n), :] = jnp.where(root[x, pl.ds(r, n), :] > 0.0, 1.2 * mid + TAU * total, 0.0)
 
-    loop(1, 15, smooth, 14)
-    for k in range(4):
-        for r, n in chunks(64, 32):
-            x = 4 + 2 * k
-            res_a, coef_a = residual(w, beta, root, x, 16 + r, n, around(w, x, 16 + r, n))
-            res_b, coef_b = residual(w, beta, root, x + 1, 16 + r, n, around(w, x + 1, 16 + r, n))
+    loop(1, 19, smooth, 9)
+
+    def restrict(k):
+        for r, n in chunks(80, 40):
+            x = 2 + 2 * k
+            res_a, coef_a = residual(w, beta, root, x, 8 + r, n, around(w, x, 8 + r, n))
+            res_b, coef_b = residual(w, beta, root, x + 1, 8 + r, n, around(w, x + 1, 8 + r, n))
             rsum[k, pl.ds(r, n), :] = res_a + res_b
             csum[k, pl.ds(r, n), :] = coef_a + coef_b
-    for k in range(4):
-        rz[pl.ds(k * 32, 32), :] = fold_rows(rsum, k, 32)
-        cz[pl.ds(k * 32, 32), :] = fold_rows(csum, k, 32)
-    qb = pair_lanes(Y1, 4, 4, 0, 0.5)
-    qc = pair_lanes(Y1, 4, 4, 16, 0.125, 2, 3)
-    t = mm(((rz[...], qb), (cz[...], qc))).T[0:24]
-
-    def copy(i):
-        block[i] = t
-
-    loop(0, block.shape[0], copy, 8 if block.shape[0] % 8 == 0 else 1)
-
-
-def plane_kernel(gx, gy, got, b, c, zlo, zhi, stage_b, stage_c):
-    width = 4 * gy
-    stage_b[...] = jnp.zeros_like(stage_b)
-    stage_c[...] = jnp.zeros_like(stage_c)
-
-    def one(i, slot):
-        for j in range(gy):
-            for a in range(4):
-                stage_b[slot, pl.ds(a * width + 4 * j, 4), :] = got[i * gy + j, pl.ds(4 * a, 4), :]
-            for a in range(2):
-                stage_c[slot, pl.ds(a * width + 4 * j, 4), :] = got[i * gy + j, pl.ds(16 + 4 * a, 4), :]
-        tb = stage_b[slot].T
-        tc = stage_c[slot].T
-        for x in range(4):
-            at = 4 * i + x
-            b[at] = tb[x * 32 : (x + 1) * 32]
-            c[at] = tc[x * 32 : (x + 1) * 32]
-            for ref, first in ((zlo, x * 32), (zhi, (x + 1) * 32 - HZ2)):
-                ref[at, pl.ds(0, HZ2), :] = tb[first : first + HZ2]
-                ref[at, pl.ds(HZ2, 5), :] = jnp.where(
-                    lane_of(5) < 64, tc[first : first + 5], lane_roll(tc[first + 5 : first + 10], 64)
-                )
-                ref[at, pl.ds(HZ2 + 5, 1), :] = jnp.zeros((1, LANES), F32)
-
-    def body(k):
-        one(2 * k, 0)
-        one(2 * k + 1, 1)
-
-    loop(0, gx // 2, body)
-
-
-def down2_kernel(gx, gy, b, c, zlo, zhi, out, zup, zdown, w_kept, beta_kept, root_kept, w, beta, root, rsum, csum, rz, cz):
-    size_x, width = 4 * gx, 4 * gy
-
-    def prepare(x, row, t, tc):
-        n = t.shape[0]
-        lane = lane_of(n)
-        c_all = jnp.where(lane < width, tc, jnp.where(lane < 2 * width, lane_roll(tc, width), lane_roll(tc, 2 * width)))
-        root_x, inv_x = roots_of(jnp.where(lane < 4 * width, c_all, 0.0))
-        root[x + OFF2, pl.ds(row, n), :] = root_x
-        beta[x + OFF2, pl.ds(8 + row, n), :] = TAU * t * inv_x
-
-    for x in list(range(OFF2)) + list(range(OFF2 + size_x, 2 * OFF2 + size_x)):
-        for ref in (beta, w, root):
-            ref[x] = jnp.zeros(ref.shape[1:], F32)
-
-    def setup(x):
-        for ref in (beta, w):
-            ref[x + OFF2, pl.ds(0, 16), :] = jnp.zeros((16, LANES), F32)
-            ref[x + OFF2, pl.ds(64, 16), :] = jnp.zeros((16, LANES), F32)
-        root[x + OFF2, pl.ds(0, 8), :] = jnp.zeros((8, LANES), F32)
-        root[x + OFF2, pl.ds(56, 8), :] = jnp.zeros((8, LANES), F32)
-        prepare(x, 16, b[x], c[x])
-        for ref, row in ((zlo, 16 - HZ2), (zhi, 48)):
-            packed = ref[x, pl.ds(HZ2, 5), :]
-            prepare(x, row, ref[x, pl.ds(0, 5), :], jnp.where(lane_of(5) < 64, packed, 0.0))
-            prepare(x, row + 5, ref[x, pl.ds(5, 5), :], jnp.where(lane_of(5) < 64, lane_roll(packed, 64), 0.0))
-
-    loop(0, size_x, setup, 8)
-
-    def smooth(x):
-        for r, n in chunks(64, 32):
-            mid, total = around_whole(beta, x, 8 + r, n, width)
-            w[x, pl.ds(8 + r, n), :] = jnp.where(root[x, pl.ds(r, n), :] > 0.0, 1.2 * mid + TAU * total, 0.0)
-
-    loop(OFF2, size_x + OFF2, smooth, 8)
-    restrict_whole(size_x, OFF2, width, w, beta, root, rsum, csum, rz, cz)
-    qb = pair_lanes(width, 0, width // 2, 0, 0.5)
-    qc = pair_lanes(width, 0, width // 2, 64, 0.125)
-    first = 4 * position("gx") - 4 + OFF2
-    for p in range(12):
-        w_kept[p] = w[first + p, pl.ds(16, 48), :]
-        beta_kept[p] = beta[first + p, pl.ds(16, 48), :]
-        root_kept[p] = root[first + p, pl.ds(8, 48), :]
-    for k in range(0, size_x // 2, 4):
-        rows = pl.ds(k * 32, 128)
-        t = mm(((rz[rows, :], qb), (cz[rows, :], qc)))
-        for i in range(4):
-            out[k + i] = t[i * 32 : (i + 1) * 32]
-            zup[k + i] = t[i * 32 + 24 - HZ3 : i * 32 + 24]
-            zdown[k + i] = t[i * 32 + 8 : i * 32 + 8 + HZ3]
+
+    loop(0, 8, restrict, 4)
+    for k in range(8):
+        rz[pl.ds(k * 40, 40), :] = fold_rows(rsum, k, 40)
+        cz[pl.ds(k * 40, 40), :] = fold_rows(csum, k, 40)
+
+    t2 = mm(((rz[...], pair_lanes(Y1, 2, 8, 0, 0.5)), (cz[...], pair_lanes(Y1, 2, 8, 32, 0.125, 2, 3))))
+    stage[...] = jnp.zeros_like(stage)
+    for x in range(8):
+        t = t2[x * 40 : (x + 1) * 40]
+        root_x, inv_x = roots_of(four_fields(t, 8))
+        root2[x] = root_x
+        beta2[x, pl.ds(8, 40), :] = TAU * t * inv_x
+        for ref in (beta2, w2):
+            ref[x, pl.ds(0, 8), :] = jnp.zeros((8, LANES), F32)
+            ref[x, pl.ds(48, 8), :] = jnp.zeros((8, LANES), F32)
+        if 1 <= x < 7:
+            stage[x % 4, pl.ds(0, 40), :] = t
+            flat = stage[x % 4].T
+            for a in range(6):
+                turned2[x - 1, pl.ds(a * 4, 4), :] = flat[a * 8 + 2 : a * 8 + 6]
+                yhi2[x - 1, pl.ds(a * H2, H2), :] = flat[a * 8 + 1 : a * 8 + 1 + H2]
+                ylo2[x - 1, pl.ds(a * H2, H2), :] = flat[a * 8 + 2 : a * 8 + 2 + H2]
+    for x in range(1, 7):
+        mid, total = around(beta2, x, 8, 40)
+        w2[x, pl.ds(8, 40), :] = jnp.where(root2[x] > 0.0, 1.2 * mid + TAU * total, 0.0)
+    for k in range(2):
+        x = 2 + 2 * k
+        res, coef = jnp.zeros((32, LANES), F32), jnp.zeros((32, LANES), F32)
+        for i in range(2):
+            res_i, coef_i = residual(w2, beta2, root2, x + i, 12, 32, around(w2, x + i, 12, 32))
+            res, coef = res + res_i, coef + coef_i
+        rsum[k, pl.ds(0, 32), :] = res
+        csum[k, pl.ds(0, 32), :] = coef
+    rows = [jnp.concatenate([fold_rows(ref, k, 16) for k in range(2)], axis=0) for ref in (rsum, csum)]
+    t3 = mm(((rows[0], pair_lanes(8, 2, 2, 0, 0.5)), (rows[1], pair_lanes(8, 2, 2, 8, 0.125, 2, 3))))
+
+    stage[0, pl.ds(0, 32), :] = t3
+    stage[0, pl.ds(32, 96), :] = jnp.zeros((96, LANES), F32)
+    flat = stage[0].T[0:16]
+    lane = lane_of(1)
+    turns = [lane_roll(flat, 32 * g) for g in range(4)]
+    packed = []
+    for r in range(3):
+        row = turns[0][4 * r : 4 * r + 1]
+        for g in range(1, 4):
+            row = jnp.where((lane >= 32 * g) & (lane < 32 * g + 32), turns[g][4 * r + g : 4 * r + g + 1], row)
+        packed.append(row)
+    for i in range(block.shape[0] // 24):
+        block[pl.ds(24 * i, 24), :] = jnp.concatenate(packed * 8, axis=0)
+    for i in range(block.shape[0] // 24 * 8, block.shape[0] // 3):
+        block[pl.ds(3 * i, 3), :] = jnp.concatenate(packed, axis=0)
+
+
+def join2_kernel(own, ylo, yhi, turned, low, high, stage):
+    stage[...] = jnp.zeros_like(stage)
+    for x in range(6):
+        slot = x % 4
+        for a in range(6):
+            stage[slot, pl.ds(a * Y2 + H2, 4), :] = own[x, pl.ds(a * 4, 4), :]
+            stage[slot, pl.ds(a * Y2, H2), :] = ylo[x, pl.ds(a * H2, H2), :]
+            stage[slot, pl.ds(a * Y2 + H2 + 4, H2), :] = yhi[x, pl.ds(a * H2, H2), :]
+        t = stage[slot].T[4:36]
+        if 1 <= x < 5:
+            turned[x - 1] = t
+        if x < 5:
+            high[x] = t
+        if x >= 1:
+            low[x - 1] = t
+
+
+def join3_kernel(own, xlo, xhi, whole, zlo, zhi):
+    for x in range(4 + 2 * H2):
+        t = xlo[x] if x < H2 else own[x - H2] if x < H2 + 4 else xhi[x - H2 - 4]
+        whole[x] = t
+        zlo[x] = t[0:8]
+        zhi[x] = t[24:32]
+
+
+def plane_kernel(gx, gy, got, own, lo4, hi4, turns, stage):
+    width = 2 * gy
+    stage[...] = jnp.zeros_like(stage)
+    for s in range(4):
+        turns[s] = lane_roll(got[...], 32 * s)
+    lane = lane_of(gy)
+    for h in range(-(-gx // 4)):
+        for i in range(12):
+            r, g = i // 4, i % 4
+            row = jnp.zeros((gy, LANES), F32)
+            for q in range(min(4, gx - 4 * h)):
+                part = turns[(q - g) % 4, pl.ds((4 * h + q) * gy * 3 + r, gy, stride=3), :]
+                row = jnp.where((lane >= 32 * q) & (lane < 32 * q + 32), part, row)
+            stage[h, pl.ds((i // 2) * width + i % 2, gy, stride=2), :] = row
+        t = stage[h].T
+        for q in range(min(4, gx - 4 * h)):
+            for x in range(2):
+                at = 2 * (4 * h + q) + x
+                rows = t[32 * q + 16 * x : 32 * q + 16 * x + 16]
+                own[at] = rows
+                lo4[at] = rows[0:4]
+                hi4[at] = rows[12:16]
 
 
 def restrict_whole(size_x, off, width, w, beta, root, rsum, csum, rz, cz):
@@ -438,30 +448,23 @@
     loop(first, first + planes, body, unroll)
 
 
-def relax_kept(first, planes, width, src, dst, beta, root):
-    def body(x):
-        for r, n in chunks(48, 24):
-            mid, total = around_whole(src, x, 8 + r, n, width)
-            dst[x, pl.ds(8 + r, n), :] = jacobi(root[x, pl.ds(r, n), :] > 0.0, mid, beta[x, pl.ds(r, n), :], total)
-
-    loop(first, first + planes, body, planes)
-
-
-def coarse_kernel(gx, gy, own, zlo, zhi, w2, beta2, root2, e2, beta3, w3, v3, root3, beta4, w4, v4, root4, rsum, csum, rz, cz, v2, w2b, fine3, fine2):
+def coarse_kernel(gx, gy, own, below, above, below2, above2, e3, beta3, w3, v3, root3, beta4, w4, v4, root4, rsum, csum, rz, cz, fine3):
     size_x, width = 2 * gx, 2 * gy
     for ref in (beta3, w3, v3, root3, beta4, w4, v4):
         ref[...] = jnp.zeros_like(ref)
 
     def prepare(x, row, t):
         n = t.shape[0]
-        root_x, inv_x = roots_of(jnp.where(lane_of(n) < 4 * width, lane_roll(t, 64), 0.0))
+        root_x, inv_x = roots_of(four_fields(t, width))
         root3[x + OFF3, pl.ds(row, n), :] = root_x
         beta3[x + OFF3, pl.ds(8 + row, n), :] = TAU * t * inv_x
 
     def setup(x):
-        prepare(x, 24 - HZ3, zlo[x])
-        prepare(x, 24, own[x, pl.ds(8, 16), :])
-        prepare(x, 40, zhi[x])
+        prepare(x, 4, below2[x])
+        prepare(x, 8, below[x])
+        prepare(x, 24, own[x])
+        prepare(x, 40, above[x])
+        prepare(x, 56, above2[x])
 
     loop(0, size_x, setup, 4)
 
@@ -495,41 +498,59 @@
     relax_whole(OFF3, size_x, 16, 32, width, v3, w3, beta3, root3, 4)
 
     first3 = 2 * position("gx") - 2 + OFF3
-    e3 = [w3[first3 + k, pl.ds(28, 24), :] * inverse(root3[first3 + k, pl.ds(20, 24), :]) for k in range(6)]
-    e3 = mm(((jnp.concatenate(e3, axis=0), repeat_lanes(width, 2 * width)),))
     for k in range(6):
-        unfold_rows(fine2, k, 24, e3[k * 24 : (k + 1) * 24])
-    for p in range(12):
-        w2b[p, pl.ds(8, 48), :] = w2[p] + root2[p] * fine2[p // 2]
-        for ref in (w2b, v2):
-            ref[p, pl.ds(0, 8), :] = jnp.zeros((8, LANES), F32)
-            ref[p, pl.ds(56, 8), :] = jnp.zeros((8, LANES), F32)
-    relax_kept(1, 10, 2 * width, w2b, v2, beta2, root2)
-    relax_kept(2, 8, 2 * width, v2, w2b, beta2, root2)
-    for k in range(8):
-        e2[k] = w2b[k + 2, pl.ds(12, 40), :] * inverse(root2[k + 2, pl.ds(4, 40), :])
-
-
-def up_kernel(gy, e2, w1, beta1, root1, w0, beta0, root0, out, w1b, v1, w0b, v0, fine1, fine0, turned):
-    width = 4 * gy
-    source_lane = lax.broadcasted_iota(jnp.int32, (LANES, LANES), 0)
-    target_lane = lane_of(LANES)
-    wanted_y = 4 * position("gy") - 2 + ((target_lane & (Y1 - 1)) >> 1)
-    wanted = (target_lane >> 4) * width + wanted_y
-    valid = (source_lane == wanted) & (wanted_y >= 0) & (wanted_y < width) & (target_lane < 4 * Y1)
-    u2 = jnp.where(valid, 1.0, 0.0).astype(jnp.bfloat16)
+        e3[k] = w3[first3 + k, pl.ds(28, 24), :] * inverse(root3[first3 + k, pl.ds(20, 24), :])
+
+
+def up_kernel(gy, e3, b2, zlo2, zhi2, kept1, kept0, out, beta2, root2, w2, v2, fine2, w1b, v1, w0b, v0, fine1, fine0, turned):
+    w1, beta1, root1 = thirds(kept1)
+    w0, beta0, root0 = thirds(kept0)
+    for ref in (w2, v2):
+        ref[...] = jnp.zeros_like(ref)
+
+    def prepare(x, row, t):
+        n = t.shape[0]
+        root_x, inv_x = roots_of(four_fields(t, Y2))
+        root2[x, pl.ds(row, n), :] = root_x
+        beta2[x, pl.ds(8 + row, n), :] = TAU * t * inv_x
+
+    def setup(x):
+        beta2[x, pl.ds(0, 8), :] = jnp.zeros((8, LANES), F32)
+        beta2[x, pl.ds(56, 8), :] = jnp.zeros((8, LANES), F32)
+        prepare(x, 0, zlo2[x])
+        prepare(x, 8, b2[x])
+        prepare(x, 40, zhi2[x])
+
+    loop(0, 4 + 2 * H2, setup, 7)
+
+    repeat = repeat_local(2 * gy, 2 * position("gy") - 2, Y2, 1)
+    e = mm(((jnp.concatenate([e3[k] for k in range(6)], axis=0), repeat),))
+    for k in range(6):
+        unfold_rows(fine2, k, 24, e[k * 24 : (k + 1) * 24])
+    for x in range(1, 13):
+        mid, total = around(beta2, x, 8, 48)
+        root_x = root2[x]
+        add = root_x * fine2[(x - 1) // 2]
+        w2[x, pl.ds(8, 48), :] = jnp.where(root_x > 0.0, 1.2 * mid + TAU * total + add, 0.0)
+    for src, dst, begin, end in ((w2, v2, 2, 12), (v2, w2, 3, 11)):
+        for x in range(begin, end):
+            mid, total = around(src, x, 8, 48)
+            dst[x, pl.ds(8, 48), :] = jacobi(root2[x] > 0.0, mid, beta2[x, pl.ds(8, 48), :], total)
+
+    u2 = repeat_local(Y2, 2, Y1, 0)
     for ref in (w1b, v1):
         for row in (0, 88):
-            ref[:, pl.ds(row, 8), :] = jnp.zeros((16, 8, LANES), F32)
+            ref[:, pl.ds(row, 8), :] = jnp.zeros((20, 8, LANES), F32)
     for ref in (w0b, v0):
         for row in (0, 152):
             ref[:, pl.ds(row, 8), :] = jnp.zeros((20, 8, LANES), F32)
     for k in range(0, 8, 4):
-        e = mm(((jnp.concatenate([e2[k + i] for i in range(4)], axis=0), u2),))
+        e2 = [w2[x, pl.ds(12, 40), :] * inverse(root2[x, pl.ds(4, 40), :]) for x in range(k + 3, k + 7)]
+        e = mm(((jnp.concatenate(e2, axis=0), u2),))
         for i in range(4):
             unfold_rows(fine1, k + i, 40, e[i * 40 : (i + 1) * 40])
-    for x in range(1, 15):
-        w1b[x, pl.ds(8, 80), :] = w1[x, pl.ds(8, 80), :] + root1[x] * fine1[x // 2]
+    for x in range(3, 17):
+        w1b[x, pl.ds(8, 80), :] = w1[x, pl.ds(8, 80), :] + root1[x, pl.ds(0, 80), :] * fine1[x // 2 - 1]
 
     def relax1(src, dst, begin, end):
         def body(x):
@@ -540,12 +561,12 @@
 
         loop(begin, end, body, end - begin)
 
-    relax1(w1b, v1, 2, 14)
-    relax1(v1, w1b, 3, 13)
-
-    u1 = repeat_to_level0()
+    relax1(w1b, v1, 4, 16)
+    relax1(v1, w1b, 5, 15)
+
+    u1 = repeat_local(Y1, H1, Y0, HY0)
     for k in range(0, 10, 2):
-        e = [w1b[x, pl.ds(12, 72), :] * inverse(root1[x, pl.ds(4, 72), :]) for x in (k + 3, k + 4)]
+        e = [w1b[x, pl.ds(12, 72), :] * inverse(root1[x, pl.ds(4, 72), :]) for x in (k + 5, k + 6)]
         e = mm(((jnp.concatenate(e, axis=0), u1),))
         for i in range(2):
             unfold_rows(fine0, k + i, 72, e[i * 72 : (i + 1) * 72])
@@ -598,10 +619,10 @@
     )(*args)
 
 
-def swap(to_up, to_down, axis):
+def swap(to_up, to_down, axis, far=1):
     n = lax.axis_size(axis)
-    from_below = lax.ppermute(to_up, axis, [(i, i + 1) for i in range(n - 1)])
-    from_above = lax.ppermute(to_down, axis, [(i + 1, i) for i in range(n - 1)])
+    from_below = lax.ppermute(to_up, axis, [(i, i + far) for i in range(n - far)])
+    from_above = lax.ppermute(to_down, axis, [(i + far, i) for i in range(n - far)])
     return from_below, from_above
 
 
@@ -641,63 +662,62 @@
     zlo, zhi = swap(zsend_hi, zsend_lo, "gz")
 
     depth = 128 + 2 * HZ0
-    own1, ysend_lo, ysend_hi, w0, beta0, root0 = call(
+    own1, ysend_lo, ysend_hi, kept0 = call(
         down0_kernel,
         (turned, zlo, zhi),
-        [(8, 48, LANES)] + [(8, 24, LANES)] * 2 + [(planes, depth + 16, LANES)] * 2 + [(planes, depth, LANES)],
+        [(8, 48, LANES)] + [(8, 6 * H1, LANES)] * 2 + [(3 * planes, depth + 16, LANES)],
         [(8, depth, LANES)] * 2 + [(4 * depth, LANES)] * 2 + [(8, LANES, LANES)],
     )
     ylo, yhi = swap(ysend_hi, ysend_lo, "gy")
-    low, high = call(join_kernel, (own1, ylo, yhi), [(4, 96, LANES)] * 2, [])
+    turned1, low, high = call(
+        join1_kernel, (own1, ylo, yhi), [(8, 80, LANES)] + [(H1, 80, LANES)] * 2, [(4, LANES, LANES)]
+    )
     xlo, xhi = swap(high, low, "gx")
 
-    block, w1, beta1, root1 = call(
+    x1, x2, x3 = 8 + 2 * H1, 4 + 2 * H2, 2 * gx
+    block, turned2, ysend_lo, ysend_hi, kept1 = call(
         down1_kernel,
-        (own1, ylo, yhi, xlo, xhi),
-        [(gx * gy, 24, LANES), (16, 96, LANES), (16, 96, LANES), (16, 80, LANES)],
-        [(4, LANES, LANES)] + [(4, 64, LANES)] * 2 + [(LANES, LANES)] * 2,
-    )
+        (turned1, xlo, xhi),
+        [(3 * gx * gy, LANES), (6, 24, LANES)] + [(6, 6 * H2, LANES)] * 2 + [(3 * x1, 96, LANES)],
+        [(8, 80, LANES)] * 2
+        + [(320, LANES)] * 2
+        + [(8, 56, LANES), (8, 40, LANES), (8, 56, LANES), (4, LANES, LANES)],
+    )
+    ylo, yhi = swap(ysend_hi, ysend_lo, "gy")
     got = whole_plane(block)
-
-    x2, x3 = 4 * gx, 2 * gx
-    b2, c2, zsend_lo, zsend_hi = call(
+    turned2, low, high = call(
+        join2_kernel, (turned2, ylo, yhi), [(4, 32, LANES)] + [(H2, 32, LANES)] * 2, [(4, LANES, LANES)]
+    )
+    xlo, xhi = swap(high, low, "gx")
+    own3, lo4, hi4 = call(
         functools.partial(plane_kernel, gx, gy),
         (got,),
-        [(x2, 32, LANES)] * 2 + [(x2, 16, LANES)] * 2,
-        [(2, LANES, LANES)] * 2,
-    )
-    zlo, zhi = swap(zsend_hi, zsend_lo, "gz")
-
-    own3, zsend_up, zsend_down, w2, beta2, root2 = call(
-        functools.partial(down2_kernel, gx, gy),
-        (b2, c2, zlo, zhi),
-        [(x3, 32, LANES)] + [(x3, HZ3, LANES)] * 2 + [(12, 48, LANES)] * 3,
-        [(x2 + 2 * OFF2, 80, LANES)] * 2
-        + [(x2 + 2 * OFF2, 64, LANES)]
-        + [(x3, 64, LANES)] * 2
-        + [(x3 * 32, LANES)] * 2,
-    )
-    zlo, zhi = swap(zsend_up, zsend_down, "gz")
-
-    (e2,) = call(
+        [(x3, 16, LANES)] + [(x3, 4, LANES)] * 2,
+        [(4, 3 * gx * gy, LANES), (2, LANES, LANES)],
+    )
+    below, above = swap(own3, own3, "gz")
+    below2, above2 = swap(hi4, lo4, "gz", 2)
+    b2, zsend_lo, zsend_hi = call(join3_kernel, (turned2, xlo, xhi), [(x2, 32, LANES)] + [(x2, 8, LANES)] * 2, [])
+    zlo2, zhi2 = swap(zsend_hi, zsend_lo, "gz")
+    (e3,) = call(
         functools.partial(coarse_kernel, gx, gy),
-        (own3, zlo, zhi, w2, beta2, root2),
-        [(8, 40, LANES)],
+        (own3, below, above, below2, above2),
+        [(6, 24, LANES)],
         [(x3 + 2 * OFF3, 80, LANES)] * 3
         + [(x3 + 2 * OFF3, 64, LANES)]
         + [(gx + 2, 48, LANES)] * 3
         + [(gx + 2, 32, LANES)]
         + [(gx, 64, LANES)] * 2
         + [(gx * 32, LANES)] * 2
-        + [(12, 64, LANES)] * 2
-        + [(gx, 32, LANES), (6, 48, LANES)],
+        + [(gx, 32, LANES)],
     )
 
     (correction,) = call(
         functools.partial(up_kernel, gy),
-        (e2, w1, beta1, root1, w0, beta0, root0),
+        (e3, b2, zlo2, zhi2, kept1, kept0),
         [(4, 16, 16, LANES)],
-        [(16, 96, LANES)] * 2
+        [(x2, 64, LANES), (x2, 48, LANES), (x2, 64, LANES), (x2, 64, LANES), (6, 48, LANES)]
+        + [(x1, 96, LANES)] * 2
         + [(20, 160, LANES)] * 2
         + [(8, 80, LANES), (10, 144, LANES), (4, LANES, LANES)],
     )

time: 142 us -> 143 us (level)
  the two profiles are of different devices: /device:TPU:261 before, /device:TPU:185 now
where the time goes in v5:
time: 143 us
  starting transfers between devices  77.6 us (54%)
  waiting for transfers between devices  35.7 us (25%)
  Pallas kernels  18.8 us (13%)
  local copies, waits for them, and re-layouts  10.2 us (7%)
    ppermute x10, starting transfers between devices, swap(): lax.ppermute(to_up, axis, [(i, i + far) for i in range(n - far)])  36.7 us
    ppermute x10, starting transfers between devices, swap(): lax.ppermute(to_down, axis, [(i + far, i) for i in range(n - far)])  29.9 us
    ppermute x10, waiting for transfers between devices, swap(): lax.ppermute(to_down, axis, [(i + far, i) for i in range(n - far)])  29.9 us
    pallas_call x10, Pallas kernels, call(): pl.pallas_call(kernel, out_shape=[jax.ShapeDtypeStruct(s, F32) for s in o...  18.2 us
    all_to_all x1, starting transfers between devices, whole_plane(): return lax.all_to_all(block, ('gx', 'gy'), 0, 0, tiled=True)  10.9 us
    unnamed x12, local copies, waits for them, and re-layouts  8.51 us
    ppermute x10, waiting for transfers between devices, swap(): lax.ppermute(to_up, axis, [(i, i + far) for i in range(n - far)])  5.85 us
  transfers between devices with their start and end apart: 21, of which 13 were waited for; matrix products, arithmetic and copies ran while one was open for 0% of the time, Pallas kernels for 3%

profile of v5, /device:TPU:185, one launch (start us, length us, event | category | flops | bytes accessed | tf_op | source)
XLA Modules:
  0.0 142.6 jit_solution(13711012527068218994)
XLA Ops:
  0.0 1.0 copy-done.2
  1.0 0.9 copy-done.3
  1.9 0.7 copy-done.4
  2.6 0.7 copy-done.5
  3.3 0.7 shard_map.46
  4.0 2.2 %collective-permute-start = (f32[5,3,16,128]{3,2,1,0:T(8,128)S(1)}, f32[5,3,16,128]{3,2,1,0:T(8,128)S(1)}, u32[]{:S(2)}, u32[]{:S(2)}) collective-permute-start(f32[5,3,16,128]{3,2,1,0:T(8,128)S(1)} %get-tuple-element.34), channel_id=1, source_target_pairs={{0,128},{128,256},{256,384},{384,512},{512,640},{640,768},{768,896... | collective-permute-start | bytes 368648 | tf_op jit(solution)/shard_map/ppermute | solution.py:624
  6.2 4.3 %collective-permute-start.1 = (f32[5,3,16,128]{3,2,1,0:T(8,128)S(1)}, f32[5,3,16,128]{3,2,1,0:T(8,128)S(1)}, u32[]{:S(2)}, u32[]{:S(2)}) collective-permute-start(f32[5,3,16,128]{3,2,1,0:T(8,128)S(1)} %get-tuple-element.36), channel_id=1, source_target_pairs={{128,0},{256,128},{384,256},{512,384},{640,512},{768,640},{896,768... | collective-permute-start | bytes 368648 | tf_op jit(solution)/shard_map/ppermute | solution.py:625
  10.5 0.8 collective-permute-done.xlo
  11.3 1.1 collective-permute-done.1.xhi
  12.4 4.5 %collective-permute-start.2 = (f32[22,15,128]{2,1,0:T(8,128)S(1)}, f32[22,15,128]{2,1,0:T(8,128)S(1)}, u32[]{:S(2)}, u32[]{:S(2)}) collective-permute-start(f32[22,15,128]{2,1,0:T(8,128)S(1)} %get-tuple-element.37), channel_id=1, source_target_pairs={{0,16},{16,32},{32,48},{48,64},{64,80},{80,96},{96,112},{1,17},{17... | collective-permute-start | bytes 506888 | tf_op jit(solution)/shard_map/ppermute | solution.py:624
  16.9 1.9 %collective-permute-start.3 = (f32[22,15,128]{2,1,0:T(8,128)S(1)}, f32[22,15,128]{2,1,0:T(8,128)S(1)}, u32[]{:S(2)}, u32[]{:S(2)}) collective-permute-start(f32[22,15,128]{2,1,0:T(8,128)S(1)} %get-tuple-element.38), channel_id=1, source_target_pairs={{16,0},{32,16},{48,32},{64,48},{80,64},{96,80},{112,96},{17,1},{33... | collective-permute-start | bytes 506888 | tf_op jit(solution)/shard_map/ppermute | solution.py:625
  18.9 0.5 collective-permute-done.2.ylo
  19.3 5.0 %collective-permute-done.3.yhi = f32[22,15,128]{2,1,0:T(8,128)S(1)} collective-permute-done((f32[22,15,128]{2,1,0:T(8,128)S(1)}, f32[22,15,128]{2,1,0:T(8,128)S(1)}, u32[]{:S(2)}, u32[]{:S(2)}) %collective-permute-start.3) | collective-permute-done | bytes 168992 | tf_op jit(solution)/shard_map/ppermute | solution.py:625
  24.4 0.7 shard_map.48
  25.1 8.0 %collective-permute-start.4 = (f32[22,16,128]{2,1,0:T(8,128)S(1)}, f32[22,16,128]{2,1,0:T(8,128)S(1)}, u32[]{:S(2)}, u32[]{:S(2)}) collective-permute-start(f32[22,16,128]{2,1,0:T(8,128)S(1)} %get-tuple-element.40), channel_id=1, source_target_pairs={{0,1},{1,2},{2,3},{3,4},{4,5},{5,6},{6,7},{7,8},{8,9},{9,10},{10,1... | collective-permute-start | bytes 540680 | tf_op jit(solution)/shard_map/ppermute | solution.py:624
  33.1 1.9 %collective-permute-start.5 = (f32[22,16,128]{2,1,0:T(8,128)S(1)}, f32[22,16,128]{2,1,0:T(8,128)S(1)}, u32[]{:S(2)}, u32[]{:S(2)}) collective-permute-start(f32[22,16,128]{2,1,0:T(8,128)S(1)} %get-tuple-element.41), channel_id=1, source_target_pairs={{1,0},{2,1},{3,2},{4,3},{5,4},{6,5},{7,6},{8,7},{9,8},{10,9},{11,1... | collective-permute-start | bytes 540680 | tf_op jit(solution)/shard_map/ppermute | solution.py:625
  35.0 0.5 collective-permute-done.4.zlo
  35.5 4.4 %collective-permute-done.5.zhi = f32[22,16,128]{2,1,0:T(8,128)S(1)} collective-permute-done((f32[22,16,128]{2,1,0:T(8,128)S(1)}, f32[22,16,128]{2,1,0:T(8,128)S(1)}, u32[]{:S(2)}, u32[]{:S(2)}) %collective-permute-start.5) | collective-permute-done | bytes 180256 | tf_op jit(solution)/shard_map/ppermute | solution.py:625
  39.9 5.4 %shard_map.49 = (f32[8,48,128]{2,1,0:T(8,128)S(1)}, f32[8,36,128]{2,1,0:T(8,128)S(1)}, f32[8,36,128]{2,1,0:T(8,128)S(1)}, f32[66,176,128]{2,1,0:T(8,128)S(1)}) custom-call(f32[22,128,128]{2,1,0:T(8,128)S(1)} %get-tuple-element.39.turned, f32[22,16,128]{2,1,0:T(8,128)S(1)} %collective-permute-done.4.zlo, f32[22,16,128]{2,1,0:T(8,128)S(1)} %collective-permute-done.5.zhi), custom_call_target="tpu_custom_call" | custom-call | tf_op jit(solution)/shard_map/pallas_call | solution.py:612
  45.3 2.5 %copy-done = f32[66,176,128]{2,1,0:T(8,128)} copy-done((f32[66,176,128]{2,1,0:T(8,128)}, f32[66,176,128]{2,1,0:T(8,128)S(1)}, u32[]{:S(2)}) %copy-start) | copy-done | bytes 5947416
  47.9 1.9 %collective-permute-start.6 = (f32[8,36,128]{2,1,0:T(8,128)S(1)}, f32[8,36,128]{2,1,0:T(8,128)S(1)}, u32[]{:S(2)}, u32[]{:S(2)}) collective-permute-start(f32[8,36,128]{2,1,0:T(8,128)S(1)} %get-tuple-element.43), channel_id=1, source_target_pairs={{0,16},{16,32},{32,48},{48,64},{64,80},{80,96},{96,112},{1,17},{17... | collective-permute-start | bytes 442376 | tf_op jit(solution)/shard_map/ppermute | solution.py:624
  49.8 3.4 %collective-permute-start.7 = (f32[8,36,128]{2,1,0:T(8,128)S(1)}, f32[8,36,128]{2,1,0:T(8,128)S(1)}, u32[]{:S(2)}, u32[]{:S(2)}) collective-permute-start(f32[8,36,128]{2,1,0:T(8,128)S(1)} %get-tuple-element.44), channel_id=1, source_target_pairs={{16,0},{32,16},{48,32},{64,48},{80,64},{96,80},{112,96},{17,1},{33... | collective-permute-start | bytes 442376 | tf_op jit(solution)/shard_map/ppermute | solution.py:625
  53.2 1.1 collective-permute-done.6.ylo
  54.2 2.8 %collective-permute-done.7.yhi = f32[8,36,128]{2,1,0:T(8,128)S(1)} collective-permute-done((f32[8,36,128]{2,1,0:T(8,128)S(1)}, f32[8,36,128]{2,1,0:T(8,128)S(1)}, u32[]{:S(2)}, u32[]{:S(2)}) %collective-permute-start.7) | collective-permute-done | bytes 147488 | tf_op jit(solution)/shard_map/ppermute | solution.py:625
  57.3 2.0 %collective-permute-start.8 = (f32[6,80,128]{2,1,0:T(8,128)S(1)}, f32[6,80,128]{2,1,0:T(8,128)S(1)}, u32[]{:S(2)}, u32[]{:S(2)}) collective-permute-start(f32[6,80,128]{2,1,0:T(8,128)S(1)} %get-tuple-element.46), channel_id=1, source_target_pairs={{0,128},{128,256},{256,384},{384,512},{512,640},{640,768},{768,896... | collective-permute-start | bytes 737288 | tf_op jit(solution)/shard_map/ppermute | solution.py:624
  59.3 5.2 %collective-permute-start.9 = (f32[6,80,128]{2,1,0:T(8,128)S(1)}, f32[6,80,128]{2,1,0:T(8,128)S(1)}, u32[]{:S(2)}, u32[]{:S(2)}) collective-permute-start(f32[6,80,128]{2,1,0:T(8,128)S(1)} %get-tuple-element.47), channel_id=1, source_target_pairs={{128,0},{256,128},{384,256},{512,384},{640,512},{768,640},{896,768... | collective-permute-start | bytes 737288 | tf_op jit(solution)/shard_map/ppermute | solution.py:625
  64.5 2.6 %collective-permute-done.8.xlo = f32[6,80,128]{2,1,0:T(8,128)S(1)} collective-permute-done((f32[6,80,128]{2,1,0:T(8,128)S(1)}, f32[6,80,128]{2,1,0:T(8,128)S(1)}, u32[]{:S(2)}, u32[]{:S(2)}) %collective-permute-start.8) | collective-permute-done | bytes 245792 | tf_op jit(solution)/shard_map/ppermute | solution.py:624
  67.1 1.8 %collective-permute-done.9.xhi = f32[6,80,128]{2,1,0:T(8,128)S(1)} collective-permute-done((f32[6,80,128]{2,1,0:T(8,128)S(1)}, f32[6,80,128]{2,1,0:T(8,128)S(1)}, u32[]{:S(2)}, u32[]{:S(2)}) %collective-permute-start.9) | collective-permute-done | bytes 245792 | tf_op jit(solution)/shard_map/ppermute | solution.py:625
  68.8 2.6 %shard_map.51 = (f32[192,128]{1,0:T(8,128)S(1)}, f32[6,24,128]{2,1,0:T(8,128)S(1)}, f32[6,30,128]{2,1,0:T(8,128)S(1)}, f32[6,30,128]{2,1,0:T(8,128)S(1)}, f32[60,96,128]{2,1,0:T(8,128)S(1)}) custom-call(f32[8,80,128]{2,1,0:T(8,128)S(1)} %get-tuple-element.45.own, f32[6,80,128]{2,1,0:T(8,128)S(1)} %collective-permute-done.8.xlo, ...), custom_call_target="tpu_custom_call" | custom-call | tf_op jit(solution)/shard_map/pallas_call | solution.py:612
  71.4 0.7 all_to_all.7
  72.1 10.9 %all-to-all-start = ((f32[64,3,128]{2,1,0:T(4,128)}), f32[64,3,128]{2,1,0:T(4,128)}, u32[]{:S(2)}, u32[]{:S(2)}) async-start(f32[64,3,128]{2,1,0:T(4,128)} %all_to_all.7), calls=%async_computation | async-start | bytes 262144 | tf_op jit(solution)/shard_map/all_to_all | solution.py:630
  83.1 4.3 %collective-permute-start.14 = (f32[6,30,128]{2,1,0:T(8,128)S(1)}, f32[6,30,128]{2,1,0:T(8,128)S(1)}, u32[]{:S(2)}, u32[]{:S(2)}) collective-permute-start(f32[6,30,128]{2,1,0:T(8,128)S(1)} %get-tuple-element.53), channel_id=1, source_target_pairs={{0,16},{16,32},{32,48},{48,64},{64,80},{80,96},{96,112},{1,17},{17... | collective-permute-start | bytes 276488 | tf_op jit(solution)/shard_map/ppermute | solution.py:624
  87.4 1.9 %collective-permute-start.15 = (f32[6,30,128]{2,1,0:T(8,128)S(1)}, f32[6,30,128]{2,1,0:T(8,128)S(1)}, u32[]{:S(2)}, u32[]{:S(2)}) collective-permute-start(f32[6,30,128]{2,1,0:T(8,128)S(1)} %get-tuple-element.54), channel_id=1, source_target_pairs={{16,0},{32,16},{48,32},{64,48},{80,64},{96,80},{112,96},{17,1},{33... | collective-permute-start | bytes 276488 | tf_op jit(solution)/shard_map/ppermute | solution.py:625
  89.3 0.5 collective-permute-done.14.ylo
  89.8 5.1 %collective-permute-done.15.yhi = f32[6,30,128]{2,1,0:T(8,128)S(1)} collective-permute-done((f32[6,30,128]{2,1,0:T(8,128)S(1)}, f32[6,30,128]{2,1,0:T(8,128)S(1)}, u32[]{:S(2)}, u32[]{:S(2)}) %collective-permute-start.15) | collective-permute-done | bytes 92192 | tf_op jit(solution)/shard_map/ppermute | solution.py:625
  95.1 2.2 %collective-permute-start.16 = (f32[5,32,128]{2,1,0:T(8,128)S(1)}, f32[5,32,128]{2,1,0:T(8,128)S(1)}, u32[]{:S(2)}, u32[]{:S(2)}) collective-permute-start(f32[5,32,128]{2,1,0:T(8,128)S(1)} %get-tuple-element.56), channel_id=1, source_target_pairs={{0,128},{128,256},{256,384},{384,512},{512,640},{640,768},{768,896... | collective-permute-start | bytes 245768 | tf_op jit(solution)/shard_map/ppermute | solution.py:624
  97.3 4.2 %collective-permute-start.17 = (f32[5,32,128]{2,1,0:T(8,128)S(1)}, f32[5,32,128]{2,1,0:T(8,128)S(1)}, u32[]{:S(2)}, u32[]{:S(2)}) collective-permute-start(f32[5,32,128]{2,1,0:T(8,128)S(1)} %get-tuple-element.57), channel_id=1, source_target_pairs={{128,0},{256,128},{384,256},{512,384},{640,512},{768,640},{896,768... | collective-permute-start | bytes 245768 | tf_op jit(solution)/shard_map/ppermute | solution.py:625
  101.6 1.0 all_to_all.9.got
  102.8 3.3 %collective-permute-start.11 = (f32[16,16,128]{2,1,0:T(8,128)S(1)}, f32[16,16,128]{2,1,0:T(8,128)S(1)}, u32[]{:S(2)}, u32[]{:S(2)}) collective-permute-start(f32[16,16,128]{2,1,0:T(8,128)S(1)} %get-tuple-element.49.own), channel_id=1, source_target_pairs={{1,0},{2,1},{3,2},{4,3},{5,4},{6,5},{7,6},{8,7},{9,8},{10,9},{11,1... | collective-permute-start | bytes 393224 | tf_op jit(solution)/shard_map/ppermute | solution.py:625
  106.1 4.8 %collective-permute-start.10 = (f32[16,16,128]{2,1,0:T(8,128)S(1)}, f32[16,16,128]{2,1,0:T(8,128)S(1)}, u32[]{:S(2)}, u32[]{:S(2)}) collective-permute-start(f32[16,16,128]{2,1,0:T(8,128)S(1)} %get-tuple-element.49.own), channel_id=1, source_target_pairs={{0,1},{1,2},{2,3},{3,4},{4,5},{5,6},{6,7},{7,8},{8,9},{9,10},{10,1... | collective-permute-start | bytes 393224 | tf_op jit(solution)/shard_map/ppermute | solution.py:624
  110.9 4.0 %collective-permute-start.12 = (f32[16,4,128]{2,1,0:T(4,128)S(1)}, f32[16,4,128]{2,1,0:T(4,128)S(1)}, u32[]{:S(2)}, u32[]{:S(2)}) collective-permute-start(f32[16,4,128]{2,1,0:T(4,128)S(1)} %get-tuple-element.50), channel_id=1, source_target_pairs={{0,2},{1,3},{2,4},{3,5},{4,6},{5,7},{6,8},{7,9},{8,10},{9,11},{10,... | collective-permute-start | bytes 98312 | tf_op jit(solution)/shard_map/ppermute | solution.py:624
  114.9 2.7 %collective-permute-start.18 = (f32[14,8,128]{2,1,0:T(8,128)S(1)}, f32[14,8,128]{2,1,0:T(8,128)S(1)}, u32[]{:S(2)}, u32[]{:S(2)}) collective-permute-start(f32[14,8,128]{2,1,0:T(8,128)S(1)} %get-tuple-element.59), channel_id=1, source_target_pairs={{0,1},{1,2},{2,3},{3,4},{4,5},{5,6},{6,7},{7,8},{8,9},{9,10},{10,1... | collective-permute-start | bytes 172040 | tf_op jit(solution)/shard_map/ppermute | solution.py:624
  117.6 1.9 %collective-permute-start.19 = (f32[14,8,128]{2,1,0:T(8,128)S(1)}, f32[14,8,128]{2,1,0:T(8,128)S(1)}, u32[]{:S(2)}, u32[]{:S(2)}) collective-permute-start(f32[14,8,128]{2,1,0:T(8,128)S(1)} %get-tuple-element.60), channel_id=1, source_target_pairs={{1,0},{2,1},{3,2},{4,3},{5,4},{6,5},{7,6},{8,7},{9,8},{10,9},{11,1... | collective-permute-start | bytes 172040 | tf_op jit(solution)/shard_map/ppermute | solution.py:625
  119.6 1.9 %collective-permute-start.13 = (f32[16,4,128]{2,1,0:T(4,128)S(1)}, f32[16,4,128]{2,1,0:T(4,128)S(1)}, u32[]{:S(2)}, u32[]{:S(2)}) collective-permute-start(f32[16,4,128]{2,1,0:T(4,128)S(1)} %get-tuple-element.51), channel_id=1, source_target_pairs={{2,0},{3,1},{4,2},{5,3},{6,4},{7,5},{8,6},{9,7},{10,8},{11,9},{12,... | collective-permute-start | bytes 98312 | tf_op jit(solution)/shard_map/ppermute | solution.py:625
  121.5 9.6 %collective-permute-done.13.above2 = f32[16,4,128]{2,1,0:T(4,128)S(1)} collective-permute-done((f32[16,4,128]{2,1,0:T(4,128)S(1)}, f32[16,4,128]{2,1,0:T(4,128)S(1)}, u32[]{:S(2)}, u32[]{:S(2)}) %collective-permute-start.13) | collective-permute-done | bytes 32800 | tf_op jit(solution)/shard_map/ppermute | solution.py:625
  131.1 3.8 %shard_map.53.e3 = f32[6,24,128]{2,1,0:T(8,128)S(1)} custom-call(f32[16,16,128]{2,1,0:T(8,128)S(1)} %get-tuple-element.49.own, f32[16,16,128]{2,1,0:T(8,128)S(1)} %collective-permute-done.10.below, f32[16,16,128]{2,1,0:T(8,128)S(1)} %collective-permute-done.11.above, f32[16,4,128]{2,1,0:T(4,128)S(1)} %collective-permute-done.12.below2, ...), custom_call_target="tpu_custom_call" | custom-call | tf_op jit(solution)/shard_map/pallas_call | solution.py:612
  135.0 2.7 %copy-done.1 = f32[66,176,128]{2,1,0:T(8,128)S(1)} copy-done((f32[66,176,128]{2,1,0:T(8,128)S(1)}, f32[66,176,128]{2,1,0:T(8,128)}, u32[]{:S(2)}) %copy-start.1) | copy-done | bytes 5947416
  137.7 4.9 %shard_map.56 = f32[4,16,16,128]{3,2,1,0:T(8,128)} custom-call(f32[6,24,128]{2,1,0:T(8,128)S(1)} %shard_map.53.e3, f32[14,32,128]{2,1,0:T(8,128)S(1)} %get-tuple-element.58.b2, f32[14,8,128]{2,1,0:T(8,128)S(1)} %collective-permute-done.18.zlo2, f32[14,8,128]{2,1,0:T(8,128)S(1)} %collective-permute-done.19.zhi2, f32[60,96,128]{2,1,0:T(8,128)S(1)} %get-tuple-element.61.kept1, ...), custom_call_target="tpu_custom_call" | custom-call | tf_op jit(solution)/shard_map/pallas_call | solution.py:612
  (19 shorter events, 0.8 us)
Async XLA Ops:
  0.0 1.0 copy-start.2
  1.0 0.9 copy-start.3
  1.9 0.7 copy-start.4
  2.6 0.7 copy-start.5
  4.0 7.3 %collective-permute-start = (f32[5,3,16,128]{3,2,1,0:T(8,128)S(1)}, f32[5,3,16,128]{3,2,1,0:T(8,128)S(1)}, u32[]{:S(2)}, u32[]{:S(2)}) collective-permute-start(f32[5,3,16,128]{3,2,1,0:T(8,128)S(1)} %get-tuple-element.34), channel_id=1, source_target_pairs={{0,128},{128,256},{256,384},{384,512},{512,640},{640,768},{768,896... | collective-permute-start | bytes 368648 | tf_op jit(solution)/shard_map/ppermute | solution.py:624
  6.2 6.1 %collective-permute-start.1 = (f32[5,3,16,128]{3,2,1,0:T(8,128)S(1)}, f32[5,3,16,128]{3,2,1,0:T(8,128)S(1)}, u32[]{:S(2)}, u32[]{:S(2)}) collective-permute-start(f32[5,3,16,128]{3,2,1,0:T(8,128)S(1)} %get-tuple-element.36), channel_id=1, source_target_pairs={{128,0},{256,128},{384,256},{512,384},{640,512},{768,640},{896,768... | collective-permute-start | bytes 368648 | tf_op jit(solution)/shard_map/ppermute | solution.py:625
  12.4 7.0 %collective-permute-start.2 = (f32[22,15,128]{2,1,0:T(8,128)S(1)}, f32[22,15,128]{2,1,0:T(8,128)S(1)}, u32[]{:S(2)}, u32[]{:S(2)}) collective-permute-start(f32[22,15,128]{2,1,0:T(8,128)S(1)} %get-tuple-element.37), channel_id=1, source_target_pairs={{0,16},{16,32},{32,48},{48,64},{64,80},{80,96},{96,112},{1,17},{17... | collective-permute-start | bytes 506888 | tf_op jit(solution)/shard_map/ppermute | solution.py:624
  16.9 7.4 %collective-permute-start.3 = (f32[22,15,128]{2,1,0:T(8,128)S(1)}, f32[22,15,128]{2,1,0:T(8,128)S(1)}, u32[]{:S(2)}, u32[]{:S(2)}) collective-permute-start(f32[22,15,128]{2,1,0:T(8,128)S(1)} %get-tuple-element.38), channel_id=1, source_target_pairs={{16,0},{32,16},{48,32},{64,48},{80,64},{96,80},{112,96},{17,1},{33... | collective-permute-start | bytes 506888 | tf_op jit(solution)/shard_map/ppermute | solution.py:625
  25.1 10.5 %collective-permute-start.4 = (f32[22,16,128]{2,1,0:T(8,128)S(1)}, f32[22,16,128]{2,1,0:T(8,128)S(1)}, u32[]{:S(2)}, u32[]{:S(2)}) collective-permute-start(f32[22,16,128]{2,1,0:T(8,128)S(1)} %get-tuple-element.40), channel_id=1, source_target_pairs={{0,1},{1,2},{2,3},{3,4},{4,5},{5,6},{6,7},{7,8},{8,9},{9,10},{10,1... | collective-permute-start | bytes 540680 | tf_op jit(solution)/shard_map/ppermute | solution.py:624
  33.1 6.8 %collective-permute-start.5 = (f32[22,16,128]{2,1,0:T(8,128)S(1)}, f32[22,16,128]{2,1,0:T(8,128)S(1)}, u32[]{:S(2)}, u32[]{:S(2)}) collective-permute-start(f32[22,16,128]{2,1,0:T(8,128)S(1)} %get-tuple-element.41), channel_id=1, source_target_pairs={{1,0},{2,1},{3,2},{4,3},{5,4},{6,5},{7,6},{8,7},{9,8},{10,9},{11,1... | collective-permute-start | bytes 540680 | tf_op jit(solution)/shard_map/ppermute | solution.py:625
  45.3 2.6 %copy-start = (f32[66,176,128]{2,1,0:T(8,128)}, f32[66,176,128]{2,1,0:T(8,128)S(1)}, u32[]{:S(2)}) copy-start(f32[66,176,128]{2,1,0:T(8,128)S(1)} %get-tuple-element.62.kept0) | copy-start | bytes 17842180
  47.9 6.3 %collective-permute-start.6 = (f32[8,36,128]{2,1,0:T(8,128)S(1)}, f32[8,36,128]{2,1,0:T(8,128)S(1)}, u32[]{:S(2)}, u32[]{:S(2)}) collective-permute-start(f32[8,36,128]{2,1,0:T(8,128)S(1)} %get-tuple-element.43), channel_id=1, source_target_pairs={{0,16},{16,32},{32,48},{48,64},{64,80},{80,96},{96,112},{1,17},{17... | collective-permute-start | bytes 442376 | tf_op jit(solution)/shard_map/ppermute | solution.py:624
  49.8 7.3 %collective-permute-start.7 = (f32[8,36,128]{2,1,0:T(8,128)S(1)}, f32[8,36,128]{2,1,0:T(8,128)S(1)}, u32[]{:S(2)}, u32[]{:S(2)}) collective-permute-start(f32[8,36,128]{2,1,0:T(8,128)S(1)} %get-tuple-element.44), channel_id=1, source_target_pairs={{16,0},{32,16},{48,32},{64,48},{80,64},{96,80},{112,96},{17,1},{33... | collective-permute-start | bytes 442376 | tf_op jit(solution)/shard_map/ppermute | solution.py:625
  57.3 9.8 %collective-permute-start.8 = (f32[6,80,128]{2,1,0:T(8,128)S(1)}, f32[6,80,128]{2,1,0:T(8,128)S(1)}, u32[]{:S(2)}, u32[]{:S(2)}) collective-permute-start(f32[6,80,128]{2,1,0:T(8,128)S(1)} %get-tuple-element.46), channel_id=1, source_target_pairs={{0,128},{128,256},{256,384},{384,512},{512,640},{640,768},{768,896... | collective-permute-start | bytes 737288 | tf_op jit(solution)/shard_map/ppermute | solution.py:624
  59.3 9.5 %collective-permute-start.9 = (f32[6,80,128]{2,1,0:T(8,128)S(1)}, f32[6,80,128]{2,1,0:T(8,128)S(1)}, u32[]{:S(2)}, u32[]{:S(2)}) collective-permute-start(f32[6,80,128]{2,1,0:T(8,128)S(1)} %get-tuple-element.47), channel_id=1, source_target_pairs={{128,0},{256,128},{384,256},{512,384},{640,512},{768,640},{896,768... | collective-permute-start | bytes 737288 | tf_op jit(solution)/shard_map/ppermute | solution.py:625
  72.1 29.4 %all-to-all-start = ((f32[64,3,128]{2,1,0:T(4,128)}), f32[64,3,128]{2,1,0:T(4,128)}, u32[]{:S(2)}, u32[]{:S(2)}) async-start(f32[64,3,128]{2,1,0:T(4,128)} %all_to_all.7), calls=%async_computation | async-start | bytes 262144 | tf_op jit(solution)/shard_map/all_to_all | solution.py:630
  83.1 6.7 %collective-permute-start.14 = (f32[6,30,128]{2,1,0:T(8,128)S(1)}, f32[6,30,128]{2,1,0:T(8,128)S(1)}, u32[]{:S(2)}, u32[]{:S(2)}) collective-permute-start(f32[6,30,128]{2,1,0:T(8,128)S(1)} %get-tuple-element.53), channel_id=1, source_target_pairs={{0,16},{16,32},{32,48},{48,64},{64,80},{80,96},{96,112},{1,17},{17... | collective-permute-start | bytes 276488 | tf_op jit(solution)/shard_map/ppermute | solution.py:624
  87.4 7.5 %collective-permute-start.15 = (f32[6,30,128]{2,1,0:T(8,128)S(1)}, f32[6,30,128]{2,1,0:T(8,128)S(1)}, u32[]{:S(2)}, u32[]{:S(2)}) collective-permute-start(f32[6,30,128]{2,1,0:T(8,128)S(1)} %get-tuple-element.54), channel_id=1, source_target_pairs={{16,0},{32,16},{48,32},{64,48},{80,64},{96,80},{112,96},{17,1},{33... | collective-permute-start | bytes 276488 | tf_op jit(solution)/shard_map/ppermute | solution.py:625
  95.1 19.8 %collective-permute-start.16 = (f32[5,32,128]{2,1,0:T(8,128)S(1)}, f32[5,32,128]{2,1,0:T(8,128)S(1)}, u32[]{:S(2)}, u32[]{:S(2)}) collective-permute-start(f32[5,32,128]{2,1,0:T(8,128)S(1)} %get-tuple-element.56), channel_id=1, source_target_pairs={{0,128},{128,256},{256,384},{384,512},{512,640},{640,768},{768,896... | collective-permute-start | bytes 245768 | tf_op jit(solution)/shard_map/ppermute | solution.py:624
  97.3 17.6 %collective-permute-start.17 = (f32[5,32,128]{2,1,0:T(8,128)S(1)}, f32[5,32,128]{2,1,0:T(8,128)S(1)}, u32[]{:S(2)}, u32[]{:S(2)}) collective-permute-start(f32[5,32,128]{2,1,0:T(8,128)S(1)} %get-tuple-element.57), channel_id=1, source_target_pairs={{128,0},{256,128},{384,256},{512,384},{640,512},{768,640},{896,768... | collective-permute-start | bytes 245768 | tf_op jit(solution)/shard_map/ppermute | solution.py:625
  102.8 28.3 %collective-permute-start.11 = (f32[16,16,128]{2,1,0:T(8,128)S(1)}, f32[16,16,128]{2,1,0:T(8,128)S(1)}, u32[]{:S(2)}, u32[]{:S(2)}) collective-permute-start(f32[16,16,128]{2,1,0:T(8,128)S(1)} %get-tuple-element.49.own), channel_id=1, source_target_pairs={{1,0},{2,1},{3,2},{4,3},{5,4},{6,5},{7,6},{8,7},{9,8},{10,9},{11,1... | collective-permute-start | bytes 393224 | tf_op jit(solution)/shard_map/ppermute | solution.py:625
  106.1 25.1 %collective-permute-start.10 = (f32[16,16,128]{2,1,0:T(8,128)S(1)}, f32[16,16,128]{2,1,0:T(8,128)S(1)}, u32[]{:S(2)}, u32[]{:S(2)}) collective-permute-start(f32[16,16,128]{2,1,0:T(8,128)S(1)} %get-tuple-element.49.own), channel_id=1, source_target_pairs={{0,1},{1,2},{2,3},{3,4},{4,5},{5,6},{6,7},{7,8},{8,9},{9,10},{10,1... | collective-permute-start | bytes 393224 | tf_op jit(solution)/shard_map/ppermute | solution.py:624
  110.9 8.7 %collective-permute-start.12 = (f32[16,4,128]{2,1,0:T(4,128)S(1)}, f32[16,4,128]{2,1,0:T(4,128)S(1)}, u32[]{:S(2)}, u32[]{:S(2)}) collective-permute-start(f32[16,4,128]{2,1,0:T(4,128)S(1)} %get-tuple-element.50), channel_id=1, source_target_pairs={{0,2},{1,3},{2,4},{3,5},{4,6},{5,7},{6,8},{7,9},{8,10},{9,11},{10,... | collective-permute-start | bytes 98312 | tf_op jit(solution)/shard_map/ppermute | solution.py:624
  114.9 20.0 %collective-permute-start.18 = (f32[14,8,128]{2,1,0:T(8,128)S(1)}, f32[14,8,128]{2,1,0:T(8,128)S(1)}, u32[]{:S(2)}, u32[]{:S(2)}) collective-permute-start(f32[14,8,128]{2,1,0:T(8,128)S(1)} %get-tuple-element.59), channel_id=1, source_target_pairs={{0,1},{1,2},{2,3},{3,4},{4,5},{5,6},{6,7},{7,8},{8,9},{9,10},{10,1... | collective-permute-start | bytes 172040 | tf_op jit(solution)/shard_map/ppermute | solution.py:624
  117.6 17.3 %collective-permute-start.19 = (f32[14,8,128]{2,1,0:T(8,128)S(1)}, f32[14,8,128]{2,1,0:T(8,128)S(1)}, u32[]{:S(2)}, u32[]{:S(2)}) collective-permute-start(f32[14,8,128]{2,1,0:T(8,128)S(1)} %get-tuple-element.60), channel_id=1, source_target_pairs={{1,0},{2,1},{3,2},{4,3},{5,4},{6,5},{7,6},{8,7},{9,8},{10,9},{11,1... | collective-permute-start | bytes 172040 | tf_op jit(solution)/shard_map/ppermute | solution.py:625
  119.6 11.6 %collective-permute-start.13 = (f32[16,4,128]{2,1,0:T(4,128)S(1)}, f32[16,4,128]{2,1,0:T(4,128)S(1)}, u32[]{:S(2)}, u32[]{:S(2)}) collective-permute-start(f32[16,4,128]{2,1,0:T(4,128)S(1)} %get-tuple-element.51), channel_id=1, source_target_pairs={{2,0},{3,1},{4,2},{5,3},{6,4},{7,5},{8,6},{9,7},{10,8},{11,9},{12,... | collective-permute-start | bytes 98312 | tf_op jit(solution)/shard_map/ppermute | solution.py:625
  135.0 2.7 %copy-start.1 = (f32[66,176,128]{2,1,0:T(8,128)S(1)}, f32[66,176,128]{2,1,0:T(8,128)}, u32[]{:S(2)}) copy-start(f32[66,176,128]{2,1,0:T(8,128)} %copy-done) | copy-start | bytes 17842180

commit v6 on v5

--- a/solution.py
+++ b/solution.py
@@ -288,7 +288,7 @@
             high[x - 8 + H1] = t
 
 
-def down1_kernel(own, xlo, xhi, block, turned2, ylo2, yhi2, kept, rsum, csum, rz, cz, beta2, root2, w2, stage):
+def down1_kernel(own, xlo, xhi, raw2, turned2, ylo2, yhi2, kept, rsum, csum, rz, cz, stage):
     w, beta, root = thirds(kept)
 
     def prepare(x, t):
@@ -329,12 +329,7 @@
     stage[...] = jnp.zeros_like(stage)
     for x in range(8):
         t = t2[x * 40 : (x + 1) * 40]
-        root_x, inv_x = roots_of(four_fields(t, 8))
-        root2[x] = root_x
-        beta2[x, pl.ds(8, 40), :] = TAU * t * inv_x
-        for ref in (beta2, w2):
-            ref[x, pl.ds(0, 8), :] = jnp.zeros((8, LANES), F32)
-            ref[x, pl.ds(48, 8), :] = jnp.zeros((8, LANES), F32)
+        raw2[x] = t
         if 1 <= x < 7:
             stage[x % 4, pl.ds(0, 40), :] = t
             flat = stage[x % 4].T
@@ -342,6 +337,16 @@
                 turned2[x - 1, pl.ds(a * 4, 4), :] = flat[a * 8 + 2 : a * 8 + 6]
                 yhi2[x - 1, pl.ds(a * H2, H2), :] = flat[a * 8 + 1 : a * 8 + 1 + H2]
                 ylo2[x - 1, pl.ds(a * H2, H2), :] = flat[a * 8 + 2 : a * 8 + 2 + H2]
+
+
+def down2_kernel(raw2, block, rsum, csum, beta2, root2, w2, stage):
+    for x in range(8):
+        root_x, inv_x = roots_of(four_fields(raw2[x], 8))
+        root2[x] = root_x
+        beta2[x, pl.ds(8, 40), :] = TAU * raw2[x] * inv_x
+        for ref in (beta2, w2):
+            ref[x, pl.ds(0, 8), :] = jnp.zeros((8, LANES), F32)
+            ref[x, pl.ds(48, 8), :] = jnp.zeros((8, LANES), F32)
     for x in range(1, 7):
         mid, total = around(beta2, x, 8, 40)
         w2[x, pl.ds(8, 40), :] = jnp.where(root2[x] > 0.0, 1.2 * mid + TAU * total, 0.0)
@@ -351,8 +356,8 @@
         for i in range(2):
             res_i, coef_i = residual(w2, beta2, root2, x + i, 12, 32, around(w2, x + i, 12, 32))
             res, coef = res + res_i, coef + coef_i
-        rsum[k, pl.ds(0, 32), :] = res
-        csum[k, pl.ds(0, 32), :] = coef
+        rsum[k] = res
+        csum[k] = coef
     rows = [jnp.concatenate([fold_rows(ref, k, 16) for k in range(2)], axis=0) for ref in (rsum, csum)]
     t3 = mm(((rows[0], pair_lanes(8, 2, 2, 0, 0.5)), (rows[1], pair_lanes(8, 2, 2, 8, 0.125, 2, 3))))
 
@@ -367,10 +372,9 @@
         for g in range(1, 4):
             row = jnp.where((lane >= 32 * g) & (lane < 32 * g + 32), turns[g][4 * r + g : 4 * r + g + 1], row)
         packed.append(row)
-    for i in range(block.shape[0] // 24):
-        block[pl.ds(24 * i, 24), :] = jnp.concatenate(packed * 8, axis=0)
-    for i in range(block.shape[0] // 24 * 8, block.shape[0] // 3):
-        block[pl.ds(3 * i, 3), :] = jnp.concatenate(packed, axis=0)
+    packed = jnp.concatenate(packed, axis=0)
+    for i in range(block.shape[0]):
+        block[i] = packed
 
 
 def join2_kernel(own, ylo, yhi, turned, low, high, stage):
@@ -390,19 +394,19 @@
             low[x - 1] = t
 
 
-def join3_kernel(own, xlo, xhi, whole, zlo, zhi):
+def plane_kernel(gx, gy, got, own2, xlo2, xhi2, own, lo4, hi4, b2, up, down, turns, stage):
+    width = 2 * gy
+    size_x = 2 * gx
     for x in range(4 + 2 * H2):
-        t = xlo[x] if x < H2 else own[x - H2] if x < H2 + 4 else xhi[x - H2 - 4]
-        whole[x] = t
-        zlo[x] = t[0:8]
-        zhi[x] = t[24:32]
-
-
-def plane_kernel(gx, gy, got, own, lo4, hi4, turns, stage):
-    width = 2 * gy
+        t = xlo2[x] if x < H2 else own2[x - H2] if x < H2 + 4 else xhi2[x - H2 - 4]
+        b2[x] = t
+        up[size_x + x // 2, pl.ds(8 * (x % 2), 8), :] = t[24:32]
+        down[size_x + x // 2, pl.ds(8 * (x % 2), 8), :] = t[0:8]
+    for i in range(gx * gy):
+        turns[0, pl.ds(3 * i, 3), :] = got[i]
     stage[...] = jnp.zeros_like(stage)
-    for s in range(4):
-        turns[s] = lane_roll(got[...], 32 * s)
+    for s in range(1, 4):
+        turns[s] = lane_roll(turns[0], 32 * s)
     lane = lane_of(gy)
     for h in range(-(-gx // 4)):
         for i in range(12):
@@ -418,6 +422,8 @@
                 at = 2 * (4 * h + q) + x
                 rows = t[32 * q + 16 * x : 32 * q + 16 * x + 16]
                 own[at] = rows
+                up[at] = rows
+                down[at] = rows
                 lo4[at] = rows[0:4]
                 hi4[at] = rows[12:16]
 
@@ -502,7 +508,7 @@
         e3[k] = w3[first3 + k, pl.ds(28, 24), :] * inverse(root3[first3 + k, pl.ds(20, 24), :])
 
 
-def up_kernel(gy, e3, b2, zlo2, zhi2, kept1, kept0, out, beta2, root2, w2, v2, fine2, w1b, v1, w0b, v0, fine1, fine0, turned):
+def up_kernel(gx, gy, e3, b2, below, above, kept1, kept0, out, beta2, root2, w2, v2, fine2, w1b, v1, w0b, v0, fine1, fine0, turned):
     w1, beta1, root1 = thirds(kept1)
     w0, beta0, root0 = thirds(kept0)
     for ref in (w2, v2):
@@ -514,14 +520,16 @@
         root2[x, pl.ds(row, n), :] = root_x
         beta2[x, pl.ds(8 + row, n), :] = TAU * t * inv_x
 
-    def setup(x):
-        beta2[x, pl.ds(0, 8), :] = jnp.zeros((8, LANES), F32)
-        beta2[x, pl.ds(56, 8), :] = jnp.zeros((8, LANES), F32)
-        prepare(x, 0, zlo2[x])
-        prepare(x, 8, b2[x])
-        prepare(x, 40, zhi2[x])
-
-    loop(0, 4 + 2 * H2, setup, 7)
+    def setup(k):
+        for i in range(2):
+            x = 2 * k + i
+            beta2[x, pl.ds(0, 8), :] = jnp.zeros((8, LANES), F32)
+            beta2[x, pl.ds(56, 8), :] = jnp.zeros((8, LANES), F32)
+            prepare(x, 0, below[2 * gx + k, pl.ds(8 * i, 8), :])
+            prepare(x, 8, b2[x])
+            prepare(x, 40, above[2 * gx + k, pl.ds(8 * i, 8), :])
+
+    loop(0, 2 + H2, setup, 7)
 
     repeat = repeat_local(2 * gy, 2 * position("gy") - 2, Y2, 1)
     e = mm(((jnp.concatenate([e3[k] for k in range(6)], axis=0), repeat),))
@@ -675,30 +683,34 @@
     xlo, xhi = swap(high, low, "gx")
 
     x1, x2, x3 = 8 + 2 * H1, 4 + 2 * H2, 2 * gx
-    block, turned2, ysend_lo, ysend_hi, kept1 = call(
+    raw2, turned2, ysend_lo, ysend_hi, kept1 = call(
         down1_kernel,
         (turned1, xlo, xhi),
-        [(3 * gx * gy, LANES), (6, 24, LANES)] + [(6, 6 * H2, LANES)] * 2 + [(3 * x1, 96, LANES)],
+        [(8, 40, LANES), (6, 24, LANES)] + [(6, 6 * H2, LANES)] * 2 + [(3 * x1, 96, LANES)],
         [(8, 80, LANES)] * 2
         + [(320, LANES)] * 2
-        + [(8, 56, LANES), (8, 40, LANES), (8, 56, LANES), (4, LANES, LANES)],
+        + [(4, LANES, LANES)],
     )
     ylo, yhi = swap(ysend_hi, ysend_lo, "gy")
+    (block,) = call(
+        down2_kernel,
+        (raw2,),
+        [(gx * gy, 3, LANES)],
+        [(2, 32, LANES)] * 2 + [(8, 56, LANES), (8, 40, LANES), (8, 56, LANES), (1, LANES, LANES)],
+    )
     got = whole_plane(block)
     turned2, low, high = call(
         join2_kernel, (turned2, ylo, yhi), [(4, 32, LANES)] + [(H2, 32, LANES)] * 2, [(4, LANES, LANES)]
     )
     xlo, xhi = swap(high, low, "gx")
-    own3, lo4, hi4 = call(
+    own3, lo4, hi4, b2, to_up, to_down = call(
         functools.partial(plane_kernel, gx, gy),
-        (got,),
-        [(x3, 16, LANES)] + [(x3, 4, LANES)] * 2,
+        (got, turned2, xlo, xhi),
+        [(x3, 16, LANES)] + [(x3, 4, LANES)] * 2 + [(x2, 32, LANES)] + [(x3 + x2 // 2, 16, LANES)] * 2,
         [(4, 3 * gx * gy, LANES), (2, LANES, LANES)],
     )
-    below, above = swap(own3, own3, "gz")
+    below, above = swap(to_up, to_down, "gz")
     below2, above2 = swap(hi4, lo4, "gz", 2)
-    b2, zsend_lo, zsend_hi = call(join3_kernel, (turned2, xlo, xhi), [(x2, 32, LANES)] + [(x2, 8, LANES)] * 2, [])
-    zlo2, zhi2 = swap(zsend_hi, zsend_lo, "gz")
     (e3,) = call(
         functools.partial(coarse_kernel, gx, gy),
         (own3, below, above, below2, above2),
@@ -713,8 +725,8 @@
     )
 
     (correction,) = call(
-        functools.partial(up_kernel, gy),
-        (e3, b2, zlo2, zhi2, kept1, kept0),
+        functools.partial(up_kernel, gx, gy),
+        (e3, b2, below, above, kept1, kept0),
         [(4, 16, 16, LANES)],
         [(x2, 64, LANES), (x2, 48, LANES), (x2, 64, LANES), (x2, 64, LANES), (6, 48, LANES)]
         + [(x1, 96, LANES)] * 2

time: 143 us -> 143 us (level)
  the two profiles are of different devices: /device:TPU:185 before, /device:TPU:310 now
where the time goes in v6:
time: 143 us; the launch traced here: 142 us
  starting transfers between devices  64.3 us (45%)
  waiting for transfers between devices  49.4 us (35%)
  Pallas kernels  19.4 us (14%)
  local copies, waits for them, and re-layouts  8.51 us (6%)
    ppermute x9, waiting for transfers between devices, swap(): lax.ppermute(to_down, axis, [(i + far, i) for i in range(n - far)])  39.9 us
    ppermute x9, starting transfers between devices, swap(): lax.ppermute(to_up, axis, [(i, i + far) for i in range(n - far)])  31.1 us
    ppermute x9, starting transfers between devices, swap(): lax.ppermute(to_down, axis, [(i + far, i) for i in range(n - far)])  24.7 us
    pallas_call x10, Pallas kernels, call(): pl.pallas_call(kernel, out_shape=[jax.ShapeDtypeStruct(s, F32) for s in o...  18.7 us
    ppermute x9, waiting for transfers between devices, swap(): lax.ppermute(to_up, axis, [(i, i + far) for i in range(n - far)])  9.45 us
    unnamed x12, local copies, waits for them, and re-layouts  8.51 us
    all_to_all x1, starting transfers between devices, whole_plane(): return lax.all_to_all(block, ('gx', 'gy'), 0, 0, tiled=True)  8.42 us
  transfers between devices with their start and end apart: 19, of which 15 were waited for; matrix products, arithmetic and copies ran while one was open for 0% of the time, Pallas kernels for 0%

profile of v6, /device:TPU:310, one launch (start us, length us, event | category | flops | bytes accessed | tf_op | source)
XLA Modules:
  0.0 141.7 jit_solution(10087290531763004113)
XLA Ops:
  0.0 1.0 copy-done.2
  1.0 0.9 copy-done.3
  1.9 0.7 copy-done.4
  2.6 0.7 copy-done.5
  3.3 0.7 shard_map.46
  4.0 4.6 %collective-permute-start = (f32[5,3,16,128]{3,2,1,0:T(8,128)S(1)}, f32[5,3,16,128]{3,2,1,0:T(8,128)S(1)}, u32[]{:S(2)}, u32[]{:S(2)}) collective-permute-start(f32[5,3,16,128]{3,2,1,0:T(8,128)S(1)} %get-tuple-element.34), channel_id=1, source_target_pairs={{0,128},{128,256},{256,384},{384,512},{512,640},{640,768},{768,896... | collective-permute-start | bytes 368648 | tf_op jit(solution)/shard_map/ppermute | solution.py:632
  8.6 1.9 %collective-permute-start.1 = (f32[5,3,16,128]{3,2,1,0:T(8,128)S(1)}, f32[5,3,16,128]{3,2,1,0:T(8,128)S(1)}, u32[]{:S(2)}, u32[]{:S(2)}) collective-permute-start(f32[5,3,16,128]{3,2,1,0:T(8,128)S(1)} %get-tuple-element.36), channel_id=1, source_target_pairs={{128,0},{256,128},{384,256},{512,384},{640,512},{768,640},{896,768... | collective-permute-start | bytes 368648 | tf_op jit(solution)/shard_map/ppermute | solution.py:633
  10.5 0.6 collective-permute-done.xlo
  11.1 5.4 %collective-permute-done.1.xhi = f32[5,3,16,128]{3,2,1,0:T(8,128)S(1)} collective-permute-done((f32[5,3,16,128]{3,2,1,0:T(8,128)S(1)}, f32[5,3,16,128]{3,2,1,0:T(8,128)S(1)}, u32[]{:S(2)}, u32[]{:S(2)}) %collective-permute-start.1) | collective-permute-done | bytes 122912 | tf_op jit(solution)/shard_map/ppermute | solution.py:633
  16.6 4.8 %collective-permute-start.2 = (f32[22,15,128]{2,1,0:T(8,128)S(1)}, f32[22,15,128]{2,1,0:T(8,128)S(1)}, u32[]{:S(2)}, u32[]{:S(2)}) collective-permute-start(f32[22,15,128]{2,1,0:T(8,128)S(1)} %get-tuple-element.37), channel_id=1, source_target_pairs={{0,16},{16,32},{32,48},{48,64},{64,80},{80,96},{96,112},{1,17},{17... | collective-permute-start | bytes 506888 | tf_op jit(solution)/shard_map/ppermute | solution.py:632
  21.5 1.9 %collective-permute-start.3 = (f32[22,15,128]{2,1,0:T(8,128)S(1)}, f32[22,15,128]{2,1,0:T(8,128)S(1)}, u32[]{:S(2)}, u32[]{:S(2)}) collective-permute-start(f32[22,15,128]{2,1,0:T(8,128)S(1)} %get-tuple-element.38), channel_id=1, source_target_pairs={{16,0},{32,16},{48,32},{64,48},{80,64},{96,80},{112,96},{17,1},{33... | collective-permute-start | bytes 506888 | tf_op jit(solution)/shard_map/ppermute | solution.py:633
  23.4 1.1 collective-permute-done.2.ylo
  24.4 5.6 %collective-permute-done.3.yhi = f32[22,15,128]{2,1,0:T(8,128)S(1)} collective-permute-done((f32[22,15,128]{2,1,0:T(8,128)S(1)}, f32[22,15,128]{2,1,0:T(8,128)S(1)}, u32[]{:S(2)}, u32[]{:S(2)}) %collective-permute-start.3) | collective-permute-done | bytes 168992 | tf_op jit(solution)/shard_map/ppermute | solution.py:633
  30.1 0.7 shard_map.48
  30.7 1.9 %collective-permute-start.4 = (f32[22,16,128]{2,1,0:T(8,128)S(1)}, f32[22,16,128]{2,1,0:T(8,128)S(1)}, u32[]{:S(2)}, u32[]{:S(2)}) collective-permute-start(f32[22,16,128]{2,1,0:T(8,128)S(1)} %get-tuple-element.40), channel_id=1, source_target_pairs={{0,1},{1,2},{2,3},{3,4},{4,5},{5,6},{6,7},{7,8},{8,9},{9,10},{10,1... | collective-permute-start | bytes 540680 | tf_op jit(solution)/shard_map/ppermute | solution.py:632
  32.7 3.6 %collective-permute-start.5 = (f32[22,16,128]{2,1,0:T(8,128)S(1)}, f32[22,16,128]{2,1,0:T(8,128)S(1)}, u32[]{:S(2)}, u32[]{:S(2)}) collective-permute-start(f32[22,16,128]{2,1,0:T(8,128)S(1)} %get-tuple-element.41), channel_id=1, source_target_pairs={{1,0},{2,1},{3,2},{4,3},{5,4},{6,5},{7,6},{8,7},{9,8},{10,9},{11,1... | collective-permute-start | bytes 540680 | tf_op jit(solution)/shard_map/ppermute | solution.py:633
  36.3 1.2 collective-permute-done.4.zlo
  37.5 1.8 %collective-permute-done.5.zhi = f32[22,16,128]{2,1,0:T(8,128)S(1)} collective-permute-done((f32[22,16,128]{2,1,0:T(8,128)S(1)}, f32[22,16,128]{2,1,0:T(8,128)S(1)}, u32[]{:S(2)}, u32[]{:S(2)}) %collective-permute-start.5) | collective-permute-done | bytes 180256 | tf_op jit(solution)/shard_map/ppermute | solution.py:633
  39.3 5.4 %shard_map.49 = (f32[8,48,128]{2,1,0:T(8,128)S(1)}, f32[8,36,128]{2,1,0:T(8,128)S(1)}, f32[8,36,128]{2,1,0:T(8,128)S(1)}, f32[66,176,128]{2,1,0:T(8,128)S(1)}) custom-call(f32[22,128,128]{2,1,0:T(8,128)S(1)} %get-tuple-element.39.turned, f32[22,16,128]{2,1,0:T(8,128)S(1)} %collective-permute-done.4.zlo, f32[22,16,128]{2,1,0:T(8,128)S(1)} %collective-permute-done.5.zhi), custom_call_target="tpu_custom_call" | custom-call | tf_op jit(solution)/shard_map/pallas_call | solution.py:620
  44.7 2.5 %copy-done = f32[66,176,128]{2,1,0:T(8,128)} copy-done((f32[66,176,128]{2,1,0:T(8,128)}, f32[66,176,128]{2,1,0:T(8,128)S(1)}, u32[]{:S(2)}) %copy-start) | copy-done | bytes 5947416
  47.3 1.9 %collective-permute-start.6 = (f32[8,36,128]{2,1,0:T(8,128)S(1)}, f32[8,36,128]{2,1,0:T(8,128)S(1)}, u32[]{:S(2)}, u32[]{:S(2)}) collective-permute-start(f32[8,36,128]{2,1,0:T(8,128)S(1)} %get-tuple-element.43), channel_id=1, source_target_pairs={{0,16},{16,32},{32,48},{48,64},{64,80},{80,96},{96,112},{1,17},{17... | collective-permute-start | bytes 442376 | tf_op jit(solution)/shard_map/ppermute | solution.py:632
  49.2 3.9 %collective-permute-start.7 = (f32[8,36,128]{2,1,0:T(8,128)S(1)}, f32[8,36,128]{2,1,0:T(8,128)S(1)}, u32[]{:S(2)}, u32[]{:S(2)}) collective-permute-start(f32[8,36,128]{2,1,0:T(8,128)S(1)} %get-tuple-element.44), channel_id=1, source_target_pairs={{16,0},{32,16},{48,32},{64,48},{80,64},{96,80},{112,96},{17,1},{33... | collective-permute-start | bytes 442376 | tf_op jit(solution)/shard_map/ppermute | solution.py:633
  53.1 1.4 collective-permute-done.6.ylo
  54.5 3.1 %collective-permute-done.7.yhi = f32[8,36,128]{2,1,0:T(8,128)S(1)} collective-permute-done((f32[8,36,128]{2,1,0:T(8,128)S(1)}, f32[8,36,128]{2,1,0:T(8,128)S(1)}, u32[]{:S(2)}, u32[]{:S(2)}) %collective-permute-start.7) | collective-permute-done | bytes 147488 | tf_op jit(solution)/shard_map/ppermute | solution.py:633
  57.6 0.2 shard_map.50
  57.8 1.9 %collective-permute-start.8 = (f32[6,80,128]{2,1,0:T(8,128)S(1)}, f32[6,80,128]{2,1,0:T(8,128)S(1)}, u32[]{:S(2)}, u32[]{:S(2)}) collective-permute-start(f32[6,80,128]{2,1,0:T(8,128)S(1)} %get-tuple-element.46), channel_id=1, source_target_pairs={{0,128},{128,256},{256,384},{384,512},{512,640},{640,768},{768,896... | collective-permute-start | bytes 737288 | tf_op jit(solution)/shard_map/ppermute | solution.py:632
  59.8 3.9 %collective-permute-start.9 = (f32[6,80,128]{2,1,0:T(8,128)S(1)}, f32[6,80,128]{2,1,0:T(8,128)S(1)}, u32[]{:S(2)}, u32[]{:S(2)}) collective-permute-start(f32[6,80,128]{2,1,0:T(8,128)S(1)} %get-tuple-element.47), channel_id=1, source_target_pairs={{128,0},{256,128},{384,256},{512,384},{640,512},{768,640},{896,768... | collective-permute-start | bytes 737288 | tf_op jit(solution)/shard_map/ppermute | solution.py:633
  63.7 3.4 %collective-permute-done.8.xlo = f32[6,80,128]{2,1,0:T(8,128)S(1)} collective-permute-done((f32[6,80,128]{2,1,0:T(8,128)S(1)}, f32[6,80,128]{2,1,0:T(8,128)S(1)}, u32[]{:S(2)}, u32[]{:S(2)}) %collective-permute-start.8) | collective-permute-done | bytes 245792 | tf_op jit(solution)/shard_map/ppermute | solution.py:632
  67.1 3.1 %collective-permute-done.9.xhi = f32[6,80,128]{2,1,0:T(8,128)S(1)} collective-permute-done((f32[6,80,128]{2,1,0:T(8,128)S(1)}, f32[6,80,128]{2,1,0:T(8,128)S(1)}, u32[]{:S(2)}, u32[]{:S(2)}) %collective-permute-start.9) | collective-permute-done | bytes 245792 | tf_op jit(solution)/shard_map/ppermute | solution.py:633
  70.2 2.1 %shard_map.51 = (f32[8,40,128]{2,1,0:T(8,128)S(1)}, f32[6,24,128]{2,1,0:T(8,128)S(1)}, f32[6,30,128]{2,1,0:T(8,128)S(1)}, f32[6,30,128]{2,1,0:T(8,128)S(1)}, f32[60,96,128]{2,1,0:T(8,128)S(1)}) custom-call(f32[8,80,128]{2,1,0:T(8,128)S(1)} %get-tuple-element.45.own, f32[6,80,128]{2,1,0:T(8,128)S(1)} %collective-permute-done.8.xlo, ...), custom_call_target="tpu_custom_call" | custom-call | tf_op jit(solution)/shard_map/pallas_call | solution.py:620
  72.3 1.3 shard_map.52
  73.5 8.4 %all-to-all-start = ((f32[64,3,128]{2,1,0:T(4,128)}), f32[64,3,128]{2,1,0:T(4,128)S(1)}, u32[]{:S(2)}, u32[]{:S(2)}) async-start(f32[64,3,128]{2,1,0:T(4,128)} %shard_map.52), calls=%async_computation | async-start | bytes 262144 | tf_op jit(solution)/shard_map/all_to_all | solution.py:638
  82.0 4.6 %collective-permute-start.10 = (f32[6,30,128]{2,1,0:T(8,128)S(1)}, f32[6,30,128]{2,1,0:T(8,128)S(1)}, u32[]{:S(2)}, u32[]{:S(2)}) collective-permute-start(f32[6,30,128]{2,1,0:T(8,128)S(1)} %get-tuple-element.50), channel_id=1, source_target_pairs={{0,16},{16,32},{32,48},{48,64},{64,80},{80,96},{96,112},{1,17},{17... | collective-permute-start | bytes 276488 | tf_op jit(solution)/shard_map/ppermute | solution.py:632
  86.5 1.9 %collective-permute-start.11 = (f32[6,30,128]{2,1,0:T(8,128)S(1)}, f32[6,30,128]{2,1,0:T(8,128)S(1)}, u32[]{:S(2)}, u32[]{:S(2)}) collective-permute-start(f32[6,30,128]{2,1,0:T(8,128)S(1)} %get-tuple-element.51), channel_id=1, source_target_pairs={{16,0},{32,16},{48,32},{64,48},{80,64},{96,80},{112,96},{17,1},{33... | collective-permute-start | bytes 276488 | tf_op jit(solution)/shard_map/ppermute | solution.py:633
  88.5 1.7 %collective-permute-done.10.ylo = f32[6,30,128]{2,1,0:T(8,128)S(1)} collective-permute-done((f32[6,30,128]{2,1,0:T(8,128)S(1)}, f32[6,30,128]{2,1,0:T(8,128)S(1)}, u32[]{:S(2)}, u32[]{:S(2)}) %collective-permute-start.10) | collective-permute-done | bytes 92192 | tf_op jit(solution)/shard_map/ppermute | solution.py:632
  90.2 4.7 %collective-permute-done.11.yhi = f32[6,30,128]{2,1,0:T(8,128)S(1)} collective-permute-done((f32[6,30,128]{2,1,0:T(8,128)S(1)}, f32[6,30,128]{2,1,0:T(8,128)S(1)}, u32[]{:S(2)}, u32[]{:S(2)}) %collective-permute-start.11) | collective-permute-done | bytes 92192 | tf_op jit(solution)/shard_map/ppermute | solution.py:633
  95.0 4.6 %collective-permute-start.12 = (f32[5,32,128]{2,1,0:T(8,128)S(1)}, f32[5,32,128]{2,1,0:T(8,128)S(1)}, u32[]{:S(2)}, u32[]{:S(2)}) collective-permute-start(f32[5,32,128]{2,1,0:T(8,128)S(1)} %get-tuple-element.53), channel_id=1, source_target_pairs={{0,128},{128,256},{256,384},{384,512},{512,640},{640,768},{768,896... | collective-permute-start | bytes 245768 | tf_op jit(solution)/shard_map/ppermute | solution.py:632
  99.7 1.9 %collective-permute-start.13 = (f32[5,32,128]{2,1,0:T(8,128)S(1)}, f32[5,32,128]{2,1,0:T(8,128)S(1)}, u32[]{:S(2)}, u32[]{:S(2)}) collective-permute-start(f32[5,32,128]{2,1,0:T(8,128)S(1)} %get-tuple-element.54), channel_id=1, source_target_pairs={{128,0},{256,128},{384,256},{512,384},{640,512},{768,640},{896,768... | collective-permute-start | bytes 245768 | tf_op jit(solution)/shard_map/ppermute | solution.py:633
  101.7 5.5 %collective-permute-done.13.xhi2 = f32[5,32,128]{2,1,0:T(8,128)S(1)} collective-permute-done((f32[5,32,128]{2,1,0:T(8,128)S(1)}, f32[5,32,128]{2,1,0:T(8,128)S(1)}, u32[]{:S(2)}, u32[]{:S(2)}) %collective-permute-start.13) | collective-permute-done | bytes 81952 | tf_op jit(solution)/shard_map/ppermute | solution.py:633
  107.2 0.3 shard_map.54
  107.5 1.9 %collective-permute-start.14 = (f32[23,16,128]{2,1,0:T(8,128)S(1)}, f32[23,16,128]{2,1,0:T(8,128)S(1)}, u32[]{:S(2)}, u32[]{:S(2)}) collective-permute-start(f32[23,16,128]{2,1,0:T(8,128)S(1)} %get-tuple-element.56), channel_id=1, source_target_pairs={{0,1},{1,2},{2,3},{3,4},{4,5},{5,6},{6,7},{7,8},{8,9},{9,10},{10,1... | collective-permute-start | bytes 565256 | tf_op jit(solution)/shard_map/ppermute | solution.py:632
  109.4 3.6 %collective-permute-start.15 = (f32[23,16,128]{2,1,0:T(8,128)S(1)}, f32[23,16,128]{2,1,0:T(8,128)S(1)}, u32[]{:S(2)}, u32[]{:S(2)}) collective-permute-start(f32[23,16,128]{2,1,0:T(8,128)S(1)} %get-tuple-element.57), channel_id=1, source_target_pairs={{1,0},{2,1},{3,2},{4,3},{5,4},{6,5},{7,6},{8,7},{9,8},{10,9},{11,1... | collective-permute-start | bytes 565256 | tf_op jit(solution)/shard_map/ppermute | solution.py:633
  113.1 4.8 %collective-permute-start.16 = (f32[16,4,128]{2,1,0:T(4,128)S(1)}, f32[16,4,128]{2,1,0:T(4,128)S(1)}, u32[]{:S(2)}, u32[]{:S(2)}) collective-permute-start(f32[16,4,128]{2,1,0:T(4,128)S(1)} %get-tuple-element.58), channel_id=1, source_target_pairs={{0,2},{1,3},{2,4},{3,5},{4,6},{5,7},{6,8},{7,9},{8,10},{9,11},{10,... | collective-permute-start | bytes 98312 | tf_op jit(solution)/shard_map/ppermute | solution.py:632
  117.9 1.9 %collective-permute-start.17 = (f32[16,4,128]{2,1,0:T(4,128)S(1)}, f32[16,4,128]{2,1,0:T(4,128)S(1)}, u32[]{:S(2)}, u32[]{:S(2)}) collective-permute-start(f32[16,4,128]{2,1,0:T(4,128)S(1)} %get-tuple-element.59), channel_id=1, source_target_pairs={{2,0},{3,1},{4,2},{5,3},{6,4},{7,5},{8,6},{9,7},{10,8},{11,9},{12,... | collective-permute-start | bytes 98312 | tf_op jit(solution)/shard_map/ppermute | solution.py:633
  119.8 10.7 %collective-permute-done.17.above2 = f32[16,4,128]{2,1,0:T(4,128)S(1)} collective-permute-done((f32[16,4,128]{2,1,0:T(4,128)S(1)}, f32[16,4,128]{2,1,0:T(4,128)S(1)}, u32[]{:S(2)}, u32[]{:S(2)}) %collective-permute-start.17) | collective-permute-done | bytes 32800 | tf_op jit(solution)/shard_map/ppermute | solution.py:633
  130.5 3.8 %shard_map.55.e3 = f32[6,24,128]{2,1,0:T(8,128)S(1)} custom-call(f32[16,16,128]{2,1,0:T(8,128)S(1)} %get-tuple-element.55.own, f32[23,16,128]{2,1,0:T(8,128)S(1)} %collective-permute-done.14.below, f32[23,16,128]{2,1,0:T(8,128)S(1)} %collective-permute-done.15.above, f32[16,4,128]{2,1,0:T(4,128)S(1)} %collective-permute-done.16.below2, ...), custom_call_target="tpu_custom_call" | custom-call | tf_op jit(solution)/shard_map/pallas_call | solution.py:620
  134.3 2.7 %copy-done.1 = f32[66,176,128]{2,1,0:T(8,128)S(1)} copy-done((f32[66,176,128]{2,1,0:T(8,128)S(1)}, f32[66,176,128]{2,1,0:T(8,128)}, u32[]{:S(2)}) %copy-start.1) | copy-done | bytes 5947416
  137.0 4.7 %shard_map.56 = f32[4,16,16,128]{3,2,1,0:T(8,128)} custom-call(f32[6,24,128]{2,1,0:T(8,128)S(1)} %shard_map.55.e3, f32[14,32,128]{2,1,0:T(8,128)S(1)} %get-tuple-element.60.b2, f32[23,16,128]{2,1,0:T(8,128)S(1)} %collective-permute-done.14.below, f32[23,16,128]{2,1,0:T(8,128)S(1)} %collective-permute-done.15.above, ...), custom_call_target="tpu_custom_call" | custom-call | tf_op jit(solution)/shard_map/pallas_call | solution.py:620
  (13 shorter events, 0.4 us)
Async XLA Ops:
  0.0 1.0 copy-start.2
  1.0 0.9 copy-start.3
  1.9 0.7 copy-start.4
  2.6 0.7 copy-start.5
  4.0 7.2 %collective-permute-start = (f32[5,3,16,128]{3,2,1,0:T(8,128)S(1)}, f32[5,3,16,128]{3,2,1,0:T(8,128)S(1)}, u32[]{:S(2)}, u32[]{:S(2)}) collective-permute-start(f32[5,3,16,128]{3,2,1,0:T(8,128)S(1)} %get-tuple-element.34), channel_id=1, source_target_pairs={{0,128},{128,256},{256,384},{384,512},{512,640},{640,768},{768,896... | collective-permute-start | bytes 368648 | tf_op jit(solution)/shard_map/ppermute | solution.py:632
  8.6 8.0 %collective-permute-start.1 = (f32[5,3,16,128]{3,2,1,0:T(8,128)S(1)}, f32[5,3,16,128]{3,2,1,0:T(8,128)S(1)}, u32[]{:S(2)}, u32[]{:S(2)}) collective-permute-start(f32[5,3,16,128]{3,2,1,0:T(8,128)S(1)} %get-tuple-element.36), channel_id=1, source_target_pairs={{128,0},{256,128},{384,256},{512,384},{640,512},{768,640},{896,768... | collective-permute-start | bytes 368648 | tf_op jit(solution)/shard_map/ppermute | solution.py:633
  16.6 7.8 %collective-permute-start.2 = (f32[22,15,128]{2,1,0:T(8,128)S(1)}, f32[22,15,128]{2,1,0:T(8,128)S(1)}, u32[]{:S(2)}, u32[]{:S(2)}) collective-permute-start(f32[22,15,128]{2,1,0:T(8,128)S(1)} %get-tuple-element.37), channel_id=1, source_target_pairs={{0,16},{16,32},{32,48},{48,64},{64,80},{80,96},{96,112},{1,17},{17... | collective-permute-start | bytes 506888 | tf_op jit(solution)/shard_map/ppermute | solution.py:632
  21.5 8.6 %collective-permute-start.3 = (f32[22,15,128]{2,1,0:T(8,128)S(1)}, f32[22,15,128]{2,1,0:T(8,128)S(1)}, u32[]{:S(2)}, u32[]{:S(2)}) collective-permute-start(f32[22,15,128]{2,1,0:T(8,128)S(1)} %get-tuple-element.38), channel_id=1, source_target_pairs={{16,0},{32,16},{48,32},{64,48},{80,64},{96,80},{112,96},{17,1},{33... | collective-permute-start | bytes 506888 | tf_op jit(solution)/shard_map/ppermute | solution.py:633
  30.7 6.8 %collective-permute-start.4 = (f32[22,16,128]{2,1,0:T(8,128)S(1)}, f32[22,16,128]{2,1,0:T(8,128)S(1)}, u32[]{:S(2)}, u32[]{:S(2)}) collective-permute-start(f32[22,16,128]{2,1,0:T(8,128)S(1)} %get-tuple-element.40), channel_id=1, source_target_pairs={{0,1},{1,2},{2,3},{3,4},{4,5},{5,6},{6,7},{7,8},{8,9},{9,10},{10,1... | collective-permute-start | bytes 540680 | tf_op jit(solution)/shard_map/ppermute | solution.py:632
  32.7 6.6 %collective-permute-start.5 = (f32[22,16,128]{2,1,0:T(8,128)S(1)}, f32[22,16,128]{2,1,0:T(8,128)S(1)}, u32[]{:S(2)}, u32[]{:S(2)}) collective-permute-start(f32[22,16,128]{2,1,0:T(8,128)S(1)} %get-tuple-element.41), channel_id=1, source_target_pairs={{1,0},{2,1},{3,2},{4,3},{5,4},{6,5},{7,6},{8,7},{9,8},{10,9},{11,1... | collective-permute-start | bytes 540680 | tf_op jit(solution)/shard_map/ppermute | solution.py:633
  44.7 2.6 %copy-start = (f32[66,176,128]{2,1,0:T(8,128)}, f32[66,176,128]{2,1,0:T(8,128)S(1)}, u32[]{:S(2)}) copy-start(f32[66,176,128]{2,1,0:T(8,128)S(1)} %get-tuple-element.62.kept0) | copy-start | bytes 17842180
  47.3 7.2 %collective-permute-start.6 = (f32[8,36,128]{2,1,0:T(8,128)S(1)}, f32[8,36,128]{2,1,0:T(8,128)S(1)}, u32[]{:S(2)}, u32[]{:S(2)}) collective-permute-start(f32[8,36,128]{2,1,0:T(8,128)S(1)} %get-tuple-element.43), channel_id=1, source_target_pairs={{0,16},{16,32},{32,48},{48,64},{64,80},{80,96},{96,112},{1,17},{17... | collective-permute-start | bytes 442376 | tf_op jit(solution)/shard_map/ppermute | solution.py:632
  49.2 8.4 %collective-permute-start.7 = (f32[8,36,128]{2,1,0:T(8,128)S(1)}, f32[8,36,128]{2,1,0:T(8,128)S(1)}, u32[]{:S(2)}, u32[]{:S(2)}) collective-permute-start(f32[8,36,128]{2,1,0:T(8,128)S(1)} %get-tuple-element.44), channel_id=1, source_target_pairs={{16,0},{32,16},{48,32},{64,48},{80,64},{96,80},{112,96},{17,1},{33... | collective-permute-start | bytes 442376 | tf_op jit(solution)/shard_map/ppermute | solution.py:633
  57.8 9.2 %collective-permute-start.8 = (f32[6,80,128]{2,1,0:T(8,128)S(1)}, f32[6,80,128]{2,1,0:T(8,128)S(1)}, u32[]{:S(2)}, u32[]{:S(2)}) collective-permute-start(f32[6,80,128]{2,1,0:T(8,128)S(1)} %get-tuple-element.46), channel_id=1, source_target_pairs={{0,128},{128,256},{256,384},{384,512},{512,640},{640,768},{768,896... | collective-permute-start | bytes 737288 | tf_op jit(solution)/shard_map/ppermute | solution.py:632
  59.8 10.4 %collective-permute-start.9 = (f32[6,80,128]{2,1,0:T(8,128)S(1)}, f32[6,80,128]{2,1,0:T(8,128)S(1)}, u32[]{:S(2)}, u32[]{:S(2)}) collective-permute-start(f32[6,80,128]{2,1,0:T(8,128)S(1)} %get-tuple-element.47), channel_id=1, source_target_pairs={{128,0},{256,128},{384,256},{512,384},{640,512},{768,640},{896,768... | collective-permute-start | bytes 737288 | tf_op jit(solution)/shard_map/ppermute | solution.py:633
  73.5 33.7 %all-to-all-start = ((f32[64,3,128]{2,1,0:T(4,128)}), f32[64,3,128]{2,1,0:T(4,128)S(1)}, u32[]{:S(2)}, u32[]{:S(2)}) async-start(f32[64,3,128]{2,1,0:T(4,128)} %shard_map.52), calls=%async_computation | async-start | bytes 262144 | tf_op jit(solution)/shard_map/all_to_all | solution.py:638
  82.0 8.2 %collective-permute-start.10 = (f32[6,30,128]{2,1,0:T(8,128)S(1)}, f32[6,30,128]{2,1,0:T(8,128)S(1)}, u32[]{:S(2)}, u32[]{:S(2)}) collective-permute-start(f32[6,30,128]{2,1,0:T(8,128)S(1)} %get-tuple-element.50), channel_id=1, source_target_pairs={{0,16},{16,32},{32,48},{48,64},{64,80},{80,96},{96,112},{1,17},{17... | collective-permute-start | bytes 276488 | tf_op jit(solution)/shard_map/ppermute | solution.py:632
  86.5 8.3 %collective-permute-start.11 = (f32[6,30,128]{2,1,0:T(8,128)S(1)}, f32[6,30,128]{2,1,0:T(8,128)S(1)}, u32[]{:S(2)}, u32[]{:S(2)}) collective-permute-start(f32[6,30,128]{2,1,0:T(8,128)S(1)} %get-tuple-element.51), channel_id=1, source_target_pairs={{16,0},{32,16},{48,32},{64,48},{80,64},{96,80},{112,96},{17,1},{33... | collective-permute-start | bytes 276488 | tf_op jit(solution)/shard_map/ppermute | solution.py:633
  95.0 6.7 %collective-permute-start.12 = (f32[5,32,128]{2,1,0:T(8,128)S(1)}, f32[5,32,128]{2,1,0:T(8,128)S(1)}, u32[]{:S(2)}, u32[]{:S(2)}) collective-permute-start(f32[5,32,128]{2,1,0:T(8,128)S(1)} %get-tuple-element.53), channel_id=1, source_target_pairs={{0,128},{128,256},{256,384},{384,512},{512,640},{640,768},{768,896... | collective-permute-start | bytes 245768 | tf_op jit(solution)/shard_map/ppermute | solution.py:632
  99.7 7.5 %collective-permute-start.13 = (f32[5,32,128]{2,1,0:T(8,128)S(1)}, f32[5,32,128]{2,1,0:T(8,128)S(1)}, u32[]{:S(2)}, u32[]{:S(2)}) collective-permute-start(f32[5,32,128]{2,1,0:T(8,128)S(1)} %get-tuple-element.54), channel_id=1, source_target_pairs={{128,0},{256,128},{384,256},{512,384},{640,512},{768,640},{896,768... | collective-permute-start | bytes 245768 | tf_op jit(solution)/shard_map/ppermute | solution.py:633
  107.5 23.0 %collective-permute-start.14 = (f32[23,16,128]{2,1,0:T(8,128)S(1)}, f32[23,16,128]{2,1,0:T(8,128)S(1)}, u32[]{:S(2)}, u32[]{:S(2)}) collective-permute-start(f32[23,16,128]{2,1,0:T(8,128)S(1)} %get-tuple-element.56), channel_id=1, source_target_pairs={{0,1},{1,2},{2,3},{3,4},{4,5},{5,6},{6,7},{7,8},{8,9},{9,10},{10,1... | collective-permute-start | bytes 565256 | tf_op jit(solution)/shard_map/ppermute | solution.py:632
  109.4 21.1 %collective-permute-start.15 = (f32[23,16,128]{2,1,0:T(8,128)S(1)}, f32[23,16,128]{2,1,0:T(8,128)S(1)}, u32[]{:S(2)}, u32[]{:S(2)}) collective-permute-start(f32[23,16,128]{2,1,0:T(8,128)S(1)} %get-tuple-element.57), channel_id=1, source_target_pairs={{1,0},{2,1},{3,2},{4,3},{5,4},{6,5},{7,6},{8,7},{9,8},{10,9},{11,1... | collective-permute-start | bytes 565256 | tf_op jit(solution)/shard_map/ppermute | solution.py:633
  113.1 6.7 %collective-permute-start.16 = (f32[16,4,128]{2,1,0:T(4,128)S(1)}, f32[16,4,128]{2,1,0:T(4,128)S(1)}, u32[]{:S(2)}, u32[]{:S(2)}) collective-permute-start(f32[16,4,128]{2,1,0:T(4,128)S(1)} %get-tuple-element.58), channel_id=1, source_target_pairs={{0,2},{1,3},{2,4},{3,5},{4,6},{5,7},{6,8},{7,9},{8,10},{9,11},{10,... | collective-permute-start | bytes 98312 | tf_op jit(solution)/shard_map/ppermute | solution.py:632
  117.9 12.6 %collective-permute-start.17 = (f32[16,4,128]{2,1,0:T(4,128)S(1)}, f32[16,4,128]{2,1,0:T(4,128)S(1)}, u32[]{:S(2)}, u32[]{:S(2)}) collective-permute-start(f32[16,4,128]{2,1,0:T(4,128)S(1)} %get-tuple-element.59), channel_id=1, source_target_pairs={{2,0},{3,1},{4,2},{5,3},{6,4},{7,5},{8,6},{9,7},{10,8},{11,9},{12,... | collective-permute-start | bytes 98312 | tf_op jit(solution)/shard_map/ppermute | solution.py:633
  134.3 2.7 %copy-start.1 = (f32[66,176,128]{2,1,0:T(8,128)S(1)}, f32[66,176,128]{2,1,0:T(8,128)}, u32[]{:S(2)}) copy-start(f32[66,176,128]{2,1,0:T(8,128)} %copy-done) | copy-start | bytes 17842180

commit v7 on v6

--- a/solution.py
+++ b/solution.py
@@ -207,11 +207,10 @@
     loop(0, 4, own, 2)
 
 
-def down0_kernel(turned, zlo, zhi, out, ylo, yhi, kept, rsum, csum, rz, cz, stage):
+def down0_kernel(turned, zlo, zhi, out, ylo, yhi, beta, root, w, rsum, csum, rz, cz, stage):
     planes = 16 + 2 * HX0
     depth = 128 + 2 * HZ0
     half = depth // 2
-    w, beta, root = thirds(kept)
     qb = pair_lanes(Y0, HY0, 8, 0, 0.5)
     qc = pair_lanes(Y0, HY0, 8, 32, 0.125, 2, 3)
 
@@ -508,9 +507,8 @@
         e3[k] = w3[first3 + k, pl.ds(28, 24), :] * inverse(root3[first3 + k, pl.ds(20, 24), :])
 
 
-def up_kernel(gx, gy, e3, b2, below, above, kept1, kept0, out, beta2, root2, w2, v2, fine2, w1b, v1, w0b, v0, fine1, fine0, turned):
+def up_kernel(gx, gy, e3, b2, below, above, kept1, beta0, root0, out, beta2, root2, w2, v2, fine2, w1b, v1, w0b, v0, fine1, fine0, turned):
     w1, beta1, root1 = thirds(kept1)
-    w0, beta0, root0 = thirds(kept0)
     for ref in (w2, v2):
         ref[...] = jnp.zeros_like(ref)
 
@@ -583,10 +581,12 @@
         for i in range(2):
             x = 2 * k + i
             for r, n in chunks(144, 48):
-                add = root0[x + 1, pl.ds(8 + r, n), :] * fine0[k, pl.ds(r, n), :]
-                w0b[x, pl.ds(8 + r, n), :] = w0[x + 1, pl.ds(16 + r, n), :] + add
-
-    loop(0, 10, up0, 10)
+                mid, total = around(beta0, x + 1, 16 + r, n)
+                root_x = root0[x + 1, pl.ds(8 + r, n), :]
+                add = root_x * fine0[k, pl.ds(r, n), :]
+                w0b[x, pl.ds(8 + r, n), :] = jnp.where(root_x > 0.0, 1.2 * mid + TAU * total + add, 0.0)
+
+    loop(0, 10, up0, 5)
 
     def first0(x):
         for r, n in chunks(144, 24):
@@ -670,11 +670,11 @@
     zlo, zhi = swap(zsend_hi, zsend_lo, "gz")
 
     depth = 128 + 2 * HZ0
-    own1, ysend_lo, ysend_hi, kept0 = call(
+    own1, ysend_lo, ysend_hi, beta0, root0 = call(
         down0_kernel,
         (turned, zlo, zhi),
-        [(8, 48, LANES)] + [(8, 6 * H1, LANES)] * 2 + [(3 * planes, depth + 16, LANES)],
-        [(8, depth, LANES)] * 2 + [(4 * depth, LANES)] * 2 + [(8, LANES, LANES)],
+        [(8, 48, LANES)] + [(8, 6 * H1, LANES)] * 2 + [(planes, depth + 16, LANES), (planes, depth, LANES)],
+        [(planes, depth + 16, LANES)] + [(8, depth, LANES)] * 2 + [(4 * depth, LANES)] * 2 + [(8, LANES, LANES)],
     )
     ylo, yhi = swap(ysend_hi, ysend_lo, "gy")
     turned1, low, high = call(
@@ -726,7 +726,7 @@
 
     (correction,) = call(
         functools.partial(up_kernel, gx, gy),
-        (e3, b2, below, above, kept1, kept0),
+        (e3, b2, below, above, kept1, beta0, root0),
         [(4, 16, 16, LANES)],
         [(x2, 64, LANES), (x2, 48, LANES), (x2, 64, LANES), (x2, 64, LANES), (6, 48, LANES)]
         + [(x1, 96, LANES)] * 2

time: 143 us -> 144 us (level)
    unnamed x12 -> x16, local copies, waits for them, and re-layouts: 8.51 us -> 8.85 us
where the time goes in v7:
time: 144 us; the launch traced here: 143 us
  starting transfers between devices  64.3 us (45%)
  waiting for transfers between devices  49.4 us (34%)
  Pallas kernels  20.1 us (14%)
  local copies, waits for them, and re-layouts  8.85 us (6%)
    ppermute x9, waiting for transfers between devices, swap(): lax.ppermute(to_down, axis, [(i + far, i) for i in range(n - far)])  39.9 us
    ppermute x9, starting transfers between devices, swap(): lax.ppermute(to_up, axis, [(i, i + far) for i in range(n - far)])  31.1 us
    ppermute x9, starting transfers between devices, swap(): lax.ppermute(to_down, axis, [(i + far, i) for i in range(n - far)])  24.7 us
    pallas_call x10, Pallas kernels, call(): pl.pallas_call(kernel, out_shape=[jax.ShapeDtypeStruct(s, F32) for s in o...  19.4 us
    ppermute x9, waiting for transfers between devices, swap(): lax.ppermute(to_up, axis, [(i, i + far) for i in range(n - far)])  9.44 us
    unnamed x16, local copies, waits for them, and re-layouts  8.85 us
    all_to_all x1, starting transfers between devices, whole_plane(): return lax.all_to_all(block, ('gx', 'gy'), 0, 0, tiled=True)  8.42 us
  transfers between devices with their start and end apart: 19, of which 15 were waited for; matrix products, arithmetic and copies ran while one was open for 0% of the time, Pallas kernels for 0%

profile of v7, /device:TPU:310, one launch (start us, length us, event | category | flops | bytes accessed | tf_op | source)
XLA Modules:
  0.0 142.9 jit_solution(1255959656176856244)
XLA Ops:
  0.0 1.0 copy-done.4
  1.0 0.9 copy-done.5
  1.9 0.7 copy-done.6
  2.6 0.7 copy-done.7
  3.3 0.7 shard_map.46
  4.0 4.6 %collective-permute-start = (f32[5,3,16,128]{3,2,1,0:T(8,128)S(1)}, f32[5,3,16,128]{3,2,1,0:T(8,128)S(1)}, u32[]{:S(2)}, u32[]{:S(2)}) collective-permute-start(f32[5,3,16,128]{3,2,1,0:T(8,128)S(1)} %get-tuple-element.35), channel_id=1, source_target_pairs={{0,128},{128,256},{256,384},{384,512},{512,640},{640,768},{768,896... | collective-permute-start | bytes 368648 | tf_op jit(solution)/shard_map/ppermute | solution.py:632
  8.6 1.9 %collective-permute-start.1 = (f32[5,3,16,128]{3,2,1,0:T(8,128)S(1)}, f32[5,3,16,128]{3,2,1,0:T(8,128)S(1)}, u32[]{:S(2)}, u32[]{:S(2)}) collective-permute-start(f32[5,3,16,128]{3,2,1,0:T(8,128)S(1)} %get-tuple-element.37), channel_id=1, source_target_pairs={{128,0},{256,128},{384,256},{512,384},{640,512},{768,640},{896,768... | collective-permute-start | bytes 368648 | tf_op jit(solution)/shard_map/ppermute | solution.py:633
  10.5 0.6 collective-permute-done.xlo
  11.1 5.4 %collective-permute-done.1.xhi = f32[5,3,16,128]{3,2,1,0:T(8,128)S(1)} collective-permute-done((f32[5,3,16,128]{3,2,1,0:T(8,128)S(1)}, f32[5,3,16,128]{3,2,1,0:T(8,128)S(1)}, u32[]{:S(2)}, u32[]{:S(2)}) %collective-permute-start.1) | collective-permute-done | bytes 122912 | tf_op jit(solution)/shard_map/ppermute | solution.py:633
  16.6 4.8 %collective-permute-start.2 = (f32[22,15,128]{2,1,0:T(8,128)S(1)}, f32[22,15,128]{2,1,0:T(8,128)S(1)}, u32[]{:S(2)}, u32[]{:S(2)}) collective-permute-start(f32[22,15,128]{2,1,0:T(8,128)S(1)} %get-tuple-element.38), channel_id=1, source_target_pairs={{0,16},{16,32},{32,48},{48,64},{64,80},{80,96},{96,112},{1,17},{17... | collective-permute-start | bytes 506888 | tf_op jit(solution)/shard_map/ppermute | solution.py:632
  21.5 1.9 %collective-permute-start.3 = (f32[22,15,128]{2,1,0:T(8,128)S(1)}, f32[22,15,128]{2,1,0:T(8,128)S(1)}, u32[]{:S(2)}, u32[]{:S(2)}) collective-permute-start(f32[22,15,128]{2,1,0:T(8,128)S(1)} %get-tuple-element.39), channel_id=1, source_target_pairs={{16,0},{32,16},{48,32},{64,48},{80,64},{96,80},{112,96},{17,1},{33... | collective-permute-start | bytes 506888 | tf_op jit(solution)/shard_map/ppermute | solution.py:633
  23.4 1.1 collective-permute-done.2.ylo
  24.4 5.6 %collective-permute-done.3.yhi = f32[22,15,128]{2,1,0:T(8,128)S(1)} collective-permute-done((f32[22,15,128]{2,1,0:T(8,128)S(1)}, f32[22,15,128]{2,1,0:T(8,128)S(1)}, u32[]{:S(2)}, u32[]{:S(2)}) %collective-permute-start.3) | collective-permute-done | bytes 168992 | tf_op jit(solution)/shard_map/ppermute | solution.py:633
  30.1 0.7 shard_map.48
  30.7 1.9 %collective-permute-start.4 = (f32[22,16,128]{2,1,0:T(8,128)S(1)}, f32[22,16,128]{2,1,0:T(8,128)S(1)}, u32[]{:S(2)}, u32[]{:S(2)}) collective-permute-start(f32[22,16,128]{2,1,0:T(8,128)S(1)} %get-tuple-element.41), channel_id=1, source_target_pairs={{0,1},{1,2},{2,3},{3,4},{4,5},{5,6},{6,7},{7,8},{8,9},{9,10},{10,1... | collective-permute-start | bytes 540680 | tf_op jit(solution)/shard_map/ppermute | solution.py:632
  32.7 3.6 %collective-permute-start.5 = (f32[22,16,128]{2,1,0:T(8,128)S(1)}, f32[22,16,128]{2,1,0:T(8,128)S(1)}, u32[]{:S(2)}, u32[]{:S(2)}) collective-permute-start(f32[22,16,128]{2,1,0:T(8,128)S(1)} %get-tuple-element.42), channel_id=1, source_target_pairs={{1,0},{2,1},{3,2},{4,3},{5,4},{6,5},{7,6},{8,7},{9,8},{10,9},{11,1... | collective-permute-start | bytes 540680 | tf_op jit(solution)/shard_map/ppermute | solution.py:633
  36.3 1.2 collective-permute-done.4.zlo
  37.5 1.8 %collective-permute-done.5.zhi = f32[22,16,128]{2,1,0:T(8,128)S(1)} collective-permute-done((f32[22,16,128]{2,1,0:T(8,128)S(1)}, f32[22,16,128]{2,1,0:T(8,128)S(1)}, u32[]{:S(2)}, u32[]{:S(2)}) %collective-permute-start.5) | collective-permute-done | bytes 180256 | tf_op jit(solution)/shard_map/ppermute | solution.py:633
  39.3 5.3 %shard_map.49 = (f32[8,48,128]{2,1,0:T(8,128)S(1)}, f32[8,36,128]{2,1,0:T(8,128)S(1)}, f32[8,36,128]{2,1,0:T(8,128)S(1)}, f32[22,176,128]{2,1,0:T(8,128)S(1)}, f32[22,160,128]{2,1,0:T(8,128)S(1)}) custom-call(f32[22,128,128]{2,1,0:T(8,128)S(1)} %get-tuple-element.40.turned, f32[22,16,128]{2,1,0:T(8,128)S(1)} %collective-permute-done.4.zlo, ...), custom_call_target="tpu_custom_call" | custom-call | tf_op jit(solution)/shard_map/pallas_call | solution.py:620
  44.6 1.3 copy-done
  45.9 1.2 copy-done.2
  47.2 1.9 %collective-permute-start.6 = (f32[8,36,128]{2,1,0:T(8,128)S(1)}, f32[8,36,128]{2,1,0:T(8,128)S(1)}, u32[]{:S(2)}, u32[]{:S(2)}) collective-permute-start(f32[8,36,128]{2,1,0:T(8,128)S(1)} %get-tuple-element.44), channel_id=1, source_target_pairs={{0,16},{16,32},{32,48},{48,64},{64,80},{80,96},{96,112},{1,17},{17... | collective-permute-start | bytes 442376 | tf_op jit(solution)/shard_map/ppermute | solution.py:632
  49.1 3.9 %collective-permute-start.7 = (f32[8,36,128]{2,1,0:T(8,128)S(1)}, f32[8,36,128]{2,1,0:T(8,128)S(1)}, u32[]{:S(2)}, u32[]{:S(2)}) collective-permute-start(f32[8,36,128]{2,1,0:T(8,128)S(1)} %get-tuple-element.45), channel_id=1, source_target_pairs={{16,0},{32,16},{48,32},{64,48},{80,64},{96,80},{112,96},{17,1},{33... | collective-permute-start | bytes 442376 | tf_op jit(solution)/shard_map/ppermute | solution.py:633
  53.0 1.4 collective-permute-done.6.ylo
  54.4 3.1 %collective-permute-done.7.yhi = f32[8,36,128]{2,1,0:T(8,128)S(1)} collective-permute-done((f32[8,36,128]{2,1,0:T(8,128)S(1)}, f32[8,36,128]{2,1,0:T(8,128)S(1)}, u32[]{:S(2)}, u32[]{:S(2)}) %collective-permute-start.7) | collective-permute-done | bytes 147488 | tf_op jit(solution)/shard_map/ppermute | solution.py:633
  57.7 1.9 %collective-permute-start.8 = (f32[6,80,128]{2,1,0:T(8,128)S(1)}, f32[6,80,128]{2,1,0:T(8,128)S(1)}, u32[]{:S(2)}, u32[]{:S(2)}) collective-permute-start(f32[6,80,128]{2,1,0:T(8,128)S(1)} %get-tuple-element.47), channel_id=1, source_target_pairs={{0,128},{128,256},{256,384},{384,512},{512,640},{640,768},{768,896... | collective-permute-start | bytes 737288 | tf_op jit(solution)/shard_map/ppermute | solution.py:632
  59.7 3.9 %collective-permute-start.9 = (f32[6,80,128]{2,1,0:T(8,128)S(1)}, f32[6,80,128]{2,1,0:T(8,128)S(1)}, u32[]{:S(2)}, u32[]{:S(2)}) collective-permute-start(f32[6,80,128]{2,1,0:T(8,128)S(1)} %get-tuple-element.48), channel_id=1, source_target_pairs={{128,0},{256,128},{384,256},{512,384},{640,512},{768,640},{896,768... | collective-permute-start | bytes 737288 | tf_op jit(solution)/shard_map/ppermute | solution.py:633
  63.6 3.4 %collective-permute-done.8.xlo = f32[6,80,128]{2,1,0:T(8,128)S(1)} collective-permute-done((f32[6,80,128]{2,1,0:T(8,128)S(1)}, f32[6,80,128]{2,1,0:T(8,128)S(1)}, u32[]{:S(2)}, u32[]{:S(2)}) %collective-permute-start.8) | collective-permute-done | bytes 245792 | tf_op jit(solution)/shard_map/ppermute | solution.py:632
  67.0 3.1 %collective-permute-done.9.xhi = f32[6,80,128]{2,1,0:T(8,128)S(1)} collective-permute-done((f32[6,80,128]{2,1,0:T(8,128)S(1)}, f32[6,80,128]{2,1,0:T(8,128)S(1)}, u32[]{:S(2)}, u32[]{:S(2)}) %collective-permute-start.9) | collective-permute-done | bytes 245792 | tf_op jit(solution)/shard_map/ppermute | solution.py:633
  70.1 2.1 %shard_map.51 = (f32[8,40,128]{2,1,0:T(8,128)S(1)}, f32[6,24,128]{2,1,0:T(8,128)S(1)}, f32[6,30,128]{2,1,0:T(8,128)S(1)}, f32[6,30,128]{2,1,0:T(8,128)S(1)}, f32[60,96,128]{2,1,0:T(8,128)S(1)}) custom-call(f32[8,80,128]{2,1,0:T(8,128)S(1)} %get-tuple-element.46.own, f32[6,80,128]{2,1,0:T(8,128)S(1)} %collective-permute-done.8.xlo, ...), custom_call_target="tpu_custom_call" | custom-call | tf_op jit(solution)/shard_map/pallas_call | solution.py:620
  72.2 1.3 shard_map.52
  73.4 8.4 %all-to-all-start = ((f32[64,3,128]{2,1,0:T(4,128)}), f32[64,3,128]{2,1,0:T(4,128)S(1)}, u32[]{:S(2)}, u32[]{:S(2)}) async-start(f32[64,3,128]{2,1,0:T(4,128)} %shard_map.52), calls=%async_computation | async-start | bytes 262144 | tf_op jit(solution)/shard_map/all_to_all | solution.py:638
  81.9 4.6 %collective-permute-start.10 = (f32[6,30,128]{2,1,0:T(8,128)S(1)}, f32[6,30,128]{2,1,0:T(8,128)S(1)}, u32[]{:S(2)}, u32[]{:S(2)}) collective-permute-start(f32[6,30,128]{2,1,0:T(8,128)S(1)} %get-tuple-element.51), channel_id=1, source_target_pairs={{0,16},{16,32},{32,48},{48,64},{64,80},{80,96},{96,112},{1,17},{17... | collective-permute-start | bytes 276488 | tf_op jit(solution)/shard_map/ppermute | solution.py:632
  86.5 1.9 %collective-permute-start.11 = (f32[6,30,128]{2,1,0:T(8,128)S(1)}, f32[6,30,128]{2,1,0:T(8,128)S(1)}, u32[]{:S(2)}, u32[]{:S(2)}) collective-permute-start(f32[6,30,128]{2,1,0:T(8,128)S(1)} %get-tuple-element.52), channel_id=1, source_target_pairs={{16,0},{32,16},{48,32},{64,48},{80,64},{96,80},{112,96},{17,1},{33... | collective-permute-start | bytes 276488 | tf_op jit(solution)/shard_map/ppermute | solution.py:633
  88.4 1.7 %collective-permute-done.10.ylo = f32[6,30,128]{2,1,0:T(8,128)S(1)} collective-permute-done((f32[6,30,128]{2,1,0:T(8,128)S(1)}, f32[6,30,128]{2,1,0:T(8,128)S(1)}, u32[]{:S(2)}, u32[]{:S(2)}) %collective-permute-start.10) | collective-permute-done | bytes 92192 | tf_op jit(solution)/shard_map/ppermute | solution.py:632
  90.1 4.7 %collective-permute-done.11.yhi = f32[6,30,128]{2,1,0:T(8,128)S(1)} collective-permute-done((f32[6,30,128]{2,1,0:T(8,128)S(1)}, f32[6,30,128]{2,1,0:T(8,128)S(1)}, u32[]{:S(2)}, u32[]{:S(2)}) %collective-permute-start.11) | collective-permute-done | bytes 92192 | tf_op jit(solution)/shard_map/ppermute | solution.py:633
  94.9 4.6 %collective-permute-start.12 = (f32[5,32,128]{2,1,0:T(8,128)S(1)}, f32[5,32,128]{2,1,0:T(8,128)S(1)}, u32[]{:S(2)}, u32[]{:S(2)}) collective-permute-start(f32[5,32,128]{2,1,0:T(8,128)S(1)} %get-tuple-element.54), channel_id=1, source_target_pairs={{0,128},{128,256},{256,384},{384,512},{512,640},{640,768},{768,896... | collective-permute-start | bytes 245768 | tf_op jit(solution)/shard_map/ppermute | solution.py:632
  99.6 1.9 %collective-permute-start.13 = (f32[5,32,128]{2,1,0:T(8,128)S(1)}, f32[5,32,128]{2,1,0:T(8,128)S(1)}, u32[]{:S(2)}, u32[]{:S(2)}) collective-permute-start(f32[5,32,128]{2,1,0:T(8,128)S(1)} %get-tuple-element.55), channel_id=1, source_target_pairs={{128,0},{256,128},{384,256},{512,384},{640,512},{768,640},{896,768... | collective-permute-start | bytes 245768 | tf_op jit(solution)/shard_map/ppermute | solution.py:633
  101.6 5.5 %collective-permute-done.13.xhi2 = f32[5,32,128]{2,1,0:T(8,128)S(1)} collective-permute-done((f32[5,32,128]{2,1,0:T(8,128)S(1)}, f32[5,32,128]{2,1,0:T(8,128)S(1)}, u32[]{:S(2)}, u32[]{:S(2)}) %collective-permute-start.13) | collective-permute-done | bytes 81952 | tf_op jit(solution)/shard_map/ppermute | solution.py:633
  107.4 1.9 %collective-permute-start.14 = (f32[23,16,128]{2,1,0:T(8,128)S(1)}, f32[23,16,128]{2,1,0:T(8,128)S(1)}, u32[]{:S(2)}, u32[]{:S(2)}) collective-permute-start(f32[23,16,128]{2,1,0:T(8,128)S(1)} %get-tuple-element.57), channel_id=1, source_target_pairs={{0,1},{1,2},{2,3},{3,4},{4,5},{5,6},{6,7},{7,8},{8,9},{9,10},{10,1... | collective-permute-start | bytes 565256 | tf_op jit(solution)/shard_map/ppermute | solution.py:632
  109.3 3.6 %collective-permute-start.15 = (f32[23,16,128]{2,1,0:T(8,128)S(1)}, f32[23,16,128]{2,1,0:T(8,128)S(1)}, u32[]{:S(2)}, u32[]{:S(2)}) collective-permute-start(f32[23,16,128]{2,1,0:T(8,128)S(1)} %get-tuple-element.58), channel_id=1, source_target_pairs={{1,0},{2,1},{3,2},{4,3},{5,4},{6,5},{7,6},{8,7},{9,8},{10,9},{11,1... | collective-permute-start | bytes 565256 | tf_op jit(solution)/shard_map/ppermute | solution.py:633
  113.0 4.8 %collective-permute-start.16 = (f32[16,4,128]{2,1,0:T(4,128)S(1)}, f32[16,4,128]{2,1,0:T(4,128)S(1)}, u32[]{:S(2)}, u32[]{:S(2)}) collective-permute-start(f32[16,4,128]{2,1,0:T(4,128)S(1)} %get-tuple-element.59), channel_id=1, source_target_pairs={{0,2},{1,3},{2,4},{3,5},{4,6},{5,7},{6,8},{7,9},{8,10},{9,11},{10,... | collective-permute-start | bytes 98312 | tf_op jit(solution)/shard_map/ppermute | solution.py:632
  117.8 1.9 %collective-permute-start.17 = (f32[16,4,128]{2,1,0:T(4,128)S(1)}, f32[16,4,128]{2,1,0:T(4,128)S(1)}, u32[]{:S(2)}, u32[]{:S(2)}) collective-permute-start(f32[16,4,128]{2,1,0:T(4,128)S(1)} %get-tuple-element.60), channel_id=1, source_target_pairs={{2,0},{3,1},{4,2},{5,3},{6,4},{7,5},{8,6},{9,7},{10,8},{11,9},{12,... | collective-permute-start | bytes 98312 | tf_op jit(solution)/shard_map/ppermute | solution.py:633
  119.7 10.7 %collective-permute-done.17.above2 = f32[16,4,128]{2,1,0:T(4,128)S(1)} collective-permute-done((f32[16,4,128]{2,1,0:T(4,128)S(1)}, f32[16,4,128]{2,1,0:T(4,128)S(1)}, u32[]{:S(2)}, u32[]{:S(2)}) %collective-permute-start.17) | collective-permute-done | bytes 32800 | tf_op jit(solution)/shard_map/ppermute | solution.py:633
  130.4 3.8 %shard_map.55.e3 = f32[6,24,128]{2,1,0:T(8,128)S(1)} custom-call(f32[16,16,128]{2,1,0:T(8,128)S(1)} %get-tuple-element.56.own, f32[23,16,128]{2,1,0:T(8,128)S(1)} %collective-permute-done.14.below, f32[23,16,128]{2,1,0:T(8,128)S(1)} %collective-permute-done.15.above, f32[16,4,128]{2,1,0:T(4,128)S(1)} %collective-permute-done.16.below2, ...), custom_call_target="tpu_custom_call" | custom-call | tf_op jit(solution)/shard_map/pallas_call | solution.py:620
  134.2 1.5 %copy-done.1 = f32[22,176,128]{2,1,0:T(8,128)S(1)} copy-done((f32[22,176,128]{2,1,0:T(8,128)S(1)}, f32[22,176,128]{2,1,0:T(8,128)}, u32[]{:S(2)}) %copy-start.1) | copy-done | bytes 1982488
  135.8 1.5 %copy-done.3 = f32[22,160,128]{2,1,0:T(8,128)S(1)} copy-done((f32[22,160,128]{2,1,0:T(8,128)S(1)}, f32[22,160,128]{2,1,0:T(8,128)}, u32[]{:S(2)}) %copy-start.3) | copy-done | bytes 1802264
  137.3 5.6 %shard_map.56 = f32[4,16,16,128]{3,2,1,0:T(8,128)} custom-call(f32[6,24,128]{2,1,0:T(8,128)S(1)} %shard_map.55.e3, f32[14,32,128]{2,1,0:T(8,128)S(1)} %get-tuple-element.61.b2, f32[23,16,128]{2,1,0:T(8,128)S(1)} %collective-permute-done.14.below, f32[23,16,128]{2,1,0:T(8,128)S(1)} %collective-permute-done.15.above, ...), custom_call_target="tpu_custom_call" | custom-call | tf_op jit(solution)/shard_map/pallas_call | solution.py:620
  (17 shorter events, 0.9 us)
Async XLA Ops:
  0.0 1.0 copy-start.4
  1.0 0.9 copy-start.5
  1.9 0.7 copy-start.6
  2.6 0.7 copy-start.7
  4.0 7.2 %collective-permute-start = (f32[5,3,16,128]{3,2,1,0:T(8,128)S(1)}, f32[5,3,16,128]{3,2,1,0:T(8,128)S(1)}, u32[]{:S(2)}, u32[]{:S(2)}) collective-permute-start(f32[5,3,16,128]{3,2,1,0:T(8,128)S(1)} %get-tuple-element.35), channel_id=1, source_target_pairs={{0,128},{128,256},{256,384},{384,512},{512,640},{640,768},{768,896... | collective-permute-start | bytes 368648 | tf_op jit(solution)/shard_map/ppermute | solution.py:632
  8.6 8.0 %collective-permute-start.1 = (f32[5,3,16,128]{3,2,1,0:T(8,128)S(1)}, f32[5,3,16,128]{3,2,1,0:T(8,128)S(1)}, u32[]{:S(2)}, u32[]{:S(2)}) collective-permute-start(f32[5,3,16,128]{3,2,1,0:T(8,128)S(1)} %get-tuple-element.37), channel_id=1, source_target_pairs={{128,0},{256,128},{384,256},{512,384},{640,512},{768,640},{896,768... | collective-permute-start | bytes 368648 | tf_op jit(solution)/shard_map/ppermute | solution.py:633
  16.6 7.8 %collective-permute-start.2 = (f32[22,15,128]{2,1,0:T(8,128)S(1)}, f32[22,15,128]{2,1,0:T(8,128)S(1)}, u32[]{:S(2)}, u32[]{:S(2)}) collective-permute-start(f32[22,15,128]{2,1,0:T(8,128)S(1)} %get-tuple-element.38), channel_id=1, source_target_pairs={{0,16},{16,32},{32,48},{48,64},{64,80},{80,96},{96,112},{1,17},{17... | collective-permute-start | bytes 506888 | tf_op jit(solution)/shard_map/ppermute | solution.py:632
  21.5 8.6 %collective-permute-start.3 = (f32[22,15,128]{2,1,0:T(8,128)S(1)}, f32[22,15,128]{2,1,0:T(8,128)S(1)}, u32[]{:S(2)}, u32[]{:S(2)}) collective-permute-start(f32[22,15,128]{2,1,0:T(8,128)S(1)} %get-tuple-element.39), channel_id=1, source_target_pairs={{16,0},{32,16},{48,32},{64,48},{80,64},{96,80},{112,96},{17,1},{33... | collective-permute-start | bytes 506888 | tf_op jit(solution)/shard_map/ppermute | solution.py:633
  30.7 6.8 %collective-permute-start.4 = (f32[22,16,128]{2,1,0:T(8,128)S(1)}, f32[22,16,128]{2,1,0:T(8,128)S(1)}, u32[]{:S(2)}, u32[]{:S(2)}) collective-permute-start(f32[22,16,128]{2,1,0:T(8,128)S(1)} %get-tuple-element.41), channel_id=1, source_target_pairs={{0,1},{1,2},{2,3},{3,4},{4,5},{5,6},{6,7},{7,8},{8,9},{9,10},{10,1... | collective-permute-start | bytes 540680 | tf_op jit(solution)/shard_map/ppermute | solution.py:632
  32.7 6.6 %collective-permute-start.5 = (f32[22,16,128]{2,1,0:T(8,128)S(1)}, f32[22,16,128]{2,1,0:T(8,128)S(1)}, u32[]{:S(2)}, u32[]{:S(2)}) collective-permute-start(f32[22,16,128]{2,1,0:T(8,128)S(1)} %get-tuple-element.42), channel_id=1, source_target_pairs={{1,0},{2,1},{3,2},{4,3},{5,4},{6,5},{7,6},{8,7},{9,8},{10,9},{11,1... | collective-permute-start | bytes 540680 | tf_op jit(solution)/shard_map/ppermute | solution.py:633
  44.6 1.3 copy-start
  45.9 1.2 copy-start.2
  47.2 7.2 %collective-permute-start.6 = (f32[8,36,128]{2,1,0:T(8,128)S(1)}, f32[8,36,128]{2,1,0:T(8,128)S(1)}, u32[]{:S(2)}, u32[]{:S(2)}) collective-permute-start(f32[8,36,128]{2,1,0:T(8,128)S(1)} %get-tuple-element.44), channel_id=1, source_target_pairs={{0,16},{16,32},{32,48},{48,64},{64,80},{80,96},{96,112},{1,17},{17... | collective-permute-start | bytes 442376 | tf_op jit(solution)/shard_map/ppermute | solution.py:632
  49.1 8.4 %collective-permute-start.7 = (f32[8,36,128]{2,1,0:T(8,128)S(1)}, f32[8,36,128]{2,1,0:T(8,128)S(1)}, u32[]{:S(2)}, u32[]{:S(2)}) collective-permute-start(f32[8,36,128]{2,1,0:T(8,128)S(1)} %get-tuple-element.45), channel_id=1, source_target_pairs={{16,0},{32,16},{48,32},{64,48},{80,64},{96,80},{112,96},{17,1},{33... | collective-permute-start | bytes 442376 | tf_op jit(solution)/shard_map/ppermute | solution.py:633
  57.7 9.2 %collective-permute-start.8 = (f32[6,80,128]{2,1,0:T(8,128)S(1)}, f32[6,80,128]{2,1,0:T(8,128)S(1)}, u32[]{:S(2)}, u32[]{:S(2)}) collective-permute-start(f32[6,80,128]{2,1,0:T(8,128)S(1)} %get-tuple-element.47), channel_id=1, source_target_pairs={{0,128},{128,256},{256,384},{384,512},{512,640},{640,768},{768,896... | collective-permute-start | bytes 737288 | tf_op jit(solution)/shard_map/ppermute | solution.py:632
  59.7 10.4 %collective-permute-start.9 = (f32[6,80,128]{2,1,0:T(8,128)S(1)}, f32[6,80,128]{2,1,0:T(8,128)S(1)}, u32[]{:S(2)}, u32[]{:S(2)}) collective-permute-start(f32[6,80,128]{2,1,0:T(8,128)S(1)} %get-tuple-element.48), channel_id=1, source_target_pairs={{128,0},{256,128},{384,256},{512,384},{640,512},{768,640},{896,768... | collective-permute-start | bytes 737288 | tf_op jit(solution)/shard_map/ppermute | solution.py:633
  73.4 33.7 %all-to-all-start = ((f32[64,3,128]{2,1,0:T(4,128)}), f32[64,3,128]{2,1,0:T(4,128)S(1)}, u32[]{:S(2)}, u32[]{:S(2)}) async-start(f32[64,3,128]{2,1,0:T(4,128)} %shard_map.52), calls=%async_computation | async-start | bytes 262144 | tf_op jit(solution)/shard_map/all_to_all | solution.py:638
  81.9 8.2 %collective-permute-start.10 = (f32[6,30,128]{2,1,0:T(8,128)S(1)}, f32[6,30,128]{2,1,0:T(8,128)S(1)}, u32[]{:S(2)}, u32[]{:S(2)}) collective-permute-start(f32[6,30,128]{2,1,0:T(8,128)S(1)} %get-tuple-element.51), channel_id=1, source_target_pairs={{0,16},{16,32},{32,48},{48,64},{64,80},{80,96},{96,112},{1,17},{17... | collective-permute-start | bytes 276488 | tf_op jit(solution)/shard_map/ppermute | solution.py:632
  86.5 8.3 %collective-permute-start.11 = (f32[6,30,128]{2,1,0:T(8,128)S(1)}, f32[6,30,128]{2,1,0:T(8,128)S(1)}, u32[]{:S(2)}, u32[]{:S(2)}) collective-permute-start(f32[6,30,128]{2,1,0:T(8,128)S(1)} %get-tuple-element.52), channel_id=1, source_target_pairs={{16,0},{32,16},{48,32},{64,48},{80,64},{96,80},{112,96},{17,1},{33... | collective-permute-start | bytes 276488 | tf_op jit(solution)/shard_map/ppermute | solution.py:633
  94.9 6.7 %collective-permute-start.12 = (f32[5,32,128]{2,1,0:T(8,128)S(1)}, f32[5,32,128]{2,1,0:T(8,128)S(1)}, u32[]{:S(2)}, u32[]{:S(2)}) collective-permute-start(f32[5,32,128]{2,1,0:T(8,128)S(1)} %get-tuple-element.54), channel_id=1, source_target_pairs={{0,128},{128,256},{256,384},{384,512},{512,640},{640,768},{768,896... | collective-permute-start | bytes 245768 | tf_op jit(solution)/shard_map/ppermute | solution.py:632
  99.6 7.5 %collective-permute-start.13 = (f32[5,32,128]{2,1,0:T(8,128)S(1)}, f32[5,32,128]{2,1,0:T(8,128)S(1)}, u32[]{:S(2)}, u32[]{:S(2)}) collective-permute-start(f32[5,32,128]{2,1,0:T(8,128)S(1)} %get-tuple-element.55), channel_id=1, source_target_pairs={{128,0},{256,128},{384,256},{512,384},{640,512},{768,640},{896,768... | collective-permute-start | bytes 245768 | tf_op jit(solution)/shard_map/ppermute | solution.py:633
  107.4 23.0 %collective-permute-start.14 = (f32[23,16,128]{2,1,0:T(8,128)S(1)}, f32[23,16,128]{2,1,0:T(8,128)S(1)}, u32[]{:S(2)}, u32[]{:S(2)}) collective-permute-start(f32[23,16,128]{2,1,0:T(8,128)S(1)} %get-tuple-element.57), channel_id=1, source_target_pairs={{0,1},{1,2},{2,3},{3,4},{4,5},{5,6},{6,7},{7,8},{8,9},{9,10},{10,1... | collective-permute-start | bytes 565256 | tf_op jit(solution)/shard_map/ppermute | solution.py:632
  109.3 21.1 %collective-permute-start.15 = (f32[23,16,128]{2,1,0:T(8,128)S(1)}, f32[23,16,128]{2,1,0:T(8,128)S(1)}, u32[]{:S(2)}, u32[]{:S(2)}) collective-permute-start(f32[23,16,128]{2,1,0:T(8,128)S(1)} %get-tuple-element.58), channel_id=1, source_target_pairs={{1,0},{2,1},{3,2},{4,3},{5,4},{6,5},{7,6},{8,7},{9,8},{10,9},{11,1... | collective-permute-start | bytes 565256 | tf_op jit(solution)/shard_map/ppermute | solution.py:633
  113.0 6.8 %collective-permute-start.16 = (f32[16,4,128]{2,1,0:T(4,128)S(1)}, f32[16,4,128]{2,1,0:T(4,128)S(1)}, u32[]{:S(2)}, u32[]{:S(2)}) collective-permute-start(f32[16,4,128]{2,1,0:T(4,128)S(1)} %get-tuple-element.59), channel_id=1, source_target_pairs={{0,2},{1,3},{2,4},{3,5},{4,6},{5,7},{6,8},{7,9},{8,10},{9,11},{10,... | collective-permute-start | bytes 98312 | tf_op jit(solution)/shard_map/ppermute | solution.py:632
  117.8 12.6 %collective-permute-start.17 = (f32[16,4,128]{2,1,0:T(4,128)S(1)}, f32[16,4,128]{2,1,0:T(4,128)S(1)}, u32[]{:S(2)}, u32[]{:S(2)}) collective-permute-start(f32[16,4,128]{2,1,0:T(4,128)S(1)} %get-tuple-element.60), channel_id=1, source_target_pairs={{2,0},{3,1},{4,2},{5,3},{6,4},{7,5},{8,6},{9,7},{10,8},{11,9},{12,... | collective-permute-start | bytes 98312 | tf_op jit(solution)/shard_map/ppermute | solution.py:633
  134.2 1.6 %copy-start.1 = (f32[22,176,128]{2,1,0:T(8,128)S(1)}, f32[22,176,128]{2,1,0:T(8,128)}, u32[]{:S(2)}) copy-start(f32[22,176,128]{2,1,0:T(8,128)} %copy-done) | copy-start | bytes 5947396
  135.8 1.5 %copy-start.3 = (f32[22,160,128]{2,1,0:T(8,128)S(1)}, f32[22,160,128]{2,1,0:T(8,128)}, u32[]{:S(2)}) copy-start(f32[22,160,128]{2,1,0:T(8,128)} %copy-done.2) | copy-start | bytes 5406724
